TPU v7x, 128 devices: a whole 4x4x4 slice. The times are simulated.
128 devices in a mesh: seq: 32 (over z, y, core), head: 4 (over x).
Axes of the slice: x: 4, y: 4, z: 4, core: 2. Of those that a mesh axis runs over, the one named last changes fastest.
Arguments:
- hidden_in: bfloat16 [8192, 1024], P('seq'), may hold values from -6 to 6
- cotangent: bfloat16 [8192, 1024], P('seq'), may hold values from -6 to 6
- log_decay: float32 [8192, 24], P('seq', 'head'), may hold values from -2 to 0, as said below
- norm_gain: float32 [1024], replicated, may hold values from 0.25 to 1.75
- query_weight: bfloat16 [1024, 512], P(None, 'head'), may hold values from -0.1875 to 0.1875
- keyvalue_weight: bfloat16 [2, 1024, 128], replicated, may hold values from -0.1875 to 0.1875
- attention_output: bfloat16 [512, 1024], P('head'), may hold values from -2 to 2
- mixer_weight: bfloat16 [2, 1024, 1536], P(None, None, 'head'), may hold values from -0.1875 to 0.1875
- state_weight: bfloat16 [1024, 256], replicated, may hold values from -0.1875 to 0.1875
- kernel_mixer: float32 [4, 1536], P(None, 'head'), may hold values from -3 to 3
- kernel_state: float32 [4, 256], replicated, may hold values from -3 to 3
- bias_mixer: float32 [1536], P('head'), may hold values from -3 to 3
- bias_state: float32 [256], replicated, may hold values from -3 to 3
- skip_gain: float32 [24], P('head'), may hold values from 0.5 to 1.5
- mixer_gain: float32 [1536], P('head'), may hold values from 0.25 to 1.75
- mixer_output: bfloat16 [1536, 1024], P('head'), may hold values from -0.15625 to 0.15625
- second_gain: float32 [1024], replicated, may hold values from 0.25 to 1.75
- gate_up: bfloat16 [2, 1024, 2048], P(None, None, 'head'), may hold values from -0.1875 to 0.1875
- down_weight: bfloat16 [2048, 1024], P('head'), may hold values from -0.125 to 0.125
Outputs:
- block_out: float32 [8192, 1024], P('seq', 'head')
- input_grads: float32 [8192, 1024], P('seq', 'head')
- gain_grads: float32 [1024], replicated
- query_grads: float32 [1024, 512], P(None, 'head')
- keyvalue_grads: float32 [2, 1024, 128], replicated
- attention_grads: float32 [512, 1024], P('head')
- mixer_grads: float32 [2, 1024, 1536], P(None, None, 'head')
- state_grads: float32 [1024, 256], replicated
- mixkernel_grads: float32 [4, 1536], P(None, 'head')
- statekernel_grads: float32 [4, 256], replicated
- mixbias_grads: float32 [1536], P('head')
- statebias_grads: float32 [256], replicated
- skip_grads: float32 [24], P('head')
- mixgain_grads: float32 [1536], P('head')
- mixout_grads: float32 [1536, 1024], P('head')
- second_grads: float32 [1024], replicated
- gateup_grads: float32 [2, 1024, 2048], P(None, None, 'head')
- down_grads: float32 [2048, 1024], P('head')
Inputs may be any that keep to these rules, and one draw needn't show every extreme that they name: `log_decay`: strictly negative; per token and Mamba head.
All inputs are finite; a program needn't handle non-finite values.
Results may differ from a plain program's by a relative error of at most 0.03.
Values may be sent and summed in bfloat16 or wider, within the bound.
A program may use at most 128 MiB of HBM per device.

v0:
```python
import functools

import jax
import jax.numpy as jnp
from jax import lax
from jax.experimental import pallas as pl
from jax.experimental.pallas import tpu as pltpu
from jax.sharding import PartitionSpec as P

D = 1024
FF = 2048
AH = 8
KVH = 2
HD = 64
MAMBA_HEADS = 24
MP = 64
NS = 128
KC = 4
EPSILON = 1e-05
SEQ = 32
HEADS = 4
ROWS = 256
MW = 384
CW = 640
HMH = 6
HIGHEST = lax.Precision.HIGHEST
MESH = pl.DeviceIdType.MESH
F32 = jnp.float32
BF16 = jnp.bfloat16
VMEM_LIMIT = 50 * 1024 * 1024


def nn(a, b):
    return jnp.dot(a, b, preferred_element_type=F32)


def nt(a, b):
    return lax.dot_general(a, b, (((1,), (1,)), ((), ())), preferred_element_type=F32)


def tn(a, b):
    return lax.dot_general(a, b, (((0,), (0,)), ((), ())), preferred_element_type=F32)


def exact(a, b, dims):
    return lax.dot_general(
        a, b, (dims, ((), ())), precision=HIGHEST, preferred_element_type=F32
    )


def sigmoid(v):
    return 1.0 / (1.0 + jnp.exp(-v))


def shape(dims, kind):
    return jax.ShapeDtypeStruct(dims, kind)


def seq_bits(s):
    core, y, z = s % 2, (s // 2) % 4, s // 8
    return {
        "c": core,
        "ya": (y + y // 2) % 2,
        "yb": y // 2,
        "za": (z + z // 2) % 2,
        "zb": z // 2,
    }


SEQ_PATHS = (
    ("c", "ya", "yb", "za", "zb"),
    ("c", "yb", "ya", "zb", "za"),
    ("c", "za", "zb", "ya", "yb"),
    ("c", "zb", "za", "yb", "ya"),
)
HEAD_PATHS = (("xa", "xb"), ("xb", "xa"))


def position(bits, path):
    at = 0
    for name in path:
        at = at * 2 + bits[name]
    return at


def block_position(s, p):
    return position(seq_bits(s), SEQ_PATHS[p])


def head_position(h, p):
    bits = {"xa": (h + h // 2) % 2, "xb": h // 2}
    return position(bits, HEAD_PATHS[p])


class Links:
    def __init__(self, send_sem, recv_sem):
        s, h = lax.axis_index("seq"), lax.axis_index("head")
        self.s, self.h = s, h
        core, y, z = s % 2, (s // 2) % 4, s // 8
        self.bits = seq_bits(s)
        self.bits["xa"] = (h + h // 2) % 2
        self.bits["xb"] = h // 2
        self.partner = {
            "c": (s + 1 - 2 * core, h),
            "ya": (s + 2 * (1 - 2 * (y % 2)), h),
            "yb": (s + 2 * (3 - 2 * y), h),
            "za": (s + 8 * (1 - 2 * (z % 2)), h),
            "zb": (s + 8 * (3 - 2 * z), h),
            "xa": (s, h + 1 - 2 * (h % 2)),
            "xb": (s, 3 - h),
            "x1": (s, (h + 1) % HEADS),
            "x2": (s, (h + 2) % HEADS),
            "x3": (s, (h + 3) % HEADS),
            "next": ((s + 1) % SEQ, h),
            "prev": ((s + SEQ - 1) % SEQ, h),
        }
        self.send_sem, self.recv_sem, self.used = send_sem, recv_sem, 0

    def barrier(self, names):
        semaphore = pltpu.get_barrier_semaphore()
        for name in names:
            pl.semaphore_signal(
                semaphore, inc=1, device_id=self.partner[name], device_id_type=MESH
            )
        pl.semaphore_wait(semaphore, len(names))

    def send(self, src, dst, name):
        k = self.used
        self.used += 1
        copy = pltpu.make_async_remote_copy(
            src_ref=src,
            dst_ref=dst,
            send_sem=self.send_sem.at[k],
            recv_sem=self.recv_sem.at[k],
            device_id=self.partner[name],
            device_id_type=MESH,
        )
        copy.start()
        return copy


SEQ_NAMES = ("c", "ya", "yb", "za", "zb")


def rows_at(start, count, unit=16):
    return pl.ds(pl.multiple_of(start, unit), count)


class Reduce:
    def __init__(self, links, path, rows, src, src_base, work, recv, out, base):
        self.links, self.path, self.rows = links, path, rows
        self.src, self.src_base = src, src_base
        self.work, self.recv, self.out, self.base = work, recv, out, base
        self.start = 0
        self.copy = None

    def begin(self, step):
        name = self.path[step]
        half = self.rows >> (step + 1)
        bit = self.links.bits[name]
        away = self.start + (1 - bit) * half
        ref, at = (self.src, self.src_base) if step == 0 else (self.work, self.base)
        landing = self.base + self.rows - (self.rows >> step)
        self.copy = self.links.send(
            ref.at[rows_at(at + away, half)], self.recv.at[pl.ds(landing, half)], name
        )

    def finish(self, step):
        name = self.path[step]
        half = self.rows >> (step + 1)
        keep = self.start + self.links.bits[name] * half
        ref, at = (self.src, self.src_base) if step == 0 else (self.work, self.base)
        landing = self.base + self.rows - (self.rows >> step)
        last = step == len(self.path) - 1
        target, offset = (self.out, self.base) if last and self.out is not None else (self.work, self.base)
        self.copy.wait()
        chunk = min(half, 32)

        def add(i, carry):
            own = ref[rows_at(at + keep + i * chunk, chunk)].astype(F32)
            other = self.recv[rows_at(landing + i * chunk, chunk)].astype(F32)
            target[rows_at(offset + keep + i * chunk, chunk)] = (own + other).astype(BF16)
            return carry

        lax.fori_loop(0, half // chunk, add, 0)
        self.start = keep

    def send_back(self, step, columns=None):
        name = self.path[step]
        size = self.rows >> (step + 1)
        at = rows_at(self.base + self.start, size, min(size, 16))
        ref = self.out.at[at] if columns is None else self.out.at[at, pl.ds(0, columns)]
        self.copy = self.links.send(ref, ref, name)

    def wait_back(self, step):
        size = self.rows >> (step + 1)
        self.copy.wait()
        self.start = self.start - self.links.bits[self.path[step]] * size


def reduce_all(jobs):
    for job in jobs:
        job.begin(0)
    for step in range(max(len(job.path) for job in jobs)):
        for job in jobs:
            if step < len(job.path):
                job.finish(step)
                if step + 1 < len(job.path):
                    job.begin(step + 1)


def gather_all(jobs, columns=None):
    columns = columns or [None] * len(jobs)
    for job, width in zip(jobs, columns):
        job.send_back(len(job.path) - 1, width)
    for step in range(max(len(job.path) for job in jobs) - 1, -1, -1):
        for job, width in zip(jobs, columns):
            if step < len(job.path):
                job.wait_back(step)
                if step:
                    job.send_back(step - 1, width)


def call(body, outs, args, scratch=(), collective=None, smem=0, copies=0, cost=None):
    vm = pl.BlockSpec(memory_space=pltpu.VMEM)
    scratch = list(scratch)
    if copies:
        scratch += [pltpu.SemaphoreType.DMA((copies,)), pltpu.SemaphoreType.DMA((copies,))]
    if collective is None:
        params = pltpu.CompilerParams(vmem_limit_bytes=VMEM_LIMIT)
    else:
        params = pltpu.CompilerParams(
            vmem_limit_bytes=VMEM_LIMIT, collective_id=collective, has_side_effects=True
        )
    in_specs = [pl.BlockSpec(memory_space=pltpu.SMEM)] * smem + [vm] * (len(args) - smem)
    return pl.pallas_call(
        body,
        out_shape=tuple(outs),
        in_specs=in_specs,
        out_specs=tuple(vm for _ in outs),
        scratch_shapes=scratch,
        compiler_params=params,
    )(*args)


class Gather:
    def __init__(self, links, path, piece, out, base):
        self.links, self.path, self.piece, self.out, self.base = links, path, piece, out, base
        self.start = position(links.bits, path) * piece
        self.rows = piece << len(path)

    send_back = Reduce.send_back
    wait_back = Reduce.wait_back


def gather_rows(links, src, out, paths=SEQ_PATHS):
    piece = src.shape[0] // len(paths)
    jobs = []
    for p, path in enumerate(paths):
        job = Gather(links, path, piece, out, p * (piece << len(path)))
        own = rows_at(job.base + job.start, piece, 8 if piece == 8 else 16)
        out[own] = src[pl.ds(p * piece, piece)]
        jobs.append(job)
    return jobs


def keyval_kernel(kv, edge, logs, kv_all, edge_in, logs_all, send_sem, recv_sem):
    links = Links(send_sem, recv_sem)
    jobs = gather_rows(links, kv, kv_all) + gather_rows(links, logs, logs_all, SEQ_PATHS[:1])
    links.barrier(SEQ_NAMES + ("next", "prev"))
    edge_copy = links.send(edge, edge_in, "next")
    gather_all(jobs)
    edge_copy.wait()


def state_kernel(state, state_all, send_sem, recv_sem):
    links = Links(send_sem, recv_sem)
    jobs = gather_rows(links, state, state_all)
    links.barrier(SEQ_NAMES)
    gather_all(jobs)


def sums_kernel(part, total, slots, send_sem, recv_sem):
    links = Links(send_sem, recv_sem)
    slots[links.h] = part[...]
    links.barrier(("x1", "x2", "x3"))
    copies = [links.send(part, slots.at[links.h], name) for name in ("x1", "x2", "x3")]
    for copy in copies:
        copy.wait()
    total[...] = (slots[0] + slots[1]) + (slots[2] + slots[3])


def head_sum_kernel(part, total, work, recv, send_sem, recv_sem):
    links = Links(send_sem, recv_sem)
    links.barrier(("xa", "xb"))
    jobs = [
        Reduce(links, path, 128, part, 128 * p, work, recv, total, 128 * p)
        for p, path in enumerate(HEAD_PATHS)
    ]
    reduce_all(jobs)
    gather_all(jobs)


def own_rows(job, count):
    return job.work[rows_at(job.base + job.start, count)]


def second_sum_kernel(part, wide, total, share, work, recv, wide_work, wide_recv, send_sem, recv_sem):
    links = Links(send_sem, recv_sem)
    links.barrier(("xa", "xb"))
    sums = [
        Reduce(links, path, 128, part, 128 * p, work, recv, total, 128 * p)
        for p, path in enumerate(HEAD_PATHS)
    ]
    shares = [
        Reduce(links, path, 512, wide, 512 * p, wide_work, wide_recv, None, 512 * p)
        for p, path in enumerate(HEAD_PATHS)
    ]
    reduce_all(sums + shares)
    gather_all(sums)
    for p, job in enumerate(shares):
        share[pl.ds(128 * p, 128)] = own_rows(job, 128)


def pair_kernel(pairs, edge, own, edge_in, work, recv, send_sem, recv_sem):
    links = Links(send_sem, recv_sem)
    links.barrier(SEQ_NAMES + ("next", "prev"))
    edge_copy = links.send(edge, edge_in, "prev")
    jobs = [
        Reduce(links, path, 2048, pairs, 2048 * p, work, recv, None, 2048 * p)
        for p, path in enumerate(SEQ_PATHS)
    ]
    reduce_all(jobs)
    for p, job in enumerate(jobs):
        own[pl.ds(64 * p, 64)] = own_rows(job, 64)
    edge_copy.wait()


def final_kernel(
    xf, xb, ms, wide, small,
    x_out, ms_out, share, small_out,
    x_work, x_recv, ms_work, ms_recv, wide_work, wide_recv, head_slots, small_y, small_z, small_x,
    small_work, small_recv, send_sem, recv_sem,
):
    links = Links(send_sem, recv_sem)
    links.barrier(SEQ_NAMES + ("xa", "xb", "x1", "x2", "x3"))
    x_jobs = [
        Reduce(
            links, path, 512, xf if p < 3 else xb, 512 * p if p < 3 else 0,
            x_work, x_recv, x_out, 512 * p,
        )
        for p, path in enumerate(SEQ_PATHS)
    ]
    ms_jobs = [
        Reduce(links, path, 512, ms, 512 * p, ms_work, ms_recv, None, 512 * p)
        for p, path in enumerate(SEQ_PATHS)
    ]
    shares = [
        Reduce(links, path, 512, wide, 512 * p, wide_work, wide_recv, None, 512 * p)
        for p, path in enumerate(HEAD_PATHS)
    ]
    small_work[0] = small[...]
    small_steps = ("c", "ya", "yb", "za", "zb")
    reduce_all(shares)
    for p, job in enumerate(shares):
        share[pl.ds(128 * p, 128)] = own_rows(job, 128)
    for step, name in enumerate(small_steps):
        copy = links.send(small_work.at[step], small_recv.at[step], name)
        copy.wait()
        small_work[step + 1] = small_work[step] + small_recv[step]
    small_x[links.h] = small_work[5]
    small_copies = [links.send(small_work.at[5], small_x.at[links.h], n) for n in ("x1", "x2", "x3")]
    reduce_all(x_jobs + ms_jobs)
    head_copies = []
    for p, job in enumerate(ms_jobs):
        at = rows_at(job.base + job.start, 16)
        if p < 2:
            piece = ms_work[at, pl.ds(384, 256)]
        else:
            piece = jnp.concatenate([ms_work[at, pl.ds(512, 128)]] * 2, axis=1)
        head_slots[links.h, pl.ds(16 * p, 16)] = piece
    slot = head_slots.at[links.h]
    head_copies = [links.send(slot, slot, n) for n in ("x1", "x2", "x3")]
    for copy in small_copies:
        copy.wait()
    total = (small_x[0] + small_x[1]) + (small_x[2] + small_x[3])
    row = lax.broadcasted_iota(jnp.int32, (8, 1024), 0)
    small_out[...] = jnp.where(row < 4, total, small_work[5])
    for copy in head_copies:
        copy.wait()
    for p, job in enumerate(ms_jobs):
        job.out = ms_out
        at = rows_at(job.base + job.start, 16)
        parts = [head_slots[k, pl.ds(16 * p, 16)].astype(F32) for k in range(HEADS)]
        if p < 2:
            ms_out[at, pl.ds(0, 384)] = ms_work[at, pl.ds(0, 384)]
            ms_out[at, pl.ds(384, 256)] = ((parts[0] + parts[1]) + (parts[2] + parts[3])).astype(BF16)
        else:
            ms_out[at, pl.ds(0, 512)] = ms_work[at, pl.ds(0, 512)]
            ms_out[at, pl.ds(512, 128)] = (parts[0] + parts[1])[:, :128].astype(BF16)
            ms_out[at, pl.ds(640, 128)] = (parts[2] + parts[3])[:, :128].astype(BF16)
    gather_all(x_jobs + ms_jobs, [None] * 4 + [640, 640, None, None])


def project_kernel(x_ref, gain, wq, wkv, wm, ws, normed, q, kv, gz, raw):
    x = x_ref[...].astype(F32)
    r1 = lax.rsqrt(jnp.mean(x * x, axis=1, keepdims=True) + EPSILON)
    n = (x * r1 * gain[...]).astype(BF16)
    normed[...] = n
    q[...] = nn(n, wq[...]).astype(BF16)
    kv[...] = nn(n, wkv[...]).astype(BF16)
    gz[...] = nn(n, wm[0])
    raw[:, pl.ds(0, MW)] = nn(n, wm[1])
    raw[:, pl.ds(MW, 256)] = nn(n, ws[...])


def widen(values):
    lane = lax.broadcasted_iota(jnp.int32, (8, MW), 1)
    row = lax.broadcasted_iota(jnp.int32, (8, MW), 0)
    spread = jnp.where((lane >= row * MP) & (lane < row * MP + MP), 1.0, 0.0)
    return exact(values, spread, ((1,), (0,)))


def decay_terms(step_ref, cum_ref):
    cum = cum_ref[...]
    step_x = widen(step_ref[...])
    cum_x = widen(cum)
    enter_x = jnp.exp(cum_x)
    tail_x = jnp.exp(cum_x[ROWS - 1 : ROWS, :] - cum_x)
    return step_x, enter_x, tail_x


def conv_kernel(idx, raw, edge, taps, bias, step, cum, pre, post, state, ext):
    keep = jnp.where(idx[0] > 0, 1.0, 0.0)
    ext[pl.ds(0, 8)] = edge[...] * keep
    ext[pl.ds(8, ROWS)] = raw[...]
    for c in range(5):
        lanes = pl.ds(128 * c, 128)
        total = bias[:, lanes] + taps[pl.ds(0, 1), lanes] * ext[pl.ds(5, ROWS), lanes]
        for k in range(1, KC):
            total = total + taps[pl.ds(k, 1), lanes] * ext[pl.ds(5 + k, ROWS), lanes]
        pre[:, lanes] = total
        post[:, lanes] = (total * sigmoid(total)).astype(BF16)
    step_x, _, tail_x = decay_terms(step, cum)
    tail_in = (post[:, pl.ds(0, MW)].astype(F32) * step_x * tail_x).astype(BF16)
    state[...] = tn(tail_in, post[:, pl.ds(MW, NS)]).astype(BF16)


def chain(idx, gathered, logs, total, forward):
    s = idx[0]
    total[...] = jnp.zeros_like(total)

    def hop(i, run):
        j = s - 1 - i if forward else s + 1 + i
        weight = jnp.exp(run)
        for seg in range(12):
            p, off = seg // 3, (seg % 3) * 32
            at = rows_at(p * 3072 + block_position(j, p) * 96 + off, 32)
            h = seg // 2
            total[pl.ds(32 * seg, 32)] += weight[h : h + 1, :] * gathered[at].astype(F32)
        return run + logs[rows_at(block_position(j, 0) * 8, 8, 8)]

    lax.fori_loop(0, s if forward else SEQ - 1 - s, hop, jnp.zeros((8, 128), F32))


def lower_mask():
    t = lax.broadcasted_iota(jnp.int32, (ROWS, ROWS), 0)
    u = lax.broadcasted_iota(jnp.int32, (ROWS, ROWS), 1)
    return u <= t


def decay_of(cum, cum_t, h, mask):
    diff = cum[:, h : h + 1] - cum_t[h : h + 1, :]
    return jnp.exp(jnp.where(mask, diff, -1e30))


def row_sums(values):
    return exact(jnp.ones((8, values.shape[1]), F32), values, ((1,), (1,)))


def column_of(rows):
    return exact(rows, jnp.full((8, 128), 0.125, F32), ((0,), (0,)))[:, 0:1]


def ssd_kernel(
    idx, post, step, cum_ref, cumt_ref, skip, gz, gathered, logs, ssd, mixed, squares, state, total
):
    chain(idx, gathered, logs, total, True)
    state[...] = total[...].astype(BF16)
    step_x, enter_x, _ = decay_terms(step, cum_ref)
    mixer_in = post[:, pl.ds(0, MW)].astype(F32)
    scaled = (mixer_in * step_x).astype(BF16)
    b, c = post[:, pl.ds(MW, NS)], post[:, pl.ds(MW + NS, NS)]
    gram = nt(c, b)
    mask = lower_mask()
    cum, cum_t = cum_ref[...], cumt_ref[...]
    left = lax.broadcasted_iota(jnp.int32, (ROWS, 128), 1) < MP
    carried = enter_x * nt(c, state[...]) + skip[...] * mixer_in
    for pair in range(3):
        lanes = slice(128 * pair, 128 * pair + 128)
        first = nn((gram * decay_of(cum, cum_t, 2 * pair, mask)).astype(BF16), scaled[:, lanes])
        second = nn((gram * decay_of(cum, cum_t, 2 * pair + 1, mask)).astype(BF16), scaled[:, lanes])
        ssd[:, pl.ds(128 * pair, 128)] = jnp.where(left, first, second) + carried[:, lanes]
    z = gz[...]
    m = ssd[...] * (z * sigmoid(z))
    mixed[...] = m
    squares[...] = row_sums(m * m)


def outputs_kernel(mixed, squares, mgain, wmo, attended, wao, gated, part):
    scale = lax.rsqrt(column_of(squares[...]) / (MAMBA_HEADS * MP) + EPSILON)
    g = (mixed[...] * scale * mgain[...]).astype(BF16)
    gated[...] = g
    for c in range(2):
        lanes = pl.ds(512 * c, 512)
        part[:, lanes] = (nn(attended[...], wao[:, lanes]) + nn(g, wmo[:, lanes])).astype(BF16)


def load_block(kv_all, j):
    return jnp.concatenate(
        [kv_all[rows_at(2048 * p + block_position(j, p) * 64, 64)] for p in range(4)], axis=0
    )


def causal(block):
    key = lax.broadcasted_iota(jnp.int32, block.shape, 0)
    query = lax.broadcasted_iota(jnp.int32, block.shape, 1)
    query = jnp.where(query >= ROWS, query - ROWS, query)
    return jnp.where(key <= query, block, -1e30)


def stacked_queries(q):
    q = q.astype(F32) * (HD ** -0.5)
    left = lax.broadcasted_iota(jnp.int32, (ROWS, 128), 1) < HD
    first = jnp.where(left, q, 0.0)
    second = jnp.where(left, pltpu.roll(q, HD, 1), 0.0)
    return jnp.concatenate([first, second], axis=0).astype(BF16)


def attend_kernel(idx, q, kv_all, attended, attended_f, totals, qp, acc):
    s = idx[0]
    qp[...] = stacked_queries(q[...])
    block = load_block(kv_all, s)
    scores = causal(nt(block, qp[...]))
    high = jnp.max(scores, axis=0, keepdims=True)
    weights = jnp.exp(scores - high)
    acc[...] = tn(block, weights.astype(BF16))

    def hop(j, running):
        high, total = running
        block = load_block(kv_all, j)
        scores = nt(block, qp[...])
        new = jnp.maximum(high, jnp.max(scores, axis=0, keepdims=True))
        fade = jnp.exp(high - new)
        weights = jnp.exp(scores - new)
        acc[...] = acc[...] * fade + tn(block, weights.astype(BF16))
        return new, total * fade + jnp.sum(weights, axis=0, keepdims=True)

    high, total = lax.fori_loop(0, s, hop, (high, jnp.sum(weights, axis=0, keepdims=True)))
    out = acc[pl.ds(HD, HD)] / total
    out = jnp.concatenate([out[:, :ROWS], out[:, ROWS:]], axis=0).T
    attended_f[...] = out
    attended[...] = out.astype(BF16)
    totals[...] = jnp.broadcast_to(high + jnp.log(total), totals.shape)


def attend_back_kernel(idx, q, kv_all, d_att, attended_f, totals, d_q, pairs, qp, dop, acc):
    s = idx[0]
    qp[...] = stacked_queries(q[...])
    d_out = d_att[...].astype(F32)
    left = lax.broadcasted_iota(jnp.int32, (ROWS, 128), 1) < HD
    first = jnp.where(left, 0.0, pltpu.roll(d_out, HD, 1))
    second = jnp.where(left, 0.0, d_out)
    dop[...] = jnp.concatenate([first, second], axis=0).astype(BF16)
    product = (d_out * attended_f[...]).T
    delta = jnp.concatenate(
        [
            jnp.sum(product[:HD], axis=0, keepdims=True),
            jnp.sum(product[HD:], axis=0, keepdims=True),
        ],
        axis=1,
    )
    total = totals[pl.ds(0, 1)]
    pairs[...] = jnp.zeros_like(pairs)

    def step(j, masked):
        block = load_block(kv_all, j)
        scores = nt(block, qp[...])
        if masked:
            scores = causal(scores)
        probs = jnp.exp(scores - total)
        d_probs = nt(block, dop[...])
        d_scores = (probs * (d_probs - delta)).astype(BF16)
        d_pair = (nn(d_scores, qp[...]) + nn(probs.astype(BF16), dop[...])).astype(BF16)
        for p in range(4):
            at = rows_at(2048 * p + block_position(j, p) * 64, 64)
            pairs[at] = d_pair[64 * p : 64 * p + 64]
        return tn(block, d_scores)

    acc[...] = step(s, True)

    def hop(j, carry):
        acc[...] += step(j, False)
        return carry

    lax.fori_loop(0, s, hop, 0)
    out = acc[pl.ds(0, HD)] * (HD ** -0.5)
    d_q[...] = jnp.concatenate([out[:, :ROWS], out[:, ROWS:]], axis=0).T.astype(BF16)


def put_wide(wide, values):
    for j in range(HEADS):
        for p in range(2):
            at = 512 * p + int(head_position(j, p)) * 128
            wide[pl.ds(at, 128)] = values[128 * p : 128 * p + 128, 256 * j : 256 * j + 256].astype(BF16)


def feed_kernel(x_ref, summed, cot_ref, gain, gu, dw, wide, back, xf, second_part, sn, out_acc, d_acc):
    residual = x_ref[...].astype(F32) + summed[...].astype(F32)
    r2 = lax.rsqrt(jnp.mean(residual * residual, axis=1, keepdims=True) + EPSILON)
    sn[...] = (residual * r2 * gain[...]).astype(BF16)
    out_acc[...] = jnp.zeros_like(out_acc)
    d_acc[...] = jnp.zeros_like(d_acc)

    def part(c, carry):
        cols = pl.ds(pl.multiple_of(c * 256, 256), 256)
        high = pl.ds(pl.multiple_of(c * 256 + 512, 256), 256)
        wg, wu, wd = gu[0, :, cols], gu[1, :, cols], dw[cols]
        gate, up = nn(sn[...], wg), nn(sn[...], wu)
        sig = sigmoid(gate)
        act_gate = gate * sig
        act = (act_gate * up).astype(BF16)
        out_acc[...] += nn(act, wd)
        xf[cols] = tn(act, cot_ref[...]).astype(BF16)
        d_act = nt(cot_ref[...], wd)
        d_gate = (d_act * up * (sig * (1.0 + gate * (1.0 - sig)))).astype(BF16)
        d_up = (d_act * act_gate).astype(BF16)
        xf[pl.ds(512, 1024), cols] = tn(sn[...], d_gate).astype(BF16)
        xf[pl.ds(512, 1024), high] = tn(sn[...], d_up).astype(BF16)
        d_acc[...] += nt(d_gate, wg) + nt(d_up, wu)
        return carry

    lax.fori_loop(0, 2, part, 0)
    put_wide(wide, out_acc[...])
    d_second = d_acc[...]
    residual = x_ref[...].astype(F32) + summed[...].astype(F32)
    second_part[...] = jnp.broadcast_to(
        jnp.sum(d_second * residual * r2, axis=0, keepdims=True), second_part.shape
    )
    weighted = d_second * gain[...]
    inner = jnp.sum(weighted * residual, axis=1, keepdims=True)
    back[...] = (r2 * weighted - residual * (r2 * r2 * r2 / D * inner)).astype(BF16)


def lower_kernel(cot, d_sum, gated, attended, wmo, wao, mixed, squares, mgain, xb, d_att, d_gated, mixgain, inner):
    low = (cot[...].astype(F32) + d_sum[...].astype(F32)).astype(BF16)
    for c in range(2):
        lanes = slice(512 * c, 512 * c + 512)
        xb[pl.ds(0, MW), pl.ds(512 * c, 512)] = tn(gated[...], low[:, lanes]).astype(BF16)
        xb[pl.ds(MW, 128), pl.ds(512 * c, 512)] = tn(attended[...], low[:, lanes]).astype(BF16)
    d_att[...] = nt(low, wao[...]).astype(BF16)
    dg = nt(low, wmo[...])
    d_gated[...] = dg
    scale = lax.rsqrt(column_of(squares[...]) / (MAMBA_HEADS * MP) + EPSILON)
    product = dg * mixed[...]
    mixgain[...] = jnp.broadcast_to(jnp.sum(product * scale, axis=0, keepdims=True), mixgain.shape)
    inner[...] = row_sums(product * mgain[...])


def ssd_back_kernel(
    d_gated, mixed, squares, inner, mgain, gz, ssd, post, step, cum_ref, cumt_ref, state,
    d_z, d_ssd, skip_part, d_scaled, d_bc, grad_state,
):
    scale = lax.rsqrt(column_of(squares[...]) / (MAMBA_HEADS * MP) + EPSILON)
    inner_col = column_of(inner[...])
    d_mixed = scale * (d_gated[...] * mgain[...]) - mixed[...] * (
        scale * scale * scale / (MAMBA_HEADS * MP) * inner_col
    )
    z = gz[...]
    sig = sigmoid(z)
    ds = d_mixed * (z * sig)
    d_ssd[...] = ds
    d_z[...] = (d_mixed * ssd[...] * (sig * (1.0 + z * (1.0 - sig)))).astype(BF16)
    step_x, enter_x, _ = decay_terms(step, cum_ref)
    mixer_in = post[:, pl.ds(0, MW)].astype(F32)
    skip_part[...] = jnp.broadcast_to(jnp.sum(ds * mixer_in, axis=0, keepdims=True), skip_part.shape)
    scaled = (mixer_in * step_x).astype(BF16)
    b, c = post[:, pl.ds(MW, NS)], post[:, pl.ds(MW + NS, NS)]
    gram = nt(c, b)
    mask = lower_mask()
    cum, cum_t = cum_ref[...], cumt_ref[...]
    left = lax.broadcasted_iota(jnp.int32, (ROWS, 128), 1) < MP
    low = ds.astype(BF16)
    d_gram = jnp.zeros((ROWS, ROWS), F32)
    for pair in range(3):
        lanes = slice(128 * pair, 128 * pair + 128)
        halves = []
        for k in range(2):
            decay = decay_of(cum, cum_t, 2 * pair + k, mask)
            here = left if k == 0 else jnp.logical_not(left)
            mine = jnp.where(here, ds[:, lanes], 0.0).astype(BF16)
            halves.append(tn((gram * decay).astype(BF16), low[:, lanes]))
            d_gram = d_gram + decay * nt(mine, scaled[:, lanes])
        d_scaled[:, pl.ds(128 * pair, 128)] = jnp.where(left, halves[0], halves[1])
    entered = (ds * enter_x).astype(BF16)
    grad_state[...] = tn(entered, c).astype(BF16)
    d_gram = d_gram.astype(BF16)
    d_bc[:, pl.ds(0, NS)] = tn(d_gram, c)
    d_bc[:, pl.ds(NS, NS)] = nn(d_gram, b) + nn(entered, state[...])


def conv_back_kernel(
    idx, gathered, logs, d_ssd, d_scaled, d_bc, skip, step, cum, post, pre, raw, edge,
    d_pre, kernel_grads, total, ext,
):
    chain(idx, gathered, logs, total, False)
    leaving = total[...].astype(BF16)
    step_x, _, tail_x = decay_terms(step, cum)
    b = post[:, pl.ds(MW, NS)]
    mixer_in = post[:, pl.ds(0, MW)].astype(F32)
    tail_in = (mixer_in * step_x * tail_x).astype(BF16)
    scaled_grad = d_scaled[...] + tail_x * nt(b, leaving)
    d_pre[:, pl.ds(0, MW)] = skip[...] * d_ssd[...] + scaled_grad * step_x
    d_pre[:, pl.ds(MW, NS)] = d_bc[:, pl.ds(0, NS)] + nn(tail_in, leaving)
    d_pre[:, pl.ds(MW + NS, NS)] = d_bc[:, pl.ds(NS, NS)]
    keep = jnp.where(idx[0] > 0, 1.0, 0.0)
    ext[pl.ds(0, 8)] = edge[...] * keep
    ext[pl.ds(8, ROWS)] = raw[...]
    for c in range(5):
        lanes = pl.ds(128 * c, 128)
        v = pre[:, lanes]
        sig = sigmoid(v)
        dp = d_pre[:, lanes] * (sig * (1.0 + v * (1.0 - sig)))
        d_pre[:, lanes] = dp
        rows = [jnp.sum(dp * ext[pl.ds(5 + k, ROWS), lanes], axis=0, keepdims=True) for k in range(KC)]
        rows.append(jnp.sum(dp, axis=0, keepdims=True))
        rows.append(jnp.zeros((3, 128), F32))
        kernel_grads[:, lanes] = jnp.concatenate(rows, axis=0)


def input_back_kernel(
    idx, d_pre, edge, taps, d_z, d_q, pair, normed, x_ref, gain, wm, ws, wq, wkv,
    ms, wide, first_part, ext, d_all, acc,
):
    keep = jnp.where(idx[0] < SEQ - 1, 1.0, 0.0)
    ext[pl.ds(0, ROWS)] = d_pre[...]
    ext[pl.ds(ROWS, 8)] = edge[...] * keep
    d_all[:, pl.ds(0, MW)] = d_z[...]
    for c in range(5):
        lanes = pl.ds(128 * c, 128)
        total = taps[pl.ds(0, 1), lanes] * ext[pl.ds(3, ROWS), lanes]
        for k in range(1, KC):
            total = total + taps[pl.ds(k, 1), lanes] * ext[pl.ds(3 - k, ROWS), lanes]
        to = 640 + 128 * c if c < 3 else 384 + 128 * (c - 3)
        d_all[:, pl.ds(to, 128)] = total.astype(BF16)
    d_all[:, pl.ds(1024, 128)] = d_q[...]
    d_all[:, pl.ds(1152, 128)] = pair[...]

    def part(i, carry):
        rows = pl.ds(pl.multiple_of(i * 256, 256), 256)
        late = pl.ds(pl.multiple_of(i * 256 + 1024, 256), 256)
        mine = normed[:, rows]
        ms[rows] = tn(mine, d_all[:, pl.ds(0, 640)]).astype(BF16)
        ms[late] = tn(mine, d_all[:, pl.ds(640, 640)]).astype(BF16)
        total = nt(d_all[:, pl.ds(0, 384)], wm[0, rows]) + nt(d_all[:, pl.ds(640, 384)], wm[1, rows])
        total = total + nt(d_all[:, pl.ds(384, 256)], ws[rows])
        total = total + nt(d_all[:, pl.ds(1024, 128)], wq[rows])
        total = total + nt(d_all[:, pl.ds(1152, 128)], wkv[rows])
        acc[:, rows] = total
        return carry

    lax.fori_loop(0, 4, part, 0)
    x = x_ref[...].astype(F32)
    r1 = lax.rsqrt(jnp.mean(x * x, axis=1, keepdims=True) + EPSILON)
    d_normed = acc[...]
    first_part[...] = jnp.broadcast_to(
        jnp.sum(d_normed * x * r1, axis=0, keepdims=True), first_part.shape
    )
    weighted = d_normed * gain[...]
    inner = jnp.sum(weighted * x, axis=1, keepdims=True)
    put_wide(wide, r1 * weighted - x * (r1 * r1 * r1 / D * inner))


def on_device(
    hidden_in, cotangent, log_decay, norm_gain, query_weight, keyvalue_weight, attention_output,
    mixer_weight, state_weight, kernel_mixer, kernel_state, bias_mixer, bias_state, skip_gain,
    mixer_gain, mixer_output, second_gain, gate_up, down_weight,
):
    s, h = lax.axis_index("seq"), lax.axis_index("head")
    idx = jnp.stack([s, h]).astype(jnp.int32)
    shared = h * (AH // HEADS) // (AH // KVH)
    pair_weight = lax.dynamic_slice_in_dim(keyvalue_weight, shared * HD, HD, 2)
    wkv = jnp.concatenate([pair_weight[0], pair_weight[1]], axis=1)
    gain1 = norm_gain.reshape(1, D)
    gain2 = second_gain.reshape(1, D)
    mgain = mixer_gain.reshape(1, MW)
    skip = jnp.repeat(skip_gain, MP).reshape(1, MW)
    taps = jnp.pad(jnp.concatenate([kernel_mixer, kernel_state], axis=1), ((0, 4), (0, 0)))
    bias = jnp.concatenate([bias_mixer, bias_state]).reshape(1, CW)
    decay = jnp.pad(log_decay, ((0, 0), (0, 2)))
    step = -decay
    cum = jnp.cumsum(decay, axis=0)
    cum_t = cum.T
    logs = jnp.broadcast_to(cum[ROWS - 1][:, None], (8, 128))

    normed, q, kv, gz, raw = call(
        project_kernel,
        [
            shape((ROWS, D), BF16), shape((ROWS, 128), BF16), shape((ROWS, 128), BF16),
            shape((ROWS, MW), F32), shape((ROWS, CW), F32),
        ],
        (hidden_in, gain1, query_weight, wkv, mixer_weight, state_weight),
    )
    kv_all, edge, logs_all = call(
        keyval_kernel,
        [shape((8192, 128), BF16), shape((8, CW), F32), shape((256, 128), F32)],
        (kv, raw[ROWS - 8 :], logs),
        collective=1, copies=26,
    )
    pre, post, local_state = call(
        conv_kernel,
        [shape((ROWS, CW), F32), shape((ROWS, CW), BF16), shape((MW, NS), BF16)],
        (idx, raw, edge, taps, bias, step, cum),
        scratch=[pltpu.VMEM((ROWS + 8, CW), F32)], smem=1,
    )
    (states,) = call(
        state_kernel, [shape((12288, NS), BF16)], (local_state,), collective=2, copies=20
    )
    attended, attended_f, totals = call(
        attend_kernel,
        [shape((ROWS, 128), BF16), shape((ROWS, 128), F32), shape((8, 512), F32)],
        (idx, q, kv_all),
        scratch=[pltpu.VMEM((512, 128), BF16), pltpu.VMEM((128, 512), F32)], smem=1,
    )
    ssd, mixed, squares, state = call(
        ssd_kernel,
        [shape((ROWS, MW), F32), shape((ROWS, MW), F32), shape((8, ROWS), F32), shape((MW, NS), BF16)],
        (idx, post, step, cum, cum_t, skip, gz, states, logs_all),
        scratch=[pltpu.VMEM((MW, NS), F32)], smem=1,
    )
    (squares,) = call(
        sums_kernel, [shape((8, ROWS), F32)], (squares,),
        scratch=[pltpu.VMEM((HEADS, 8, ROWS), F32)], collective=3, copies=3,
    )
    gated, part = call(
        outputs_kernel,
        [shape((ROWS, MW), BF16), shape((ROWS, D), BF16)],
        (mixed, squares, mgain, mixer_output, attended, attention_output),
    )
    (summed,) = call(
        head_sum_kernel, [shape((ROWS, D), BF16)], (part,),
        scratch=[pltpu.VMEM((ROWS, D), BF16)] * 2, collective=4, copies=8,
    )
    wide, back, xf, second_part = call(
        feed_kernel,
        [
            shape((1024, 256), BF16), shape((ROWS, D), BF16), shape((1536, D), BF16),
            shape((8, D), F32),
        ],
        (hidden_in, summed, cotangent, gain2, gate_up, down_weight),
        scratch=[pltpu.VMEM((ROWS, D), BF16), pltpu.VMEM((ROWS, D), F32), pltpu.VMEM((ROWS, D), F32)],
    )
    d_sum, out_share = call(
        second_sum_kernel,
        [shape((ROWS, D), BF16), shape((ROWS, 256), BF16)],
        (back, wide),
        scratch=[pltpu.VMEM((ROWS, D), BF16)] * 2 + [pltpu.VMEM((1024, 256), BF16)] * 2,
        collective=5, copies=12,
    )
    xb, d_att, d_gated, mixgain, inner = call(
        lower_kernel,
        [
            shape((512, D), BF16), shape((ROWS, 128), BF16), shape((ROWS, MW), F32),
            shape((8, MW), F32), shape((8, ROWS), F32),
        ],
        (cotangent, d_sum, gated, attended, mixer_output, attention_output, mixed, squares, mgain),
    )
    (inner,) = call(
        sums_kernel, [shape((8, ROWS), F32)], (inner,),
        scratch=[pltpu.VMEM((HEADS, 8, ROWS), F32)], collective=3, copies=3,
    )
    d_z, d_ssd, skip_part, d_scaled, d_bc, grad_state = call(
        ssd_back_kernel,
        [
            shape((ROWS, MW), BF16), shape((ROWS, MW), F32), shape((8, MW), F32),
            shape((ROWS, MW), F32), shape((ROWS, 256), F32), shape((MW, NS), BF16),
        ],
        (d_gated, mixed, squares, inner, mgain, gz, ssd, post, step, cum, cum_t, state),
    )
    (grad_states,) = call(
        state_kernel, [shape((12288, NS), BF16)], (grad_state,), collective=2, copies=20
    )
    d_pre, kernel_grads = call(
        conv_back_kernel,
        [shape((ROWS, CW), F32), shape((8, CW), F32)],
        (idx, grad_states, logs_all, d_ssd, d_scaled, d_bc, skip, step, cum, post, pre, raw, edge),
        scratch=[pltpu.VMEM((MW, NS), F32), pltpu.VMEM((ROWS + 8, CW), F32)], smem=1,
    )
    d_q, pairs = call(
        attend_back_kernel,
        [shape((ROWS, 128), BF16), shape((8192, 128), BF16)],
        (idx, q, kv_all, d_att, attended_f, totals),
        scratch=[
            pltpu.VMEM((512, 128), BF16), pltpu.VMEM((512, 128), BF16), pltpu.VMEM((128, 512), F32),
        ],
        smem=1,
    )
    pair, edge_back = call(
        pair_kernel,
        [shape((ROWS, 128), BF16), shape((8, CW), F32)],
        (pairs, d_pre[:8]),
        scratch=[pltpu.VMEM((8192, 128), BF16)] * 2, collective=6, copies=21,
    )
    ms, back_wide, first_part = call(
        input_back_kernel,
        [shape((2048, CW), BF16), shape((1024, 256), BF16), shape((8, D), F32)],
        (
            idx, d_pre, edge_back, taps, d_z, d_q, pair, normed, hidden_in, gain1, mixer_weight,
            state_weight, query_weight, wkv,
        ),
        scratch=[
            pltpu.VMEM((ROWS + 8, CW), F32), pltpu.VMEM((ROWS, 1280), BF16), pltpu.VMEM((ROWS, D), F32),
        ],
        smem=1,
    )
    blank = jnp.zeros((256,), F32)
    small = jnp.stack(
        [
            first_part[0],
            second_part[0],
            kernel_grads[:KC, MW:].reshape(-1),
            jnp.concatenate([kernel_grads[KC, MW:], blank, blank, blank]),
            jnp.concatenate([kernel_grads[0, :MW], kernel_grads[KC, :MW], blank]),
            jnp.concatenate([kernel_grads[1, :MW], mixgain[0], blank]),
            jnp.concatenate([kernel_grads[2, :MW], skip_part[0], blank]),
            jnp.concatenate([kernel_grads[3, :MW], blank, blank, blank[:128]]),
        ]
    )
    x_out, ms_out, in_share, small = call(
        final_kernel,
        [
            shape((2048, D), BF16), shape((2048, 768), BF16), shape((ROWS, 256), BF16),
            shape((8, D), F32),
        ],
        (xf, xb, ms, back_wide, small),
        scratch=[
            pltpu.VMEM((2048, D), BF16), pltpu.VMEM((2048, D), BF16),
            pltpu.VMEM((2048, CW), BF16), pltpu.VMEM((2048, CW), BF16),
            pltpu.VMEM((1024, 256), BF16), pltpu.VMEM((1024, 256), BF16),
            pltpu.VMEM((HEADS, 64, 256), BF16),
            pltpu.VMEM((8, 128), F32), pltpu.VMEM((8, 128), F32),
            pltpu.VMEM((HEADS, 8, D), F32),
            pltpu.VMEM((6, 8, D), F32), pltpu.VMEM((5, 8, D), F32),
        ],
        collective=7, copies=100,
    )

    def columns(values):
        return lax.dynamic_slice_in_dim(values, h * 256, 256, 1).astype(F32)

    block_out = columns(hidden_in) + columns(summed) + out_share.astype(F32)
    input_grads = columns(cotangent) + columns(d_sum) + in_share.astype(F32)
    x_f = x_out
    gateup = x_f[512:1536]
    head, tail = ms_out[:1024], ms_out[1024:]
    gateup_grads = jnp.stack([gateup[:, :512], gateup[:, 512:]]).astype(F32)
    mixer_grads = jnp.stack([head[:, :MW], tail[:, :MW]]).astype(F32)
    keys = jnp.concatenate([tail[:, 512:576], tail[:, 640:704]], axis=1)
    values = jnp.concatenate([tail[:, 576:640], tail[:, 704:768]], axis=1)
    return (
        block_out,
        input_grads,
        small[0],
        tail[:, MW:512].astype(F32),
        jnp.stack([keys, values]).astype(F32),
        x_f[1920:].astype(F32),
        mixer_grads,
        head[:, MW:640].astype(F32),
        small[4:8, :MW],
        small[2].reshape(KC, 256),
        small[4, MW : 2 * MW],
        small[3, :256],
        jnp.sum(small[6, MW : 2 * MW].reshape(HMH, MP), axis=1),
        small[5, MW : 2 * MW],
        x_f[1536:1920].astype(F32),
        small[1],
        gateup_grads,
        x_f[:512].astype(F32),
    )


def solution(mesh):
    return jax.shard_map(
        on_device,
        mesh=mesh,
        in_specs=(
            P("seq", None), P("seq", None), P("seq", "head"), P(), P(None, "head"), P(),
            P("head", None), P(None, None, "head"), P(), P(None, "head"), P(), P("head"), P(),
            P("head"), P("head"), P("head", None), P(), P(None, None, "head"), P("head", None),
        ),
        out_specs=(
            P("seq", "head"), P("seq", "head"), P(), P(None, "head"), P(), P("head", None),
            P(None, None, "head"), P(), P(None, "head"), P(), P("head"), P(), P("head"), P("head"),
            P("head", None), P(), P(None, None, "head"), P("head", None),
        ),
        check_vma=False,
    )
```

profile of v0, /device:TPU:1, one launch (start us, length us, event | category | flops | bytes accessed | tf_op | source)
XLA Modules:
  0.0 331.4 jit_solution(18348185925048242579)
XLA Ops:
  5.8 1.2 dynamic-slice_bitcast_fusion.1
  8.0 2.6 shard_map.322
  11.4 25.0 %shard_map.323 = (bf16[8192,128]{1,0:T(8,128)(2,1)S(1)}, f32[8,640]{1,0:T(8,128)S(1)}, f32[256,128]{1,0:T(8,128)S(1)}) custom-call(bf16[256,128]{1,0:T(8,128)(2,1)S(1)} %get-tuple-element.69.kv, f32[8,640]{1,0:T(8,128)S(1)} %slice.135.edge, f32[8,128]{1,0:T(8,128)S(1)} %broadcast_in_dim.14.logs), custom_call_target="tpu_custom_call" | custom-call | tf_op jit(solution)/shard_map/pallas_call | solution.py:236
  36.5 1.7 shard_map.328
  38.2 2.0 shard_map.324
  40.2 34.6 %shard_map.325.gathered = bf16[12288,128]{1,0:T(8,128)(2,1)S(1)} custom-call(bf16[384,128]{1,0:T(8,128)(2,1)S(1)} %get-tuple-element.73.state), custom_call_target="tpu_custom_call" | custom-call | tf_op jit(solution)/shard_map/pallas_call | solution.py:236
  74.9 1.7 copy-done.1
  76.5 4.2 %shard_map.326 = (f32[256,384]{1,0:T(8,128)S(1)}, f32[256,384]{1,0:T(8,128)S(1)}, f32[8,256]{1,0:T(8,128)S(1)}, bf16[384,128]{1,0:T(8,128)(2,1)S(1)}) custom-call(s32[2]{0:T(128)S(1)} %pad_add_fusion.idx, bf16[256,640]{1,0:T(8,128)(2,1)S(1)} %get-tuple-element.71.post, f32[256,8]{1,0:T(8,128)S(1)} %get-tuple-element.136.step, f32[256,8]{1,0:T(8,128)S(1)} %bitcast.44, ...), custom_call_target="tpu_custom_call" | custom-call | tf_op jit(solution)/shard_map/pallas_call | solution.py:236
  80.7 4.9 %shard_map.327.squares = f32[8,256]{1,0:T(8,128)S(1)} custom-call(f32[8,256]{1,0:T(8,128)S(1)} %get-tuple-element.76.part), custom_call_target="tpu_custom_call" | custom-call | tf_op jit(solution)/shard_map/pallas_call | solution.py:236
  86.7 15.2 %shard_map.330.summed = bf16[256,1024]{1,0:T(8,128)(2,1)S(1)} custom-call(bf16[256,1024]{1,0:T(8,128)(2,1)S(1)} %get-tuple-element.80.part), custom_call_target="tpu_custom_call" | custom-call | tf_op jit(solution)/shard_map/pallas_call | solution.py:236
  102.0 8.0 %shard_map.331 = (bf16[1024,256]{1,0:T(8,128)(2,1)S(1)}, bf16[256,1024]{1,0:T(8,128)(2,1)S(1)}, bf16[1536,1024]{1,0:T(8,128)(2,1)}, f32[8,1024]{1,0:T(8,128)S(1)}) custom-call(bf16[256,1024]{1,0:T(8,128)(2,1)S(1)} %copy-done.3, bf16[256,1024]{1,0:T(8,128)(2,1)S(1)} %shard_map.330.summed, bf16[256,1024]{1,0:T(8,128)(2,1)S(1)} %copy-done.5, ...), custom_call_target="tpu_custom_call" | custom-call | tf_op jit(solution)/shard_map/pallas_call | solution.py:236
  110.0 16.9 %shard_map.332 = (bf16[256,1024]{1,0:T(8,128)(2,1)S(1)}, bf16[256,256]{1,0:T(8,128)(2,1)S(1)}) custom-call(bf16[256,1024]{1,0:T(8,128)(2,1)S(1)} %get-tuple-element.81.part, bf16[1024,256]{1,0:T(8,128)(2,1)S(1)} %get-tuple-element.82.wide), custom_call_target="tpu_custom_call" | custom-call | tf_op jit(solution)/shard_map/pallas_call | solution.py:236
  127.0 2.3 shard_map.333
  129.3 3.0 shard_map.338
  132.3 4.6 %shard_map.334.inner = f32[8,256]{1,0:T(8,128)S(1)} custom-call(f32[8,256]{1,0:T(8,128)S(1)} %get-tuple-element.89.part), custom_call_target="tpu_custom_call" | custom-call | tf_op jit(solution)/shard_map/pallas_call | solution.py:236
  137.0 2.1 shard_map.335
  139.1 44.4 %shard_map.336.gathered = bf16[12288,128]{1,0:T(8,128)(2,1)S(1)} custom-call(bf16[384,128]{1,0:T(8,128)(2,1)S(1)} %get-tuple-element.92.state), custom_call_target="tpu_custom_call" | custom-call | tf_op jit(solution)/shard_map/pallas_call | solution.py:236
  183.6 1.7 copy-done
  185.2 5.5 %shard_map.337 = (f32[256,640]{1,0:T(8,128)S(1)}, f32[8,640]{1,0:T(8,128)S(1)}) custom-call(s32[2]{0:T(128)S(1)} %pad_add_fusion.idx, bf16[12288,128]{1,0:T(8,128)(2,1)} %copy-done, f32[256,128]{1,0:T(8,128)S(1)} %get-tuple-element.74.logs, f32[256,384]{1,0:T(8,128)S(1)} %get-tuple-element.93.d_ssd, f32[256,384]{1,0:T(8,128)S(1)} %get-tuple-element.94.d_scaled, ...), custom_call_target="tpu_custom_call" | custom-call | tf_op jit(solution)/shard_map/pallas_call | solution.py:236
  190.9 17.6 %shard_map.339 = (bf16[256,128]{1,0:T(8,128)(2,1)S(1)}, f32[8,640]{1,0:T(8,128)S(1)}) custom-call(bf16[8192,128]{1,0:T(8,128)(2,1)S(1)} %get-tuple-element.101.pairs, f32[8,640]{1,0:T(8,128)S(1)} %slice.139.edge), custom_call_target="tpu_custom_call" | custom-call | tf_op jit(solution)/shard_map/pallas_call | solution.py:236
  208.5 6.0 %shard_map.340 = (bf16[2048,640]{1,0:T(8,128)(2,1)}, bf16[1024,256]{1,0:T(8,128)(2,1)S(1)}, f32[8,1024]{1,0:T(8,128)S(1)}) custom-call(s32[2]{0:T(128)S(1)} %pad_add_fusion.idx, f32[256,640]{1,0:T(8,128)S(1)} %get-tuple-element.97.d_pre, f32[8,640]{1,0:T(8,128)S(1)} %get-tuple-element.102.edge, f32[8,640]{1,0:T(8,128)S(1)} %copy-done.18, ...), custom_call_target="tpu_custom_call" | custom-call | tf_op jit(solution)/shard_map/pallas_call | solution.py:236
  216.4 91.6 %shard_map.341 = (bf16[2048,1024]{1,0:T(8,128)(2,1)}, bf16[2048,768]{1,0:T(8,128)(2,1)}, bf16[256,256]{1,0:T(8,128)(2,1)S(1)}, f32[8,1024]{1,0:T(8,128)S(1)}) custom-call(bf16[1536,1024]{1,0:T(8,128)(2,1)} %get-tuple-element.85.xf, bf16[512,1024]{1,0:T(8,128)(2,1)S(1)} %copy-done.7, bf16[2048,640]{1,0:T(8,128)(2,1)} %get-tuple-element.107.ms, ...), custom_call_target="tpu_custom_call" | custom-call | tf_op jit(solution)/shard_map/pallas_call | solution.py:236
  308.1 1.8 convert_add_fusion
  313.6 1.8 slice_convert_fusion.4
  315.4 1.8 slice_convert_fusion.3
  317.1 2.1 slice_convert_fusion.2
  319.2 1.5 fusion
  320.7 1.5 slice_bitcast_fusion.3
  323.6 1.9 maximum_convert_fusion.1
  326.0 1.3 slice_convert_fusion.1
  327.4 1.6 slice_convert_fusion
  329.1 2.3 maximum_convert_fusion
  (100 shorter events, 15.6 us)
Async XLA Ops:
  0.7 6.6 %copy-start.3 = (bf16[256,1024]{1,0:T(8,128)(2,1)S(1)}, bf16[256,1024]{1,0:T(8,128)(2,1)}, u32[]{:S(2)}) copy-start(bf16[256,1024]{1,0:T(8,128)(2,1)} %x_ref.5) | copy-start | bytes 1572868
  0.7 6.6 %copy-start.6 = (bf16[1024,256]{1,0:T(8,128)(2,1)S(1)}, bf16[1024,256]{1,0:T(8,128)(2,1)}, u32[]{:S(2)}) copy-start(bf16[1024,256]{1,0:T(8,128)(2,1)} %ws.3) | copy-start | bytes 1572868
  0.7 6.6 %copy-start.8 = (bf16[1024,128]{1,0:T(8,128)(2,1)S(1)}, bf16[1024,128]{1,0:T(8,128)(2,1)}, u32[]{:S(2)}) copy-start(bf16[1024,128]{1,0:T(8,128)(2,1)} %wq.3) | copy-start | bytes 786436
  3.1 71.8 %copy-start.23 = (f32[1,384]{1,0:T(1,128)}, f32[1,384]{1,0:T(1,128)S(1)}, u32[]{:S(2)}) copy-start(f32[1,384]{1,0:T(1,128)S(1)} %reshape_reshape.3.skip) | copy-start | bytes 4612
  3.8 34.4 %copy-start.17 = (f32[8,640]{1,0:T(8,128)}, f32[8,640]{1,0:T(8,128)S(1)}, u32[]{:S(2)}) copy-start(f32[8,640]{1,0:T(8,128)S(1)} %select_maximum_fusion.taps) | copy-start | bytes 61444
  7.3 0.7 copy-start.21
  10.6 0.8 copy-start.15
  36.5 38.4 %copy-start.2 = (bf16[8192,128]{1,0:T(8,128)(2,1)}, bf16[8192,128]{1,0:T(8,128)(2,1)S(1)}, u32[]{:S(2)}) copy-start(bf16[8192,128]{1,0:T(8,128)(2,1)S(1)} %get-tuple-element.78.kv_all) | copy-start | bytes 6291460
  40.2 45.4 %copy-start.4 = (bf16[384,1024]{1,0:T(8,128)(2,1)S(1)}, bf16[384,1024]{1,0:T(8,128)(2,1)}, u32[]{:S(2)}) copy-start(bf16[384,1024]{1,0:T(8,128)(2,1)} %wmo.3) | copy-start | bytes 2359300
  40.2 45.4 %copy-start.11 = (bf16[128,1024]{1,0:T(8,128)(2,1)S(1)}, bf16[128,1024]{1,0:T(8,128)(2,1)}, u32[]{:S(2)}) copy-start(bf16[128,1024]{1,0:T(8,128)(2,1)} %wao.3) | copy-start | bytes 786436
  74.9 1.7 copy-start.1
  76.5 25.4 %copy-start.5 = (bf16[256,1024]{1,0:T(8,128)(2,1)S(1)}, bf16[256,1024]{1,0:T(8,128)(2,1)}, u32[]{:S(2)}) copy-start(bf16[256,1024]{1,0:T(8,128)(2,1)} %cot.1) | copy-start | bytes 1572868
  76.5 25.4 %copy-start.10 = (bf16[512,1024]{1,0:T(8,128)(2,1)S(1)}, bf16[512,1024]{1,0:T(8,128)(2,1)}, u32[]{:S(2)}) copy-start(bf16[512,1024]{1,0:T(8,128)(2,1)} %dw.1) | copy-start | bytes 3145732
  76.5 25.4 %copy-start.25 = (f32[1024]{0:T(1024)S(1)}, f32[1024]{0:T(1024)}, u32[]{:S(2)}) copy-start(f32[1024]{0:T(1024)} %param.35) | copy-start | bytes 12292
  127.0 2.4 copy-start.12
  127.0 12.1 %copy-start.19 = (bf16[256,256]{1,0:T(8,128)(2,1)}, bf16[256,256]{1,0:T(8,128)(2,1)S(1)}, u32[]{:S(2)}) copy-start(bf16[256,256]{1,0:T(8,128)(2,1)S(1)} %get-tuple-element.83) | copy-start | bytes 393220
  132.3 52.9 %copy-start.24 = (f32[1,384]{1,0:T(1,128)S(1)}, f32[1,384]{1,0:T(1,128)}, u32[]{:S(2)}) copy-start(f32[1,384]{1,0:T(1,128)} %copy-done.23) | copy-start | bytes 4612
  183.5 1.7 copy-start
  185.2 23.3 %copy-start.9 = (bf16[1024,128]{1,0:T(8,128)(2,1)S(1)}, bf16[1024,128]{1,0:T(8,128)(2,1)}, u32[]{:S(2)}) copy-start(bf16[1024,128]{1,0:T(8,128)(2,1)} %wq.3) | copy-start | bytes 786436
  185.2 23.3 %copy-start.16 = (bf16[256,1024]{1,0:T(8,128)(2,1)S(1)}, bf16[256,1024]{1,0:T(8,128)(2,1)}, u32[]{:S(2)}) copy-start(bf16[256,1024]{1,0:T(8,128)(2,1)} %copy-done.15) | copy-start | bytes 1572868
  185.2 23.3 %copy-start.18 = (f32[8,640]{1,0:T(8,128)S(1)}, f32[8,640]{1,0:T(8,128)}, u32[]{:S(2)}) copy-start(f32[8,640]{1,0:T(8,128)} %copy-done.17) | copy-start | bytes 61444
  185.2 23.3 %copy-start.22 = (f32[1024]{0:T(1024)S(1)}, f32[1024]{0:T(1024)}, u32[]{:S(2)}) copy-start(f32[1024]{0:T(1024)} %param.22) | copy-start | bytes 12292
  190.9 24.5 %copy-start.7 = (bf16[512,1024]{1,0:T(8,128)(2,1)S(1)}, bf16[512,1024]{1,0:T(8,128)(2,1)}, u32[]{:S(2)}) copy-start(bf16[512,1024]{1,0:T(8,128)(2,1)} %get-tuple-element.87.xb) | copy-start | bytes 3145732
  214.5 0.8 copy-start.13
  215.4 1.0 copy-start.14
  216.4 91.6 %copy-start.20 = (bf16[256,256]{1,0:T(8,128)(2,1)S(1)}, bf16[256,256]{1,0:T(8,128)(2,1)}, u32[]{:S(2)}) copy-start(bf16[256,256]{1,0:T(8,128)(2,1)} %copy-done.19) | copy-start | bytes 393220
  322.5 3.5 %copy-start.26 = (bf16[2048,1024]{1,0:T(8,128)(2,1)S(1)}, bf16[2048,1024]{1,0:T(8,128)(2,1)}, u32[]{:S(2)}) copy-start(bf16[2048,1024]{1,0:T(8,128)(2,1)} %get-tuple-element.117) | copy-start | bytes 12582916
where the time goes:
time: 332 us; the launch traced here: 331 us
  Pallas kernels  293 us (88%)
  other arithmetic  18.8 us (6%)
  local copies, waits for them, and re-layouts  17.8 us (5%)
    pallas_call x20, Pallas kernels, call(): pl.pallas_call(body, out_shape=tuple(outs), in_specs=in_specs, out_specs=...  293 us
    unnamed x57, local copies, waits for them, and re-layouts  8.13 us

commit v1 on v0

--- a/solution.py
+++ b/solution.py
@@ -116,13 +116,19 @@
         }
         self.send_sem, self.recv_sem, self.used = send_sem, recv_sem, 0
 
-    def barrier(self, names):
+    def greet(self, names):
         semaphore = pltpu.get_barrier_semaphore()
         for name in names:
             pl.semaphore_signal(
                 semaphore, inc=1, device_id=self.partner[name], device_id_type=MESH
             )
-        pl.semaphore_wait(semaphore, len(names))
+
+    def met(self, names):
+        pl.semaphore_wait(pltpu.get_barrier_semaphore(), len(names))
+
+    def barrier(self, names):
+        self.greet(names)
+        self.met(names)
 
     def send(self, src, dst, name):
         k = self.used
@@ -139,6 +145,7 @@
         return copy
 
 
+DONE = object()
 SEQ_NAMES = ("c", "ya", "yb", "za", "zb")
 
 
@@ -198,10 +205,11 @@
         self.start = self.start - self.links.bits[self.path[step]] * size
 
 
-def reduce_all(jobs):
+def reduce_steps(jobs):
     for job in jobs:
         job.begin(0)
     for step in range(max(len(job.path) for job in jobs)):
+        yield
         for job in jobs:
             if step < len(job.path):
                 job.finish(step)
@@ -209,16 +217,38 @@
                     job.begin(step + 1)
 
 
-def gather_all(jobs, columns=None):
+def gather_steps(jobs, columns=None):
     columns = columns or [None] * len(jobs)
     for job, width in zip(jobs, columns):
         job.send_back(len(job.path) - 1, width)
     for step in range(max(len(job.path) for job in jobs) - 1, -1, -1):
+        yield
         for job, width in zip(jobs, columns):
             if step < len(job.path):
                 job.wait_back(step)
                 if step:
                     job.send_back(step - 1, width)
+
+
+def finish(*runs):
+    runs = list(runs)
+    while runs:
+        for run in list(runs):
+            if next(run, DONE) is DONE:
+                runs.remove(run)
+
+
+def advance(*runs):
+    for run in runs:
+        next(run, DONE)
+
+
+def reduce_all(jobs):
+    finish(reduce_steps(jobs))
+
+
+def gather_all(jobs, columns=None):
+    finish(gather_steps(jobs, columns))
 
 
 def call(body, outs, args, scratch=(), collective=None, smem=0, copies=0, cost=None):
@@ -264,15 +294,6 @@
     return jobs
 
 
-def keyval_kernel(kv, edge, logs, kv_all, edge_in, logs_all, send_sem, recv_sem):
-    links = Links(send_sem, recv_sem)
-    jobs = gather_rows(links, kv, kv_all) + gather_rows(links, logs, logs_all, SEQ_PATHS[:1])
-    links.barrier(SEQ_NAMES + ("next", "prev"))
-    edge_copy = links.send(edge, edge_in, "next")
-    gather_all(jobs)
-    edge_copy.wait()
-
-
 def state_kernel(state, state_all, send_sem, recv_sem):
     links = Links(send_sem, recv_sem)
     jobs = gather_rows(links, state, state_all)
@@ -288,17 +309,6 @@
     for copy in copies:
         copy.wait()
     total[...] = (slots[0] + slots[1]) + (slots[2] + slots[3])
-
-
-def head_sum_kernel(part, total, work, recv, send_sem, recv_sem):
-    links = Links(send_sem, recv_sem)
-    links.barrier(("xa", "xb"))
-    jobs = [
-        Reduce(links, path, 128, part, 128 * p, work, recv, total, 128 * p)
-        for p, path in enumerate(HEAD_PATHS)
-    ]
-    reduce_all(jobs)
-    gather_all(jobs)
 
 
 def own_rows(job, count):
@@ -339,7 +349,7 @@
 def final_kernel(
     xf, xb, ms, wide, small,
     x_out, ms_out, share, small_out,
-    x_work, x_recv, ms_work, ms_recv, wide_work, wide_recv, head_slots, small_y, small_z, small_x,
+    x_work, x_recv, ms_work, ms_recv, wide_work, wide_recv, head_slots, small_x,
     small_work, small_recv, send_sem, recv_sem,
 ):
     links = Links(send_sem, recv_sem)
@@ -360,18 +370,25 @@
         for p, path in enumerate(HEAD_PATHS)
     ]
     small_work[0] = small[...]
-    small_steps = ("c", "ya", "yb", "za", "zb")
-    reduce_all(shares)
+
+    def vectors():
+        for step, name in enumerate(SEQ_NAMES):
+            copy = links.send(small_work.at[step], small_recv.at[step], name)
+            yield
+            copy.wait()
+            small_work[step + 1] = small_work[step] + small_recv[step]
+        small_x[links.h] = small_work[5]
+        copies = [links.send(small_work.at[5], small_x.at[links.h], n) for n in ("x1", "x2", "x3")]
+        yield
+        for copy in copies:
+            copy.wait()
+        total = (small_x[0] + small_x[1]) + (small_x[2] + small_x[3])
+        row = lax.broadcasted_iota(jnp.int32, (8, 1024), 0)
+        small_out[...] = jnp.where(row < 4, total, small_work[5])
+
+    finish(reduce_steps(x_jobs + ms_jobs), reduce_steps(shares), vectors())
     for p, job in enumerate(shares):
         share[pl.ds(128 * p, 128)] = own_rows(job, 128)
-    for step, name in enumerate(small_steps):
-        copy = links.send(small_work.at[step], small_recv.at[step], name)
-        copy.wait()
-        small_work[step + 1] = small_work[step] + small_recv[step]
-    small_x[links.h] = small_work[5]
-    small_copies = [links.send(small_work.at[5], small_x.at[links.h], n) for n in ("x1", "x2", "x3")]
-    reduce_all(x_jobs + ms_jobs)
-    head_copies = []
     for p, job in enumerate(ms_jobs):
         at = rows_at(job.base + job.start, 16)
         if p < 2:
@@ -381,11 +398,6 @@
         head_slots[links.h, pl.ds(16 * p, 16)] = piece
     slot = head_slots.at[links.h]
     head_copies = [links.send(slot, slot, n) for n in ("x1", "x2", "x3")]
-    for copy in small_copies:
-        copy.wait()
-    total = (small_x[0] + small_x[1]) + (small_x[2] + small_x[3])
-    row = lax.broadcasted_iota(jnp.int32, (8, 1024), 0)
-    small_out[...] = jnp.where(row < 4, total, small_work[5])
     for copy in head_copies:
         copy.wait()
     for p, job in enumerate(ms_jobs):
@@ -402,18 +414,6 @@
     gather_all(x_jobs + ms_jobs, [None] * 4 + [640, 640, None, None])
 
 
-def project_kernel(x_ref, gain, wq, wkv, wm, ws, normed, q, kv, gz, raw):
-    x = x_ref[...].astype(F32)
-    r1 = lax.rsqrt(jnp.mean(x * x, axis=1, keepdims=True) + EPSILON)
-    n = (x * r1 * gain[...]).astype(BF16)
-    normed[...] = n
-    q[...] = nn(n, wq[...]).astype(BF16)
-    kv[...] = nn(n, wkv[...]).astype(BF16)
-    gz[...] = nn(n, wm[0])
-    raw[:, pl.ds(0, MW)] = nn(n, wm[1])
-    raw[:, pl.ds(MW, 256)] = nn(n, ws[...])
-
-
 def widen(values):
     lane = lax.broadcasted_iota(jnp.int32, (8, MW), 1)
     row = lax.broadcasted_iota(jnp.int32, (8, MW), 0)
@@ -430,24 +430,17 @@
     return step_x, enter_x, tail_x
 
 
-def conv_kernel(idx, raw, edge, taps, bias, step, cum, pre, post, state, ext):
-    keep = jnp.where(idx[0] > 0, 1.0, 0.0)
-    ext[pl.ds(0, 8)] = edge[...] * keep
-    ext[pl.ds(8, ROWS)] = raw[...]
+def conv_forward(ext, taps, bias, pre, post):
     for c in range(5):
         lanes = pl.ds(128 * c, 128)
-        total = bias[:, lanes] + taps[pl.ds(0, 1), lanes] * ext[pl.ds(5, ROWS), lanes]
+        total = bias[:, lanes] + taps[pl.ds(0, 1), lanes] * ext[pl.ds(13, ROWS), lanes]
         for k in range(1, KC):
-            total = total + taps[pl.ds(k, 1), lanes] * ext[pl.ds(5 + k, ROWS), lanes]
+            total = total + taps[pl.ds(k, 1), lanes] * ext[pl.ds(13 + k, ROWS), lanes]
         pre[:, lanes] = total
         post[:, lanes] = (total * sigmoid(total)).astype(BF16)
-    step_x, _, tail_x = decay_terms(step, cum)
-    tail_in = (post[:, pl.ds(0, MW)].astype(F32) * step_x * tail_x).astype(BF16)
-    state[...] = tn(tail_in, post[:, pl.ds(MW, NS)]).astype(BF16)
-
-
-def chain(idx, gathered, logs, total, forward):
-    s = idx[0]
+
+
+def chain(s, gathered, logs, total, forward):
     total[...] = jnp.zeros_like(total)
 
     def hop(i, run):
@@ -482,12 +475,7 @@
     return exact(rows, jnp.full((8, 128), 0.125, F32), ((0,), (0,)))[:, 0:1]
 
 
-def ssd_kernel(
-    idx, post, step, cum_ref, cumt_ref, skip, gz, gathered, logs, ssd, mixed, squares, state, total
-):
-    chain(idx, gathered, logs, total, True)
-    state[...] = total[...].astype(BF16)
-    step_x, enter_x, _ = decay_terms(step, cum_ref)
+def ssd_forward(post, step_x, enter_x, cum_ref, cumt_ref, skip, gz, state, ssd, mixed, squares):
     mixer_in = post[:, pl.ds(0, MW)].astype(F32)
     scaled = (mixer_in * step_x).astype(BF16)
     b, c = post[:, pl.ds(MW, NS)], post[:, pl.ds(MW + NS, NS)]
@@ -507,15 +495,6 @@
     squares[...] = row_sums(m * m)
 
 
-def outputs_kernel(mixed, squares, mgain, wmo, attended, wao, gated, part):
-    scale = lax.rsqrt(column_of(squares[...]) / (MAMBA_HEADS * MP) + EPSILON)
-    g = (mixed[...] * scale * mgain[...]).astype(BF16)
-    gated[...] = g
-    for c in range(2):
-        lanes = pl.ds(512 * c, 512)
-        part[:, lanes] = (nn(attended[...], wao[:, lanes]) + nn(g, wmo[:, lanes])).astype(BF16)
-
-
 def load_block(kv_all, j):
     return jnp.concatenate(
         [kv_all[rows_at(2048 * p + block_position(j, p) * 64, 64)] for p in range(4)], axis=0
@@ -537,14 +516,59 @@
     return jnp.concatenate([first, second], axis=0).astype(BF16)
 
 
-def attend_kernel(idx, q, kv_all, attended, attended_f, totals, qp, acc):
-    s = idx[0]
+FORWARD_NAMES = SEQ_NAMES + ("next", "prev", "x1", "x2", "x3")
+
+
+def forward_kernel(
+    x_ref, gain, wq, wkv, wm, ws, taps, bias, step, cum_ref, cumt_ref, logs, skip, mgain, wmo, wao,
+    normed, q, kv_all, logs_all, gz, ext, pre, post, attended, attended_f, totals, ssd, mixed,
+    squares, state, gated, summed,
+    kv, x_edge, edge_normed, local, states, chained, qp, acc, own_squares, slots, proj, part, work,
+    recv, send_sem, recv_sem,
+):
+    links = Links(send_sem, recv_sem)
+    s = links.s
+    links.greet(FORWARD_NAMES)
+
+    def normalise(rows):
+        x = rows.astype(F32)
+        r1 = lax.rsqrt(jnp.mean(x * x, axis=1, keepdims=True) + EPSILON)
+        return (x * r1 * gain[...]).astype(BF16)
+
+    n = normalise(x_ref[...])
+    normed[...] = n
+    kv[...] = nn(n, wkv[...]).astype(BF16)
+    q[...] = nn(n, wq[...]).astype(BF16)
+    key_jobs = gather_rows(links, kv, kv_all) + gather_rows(links, logs, logs_all, SEQ_PATHS[:1])
+    links.met(FORWARD_NAMES)
+    edge_copy = links.send(x_ref.at[pl.ds(ROWS - 16, 16)], x_edge, "next")
+    keys = gather_steps(key_jobs)
+    advance(keys)
+    gz[...] = nn(normed[...], wm[0])
+    advance(keys)
+    ext[pl.ds(16, ROWS), pl.ds(0, MW)] = nn(normed[...], wm[1])
+    ext[pl.ds(16, ROWS), pl.ds(MW, 256)] = nn(normed[...], ws[...])
+    edge_copy.wait()
+    advance(keys)
+    keep = jnp.where(s > 0, 1.0, 0.0)
+    edge_normed[...] = normalise(x_edge[...])
+    ext[pl.ds(0, 16), pl.ds(0, MW)] = nn(edge_normed[...], wm[1]) * keep
+    ext[pl.ds(0, 16), pl.ds(MW, 256)] = nn(edge_normed[...], ws[...]) * keep
+    conv_forward(ext, taps, bias, pre, post)
+    advance(keys)
+    step_x, enter_x, tail_x = decay_terms(step, cum_ref)
+    tail_in = (post[:, pl.ds(0, MW)].astype(F32) * step_x * tail_x).astype(BF16)
+    local[...] = tn(tail_in, post[:, pl.ds(MW, NS)]).astype(BF16)
+    entering = gather_steps(gather_rows(links, local, states))
+    advance(entering, keys)
+
     qp[...] = stacked_queries(q[...])
-    block = load_block(kv_all, s)
-    scores = causal(nt(block, qp[...]))
+    scores = causal(nt(kv[...], qp[...]))
     high = jnp.max(scores, axis=0, keepdims=True)
     weights = jnp.exp(scores - high)
-    acc[...] = tn(block, weights.astype(BF16))
+    acc[...] = tn(kv[...], weights.astype(BF16))
+    advance(entering)
+    finish(keys)
 
     def hop(j, running):
         high, total = running
@@ -556,12 +580,40 @@
         acc[...] = acc[...] * fade + tn(block, weights.astype(BF16))
         return new, total * fade + jnp.sum(weights, axis=0, keepdims=True)
 
-    high, total = lax.fori_loop(0, s, hop, (high, jnp.sum(weights, axis=0, keepdims=True)))
+    running = (high, jnp.sum(weights, axis=0, keepdims=True))
+    for turn in range(4):
+        running = lax.fori_loop((s * turn) // 4, (s * (turn + 1)) // 4, hop, running)
+        advance(entering)
+    high, total = running
     out = acc[pl.ds(HD, HD)] / total
     out = jnp.concatenate([out[:, :ROWS], out[:, ROWS:]], axis=0).T
     attended_f[...] = out
     attended[...] = out.astype(BF16)
     totals[...] = jnp.broadcast_to(high + jnp.log(total), totals.shape)
+    finish(entering)
+
+    chain(s, states, logs_all, chained, True)
+    state[...] = chained[...].astype(BF16)
+    ssd_forward(post, step_x, enter_x, cum_ref, cumt_ref, skip, gz, state, ssd, mixed, own_squares)
+    slots[links.h] = own_squares[...]
+    copies = [links.send(own_squares, slots.at[links.h], name) for name in ("x1", "x2", "x3")]
+    for c in range(2):
+        lanes = pl.ds(512 * c, 512)
+        proj[:, lanes] = nn(attended[...], wao[:, lanes])
+    for copy in copies:
+        copy.wait()
+    squares[...] = (slots[0] + slots[1]) + (slots[2] + slots[3])
+    scale = lax.rsqrt(column_of(squares[...]) / (MAMBA_HEADS * MP) + EPSILON)
+    gated[...] = (mixed[...] * scale * mgain[...]).astype(BF16)
+    for c in range(2):
+        lanes = pl.ds(512 * c, 512)
+        part[:, lanes] = (proj[:, lanes] + nn(gated[...], wmo[:, lanes])).astype(BF16)
+    jobs = [
+        Reduce(links, path, 128, part, 128 * p, work, recv, summed, 128 * p)
+        for p, path in enumerate(HEAD_PATHS)
+    ]
+    reduce_all(jobs)
+    gather_all(jobs)
 
 
 def attend_back_kernel(idx, q, kv_all, d_att, attended_f, totals, d_q, pairs, qp, dop, acc):
@@ -710,10 +762,10 @@
 
 
 def conv_back_kernel(
-    idx, gathered, logs, d_ssd, d_scaled, d_bc, skip, step, cum, post, pre, raw, edge,
-    d_pre, kernel_grads, total, ext,
+    idx, gathered, logs, d_ssd, d_scaled, d_bc, skip, step, cum, post, pre, ext,
+    d_pre, kernel_grads, total,
 ):
-    chain(idx, gathered, logs, total, False)
+    chain(idx[0], gathered, logs, total, False)
     leaving = total[...].astype(BF16)
     step_x, _, tail_x = decay_terms(step, cum)
     b = post[:, pl.ds(MW, NS)]
@@ -723,16 +775,13 @@
     d_pre[:, pl.ds(0, MW)] = skip[...] * d_ssd[...] + scaled_grad * step_x
     d_pre[:, pl.ds(MW, NS)] = d_bc[:, pl.ds(0, NS)] + nn(tail_in, leaving)
     d_pre[:, pl.ds(MW + NS, NS)] = d_bc[:, pl.ds(NS, NS)]
-    keep = jnp.where(idx[0] > 0, 1.0, 0.0)
-    ext[pl.ds(0, 8)] = edge[...] * keep
-    ext[pl.ds(8, ROWS)] = raw[...]
     for c in range(5):
         lanes = pl.ds(128 * c, 128)
         v = pre[:, lanes]
         sig = sigmoid(v)
         dp = d_pre[:, lanes] * (sig * (1.0 + v * (1.0 - sig)))
         d_pre[:, lanes] = dp
-        rows = [jnp.sum(dp * ext[pl.ds(5 + k, ROWS), lanes], axis=0, keepdims=True) for k in range(KC)]
+        rows = [jnp.sum(dp * ext[pl.ds(13 + k, ROWS), lanes], axis=0, keepdims=True) for k in range(KC)]
         rows.append(jnp.sum(dp, axis=0, keepdims=True))
         rows.append(jnp.zeros((3, 128), F32))
         kernel_grads[:, lanes] = jnp.concatenate(rows, axis=0)
@@ -779,6 +828,51 @@
     weighted = d_normed * gain[...]
     inner = jnp.sum(weighted * x, axis=1, keepdims=True)
     put_wide(wide, r1 * weighted - x * (r1 * r1 * r1 / D * inner))
+
+
+def widths_kernel(
+    down_in, gateup_in, mixout_in, attn_in, head, tail,
+    down, gateup, mixout, attn, mixer, query, keyval, state,
+):
+    down[...] = down_in[...].astype(F32)
+    gateup[0] = gateup_in[:, pl.ds(0, 512)].astype(F32)
+    gateup[1] = gateup_in[:, pl.ds(512, 512)].astype(F32)
+    mixout[...] = mixout_in[...].astype(F32)
+    attn[...] = attn_in[...].astype(F32)
+    mixer[0] = head[:, pl.ds(0, MW)].astype(F32)
+    mixer[1] = tail[:, pl.ds(0, MW)].astype(F32)
+    state[...] = head[:, pl.ds(MW, 256)].astype(F32)
+    query[...] = tail[:, pl.ds(MW, 128)].astype(F32)
+    first, second = tail[:, pl.ds(512, 128)].astype(F32), tail[:, pl.ds(640, 128)].astype(F32)
+    left = lax.broadcasted_iota(jnp.int32, first.shape, 1) < HD
+    keyval[0] = jnp.where(left, first, pltpu.roll(second, HD, 1))
+    keyval[1] = jnp.where(left, pltpu.roll(first, HD, 1), second)
+
+
+def widened(x_out, ms_out):
+    def rows(count, width, offset=0):
+        return pl.BlockSpec((count, width), lambda i: (i + offset, 0))
+
+    def halves(count, width):
+        return pl.BlockSpec((2, count, width), lambda i: (0, i, 0))
+
+    return pl.pallas_call(
+        widths_kernel,
+        grid=(4,),
+        out_shape=(
+            shape((512, D), F32), shape((2, D, 512), F32), shape((MW, D), F32), shape((128, D), F32),
+            shape((2, D, MW), F32), shape((D, 128), F32), shape((2, D, 128), F32), shape((D, 256), F32),
+        ),
+        in_specs=[
+            rows(128, D), rows(256, D, 2), rows(96, D, 16), rows(32, D, 60),
+            rows(256, 768), rows(256, 768, 4),
+        ],
+        out_specs=(
+            rows(128, D), halves(256, 512), rows(96, D), rows(32, D),
+            halves(256, MW), rows(256, 128), halves(256, 128), rows(256, 256),
+        ),
+        compiler_params=pltpu.CompilerParams(vmem_limit_bytes=VMEM_LIMIT),
+    )(x_out, x_out, x_out, x_out, ms_out, ms_out)
 
 
 def on_device(
@@ -803,53 +897,31 @@
     cum_t = cum.T
     logs = jnp.broadcast_to(cum[ROWS - 1][:, None], (8, 128))
 
-    normed, q, kv, gz, raw = call(
-        project_kernel,
+    (
+        normed, q, kv_all, logs_all, gz, ext, pre, post, attended, attended_f, totals, ssd, mixed,
+        squares, state, gated, summed,
+    ) = call(
+        forward_kernel,
         [
-            shape((ROWS, D), BF16), shape((ROWS, 128), BF16), shape((ROWS, 128), BF16),
-            shape((ROWS, MW), F32), shape((ROWS, CW), F32),
+            shape((ROWS, D), BF16), shape((ROWS, 128), BF16), shape((8192, 128), BF16),
+            shape((256, 128), F32), shape((ROWS, MW), F32), shape((ROWS + 16, CW), F32),
+            shape((ROWS, CW), F32), shape((ROWS, CW), BF16), shape((ROWS, 128), BF16),
+            shape((ROWS, 128), F32), shape((8, 512), F32), shape((ROWS, MW), F32),
+            shape((ROWS, MW), F32), shape((8, ROWS), F32), shape((MW, NS), BF16),
+            shape((ROWS, MW), BF16), shape((ROWS, D), BF16),
         ],
-        (hidden_in, gain1, query_weight, wkv, mixer_weight, state_weight),
-    )
-    kv_all, edge, logs_all = call(
-        keyval_kernel,
-        [shape((8192, 128), BF16), shape((8, CW), F32), shape((256, 128), F32)],
-        (kv, raw[ROWS - 8 :], logs),
-        collective=1, copies=26,
-    )
-    pre, post, local_state = call(
-        conv_kernel,
-        [shape((ROWS, CW), F32), shape((ROWS, CW), BF16), shape((MW, NS), BF16)],
-        (idx, raw, edge, taps, bias, step, cum),
-        scratch=[pltpu.VMEM((ROWS + 8, CW), F32)], smem=1,
-    )
-    (states,) = call(
-        state_kernel, [shape((12288, NS), BF16)], (local_state,), collective=2, copies=20
-    )
-    attended, attended_f, totals = call(
-        attend_kernel,
-        [shape((ROWS, 128), BF16), shape((ROWS, 128), F32), shape((8, 512), F32)],
-        (idx, q, kv_all),
-        scratch=[pltpu.VMEM((512, 128), BF16), pltpu.VMEM((128, 512), F32)], smem=1,
-    )
-    ssd, mixed, squares, state = call(
-        ssd_kernel,
-        [shape((ROWS, MW), F32), shape((ROWS, MW), F32), shape((8, ROWS), F32), shape((MW, NS), BF16)],
-        (idx, post, step, cum, cum_t, skip, gz, states, logs_all),
-        scratch=[pltpu.VMEM((MW, NS), F32)], smem=1,
-    )
-    (squares,) = call(
-        sums_kernel, [shape((8, ROWS), F32)], (squares,),
-        scratch=[pltpu.VMEM((HEADS, 8, ROWS), F32)], collective=3, copies=3,
-    )
-    gated, part = call(
-        outputs_kernel,
-        [shape((ROWS, MW), BF16), shape((ROWS, D), BF16)],
-        (mixed, squares, mgain, mixer_output, attended, attention_output),
-    )
-    (summed,) = call(
-        head_sum_kernel, [shape((ROWS, D), BF16)], (part,),
-        scratch=[pltpu.VMEM((ROWS, D), BF16)] * 2, collective=4, copies=8,
+        (
+            hidden_in, gain1, query_weight, wkv, mixer_weight, state_weight, taps, bias, step, cum,
+            cum_t, logs, skip, mgain, mixer_output, attention_output,
+        ),
+        scratch=[
+            pltpu.VMEM((ROWS, 128), BF16), pltpu.VMEM((16, D), BF16), pltpu.VMEM((16, D), BF16),
+            pltpu.VMEM((MW, NS), BF16), pltpu.VMEM((12288, NS), BF16), pltpu.VMEM((MW, NS), F32),
+            pltpu.VMEM((512, 128), BF16), pltpu.VMEM((128, 512), F32), pltpu.VMEM((8, ROWS), F32),
+            pltpu.VMEM((HEADS, 8, ROWS), F32), pltpu.VMEM((ROWS, D), F32),
+            pltpu.VMEM((ROWS, D), BF16), pltpu.VMEM((ROWS, D), BF16), pltpu.VMEM((ROWS, D), BF16),
+        ],
+        collective=1, copies=60,
     )
     wide, back, xf, second_part = call(
         feed_kernel,
@@ -893,8 +965,8 @@
     d_pre, kernel_grads = call(
         conv_back_kernel,
         [shape((ROWS, CW), F32), shape((8, CW), F32)],
-        (idx, grad_states, logs_all, d_ssd, d_scaled, d_bc, skip, step, cum, post, pre, raw, edge),
-        scratch=[pltpu.VMEM((MW, NS), F32), pltpu.VMEM((ROWS + 8, CW), F32)], smem=1,
+        (idx, grad_states, logs_all, d_ssd, d_scaled, d_bc, skip, step, cum, post, pre, ext),
+        scratch=[pltpu.VMEM((MW, NS), F32)], smem=1,
     )
     d_q, pairs = call(
         attend_back_kernel,
@@ -948,7 +1020,6 @@
             pltpu.VMEM((2048, CW), BF16), pltpu.VMEM((2048, CW), BF16),
             pltpu.VMEM((1024, 256), BF16), pltpu.VMEM((1024, 256), BF16),
             pltpu.VMEM((HEADS, 64, 256), BF16),
-            pltpu.VMEM((8, 128), F32), pltpu.VMEM((8, 128), F32),
             pltpu.VMEM((HEADS, 8, D), F32),
             pltpu.VMEM((6, 8, D), F32), pltpu.VMEM((5, 8, D), F32),
         ],
@@ -960,32 +1031,26 @@
 
     block_out = columns(hidden_in) + columns(summed) + out_share.astype(F32)
     input_grads = columns(cotangent) + columns(d_sum) + in_share.astype(F32)
-    x_f = x_out
-    gateup = x_f[512:1536]
-    head, tail = ms_out[:1024], ms_out[1024:]
-    gateup_grads = jnp.stack([gateup[:, :512], gateup[:, 512:]]).astype(F32)
-    mixer_grads = jnp.stack([head[:, :MW], tail[:, :MW]]).astype(F32)
-    keys = jnp.concatenate([tail[:, 512:576], tail[:, 640:704]], axis=1)
-    values = jnp.concatenate([tail[:, 576:640], tail[:, 704:768]], axis=1)
+    down, gateup, mixout, attn, mixer, query, keyval, state_total = widened(x_out, ms_out)
     return (
         block_out,
         input_grads,
         small[0],
-        tail[:, MW:512].astype(F32),
-        jnp.stack([keys, values]).astype(F32),
-        x_f[1920:].astype(F32),
-        mixer_grads,
-        head[:, MW:640].astype(F32),
+        query,
+        keyval,
+        attn,
+        mixer,
+        state_total,
         small[4:8, :MW],
         small[2].reshape(KC, 256),
         small[4, MW : 2 * MW],
         small[3, :256],
         jnp.sum(small[6, MW : 2 * MW].reshape(HMH, MP), axis=1),
         small[5, MW : 2 * MW],
-        x_f[1536:1920].astype(F32),
+        mixout,
         small[1],
-        gateup_grads,
-        x_f[:512].astype(F32),
+        gateup,
+        down,
     )
 
 

time: 332 us -> 278 us (0.84)
  Pallas kernels: 293 us -> 260 us
  other arithmetic: 18.8 us -> 4.81 us
  local copies, waits for them, and re-layouts: 17.8 us -> 12 us
    pallas_call x20 -> x12, Pallas kernels: 293 us -> 253 us  [call(): pl.pallas_call(body, out_shape=tuple(outs), in_specs=in_specs, out_specs=...]
    convert_element_type x8 -> x0, other arithmetic: 13.7 us -> none  [the longest x1 2.29 us: on_device(): gateup_grads = jnp.stack([gateup[:, :512], gateup[:, 512:]]).astype(F32)]
    pallas_call x0 -> x1, Pallas kernels: none -> 7.06 us  [widened(): pl.pallas_call(widths_kernel, grid=(4,), out_shape=(shape((512, D), F32),...]
    unnamed x57 -> x41, local copies, waits for them, and re-layouts: 8.13 us -> 5.5 us
where the time goes in v1:
time: 278 us
  Pallas kernels  260 us (94%)
  local copies, waits for them, and re-layouts  12 us (4%)
  other arithmetic  4.81 us (2%)
    pallas_call x12, Pallas kernels, call(): pl.pallas_call(body, out_shape=tuple(outs), in_specs=in_specs, out_specs=...  253 us
    pallas_call x1, Pallas kernels, widened(): pl.pallas_call(widths_kernel, grid=(4,), out_shape=(shape((512, D), F32),...  7.06 us

profile of v1, /device:TPU:1, one launch (start us, length us, event | category | flops | bytes accessed | tf_op | source)
XLA Modules:
  0.0 277.6 jit_solution(9622224343338042133)
XLA Ops:
  0.8 0.7 reshape.63.mgain
  1.5 0.7 pad_maximum_fusion.4
  2.2 0.7 broadcast_in_dim.15
  3.0 0.7 select_maximum_fusion.taps
  3.7 0.8 copy.42
  4.7 0.6 reduce-window.6
  5.2 0.2 slice_reduce_fusion
  5.8 1.2 dynamic-slice_bitcast_fusion.1
  7.1 0.1 pad_maximum_fusion.wkv
  7.3 66.8 %shard_map.322 = (bf16[256,1024]{1,0:T(8,128)(2,1)S(1)}, bf16[256,128]{1,0:T(8,128)(2,1)S(1)}, bf16[8192,128]{1,0:T(8,128)(2,1)}, f32[256,128]{1,0:T(8,128)S(1)}...) custom-call(bf16[256,1024]{1,0:T(8,128)(2,1)} %x_ref.5, ...), custom_call_target="tpu_custom_call" | custom-call | tf_op jit(solution)/shard_map/pallas_call | solution.py:266
  74.2 1.0 copy-done.10
  75.2 8.1 %shard_map.323 = (bf16[1024,256]{1,0:T(8,128)(2,1)S(1)}, bf16[256,1024]{1,0:T(8,128)(2,1)S(1)}, bf16[1536,1024]{1,0:T(8,128)(2,1)}, f32[8,1024]{1,0:T(8,128)S(1)}) custom-call(bf16[256,1024]{1,0:T(8,128)(2,1)S(1)} %copy-done.2, bf16[256,1024]{1,0:T(8,128)(2,1)S(1)} %copy-done.10, bf16[256,1024]{1,0:T(8,128)(2,1)S(1)} %copy-done.4, f32[1,1024]{1,0:T(1,128)S(1)} %bitcast.36, ...), custom_call_target="tpu_custom_call" | custom-call | tf_op jit(solution)/shard_map/pallas_call | solution.py:266
  83.3 16.5 %shard_map.324 = (bf16[256,1024]{1,0:T(8,128)(2,1)S(1)}, bf16[256,256]{1,0:T(8,128)(2,1)S(1)}) custom-call(bf16[256,1024]{1,0:T(8,128)(2,1)S(1)} %get-tuple-element.74.part, bf16[1024,256]{1,0:T(8,128)(2,1)S(1)} %get-tuple-element.75.wide), custom_call_target="tpu_custom_call" | custom-call | tf_op jit(solution)/shard_map/pallas_call | solution.py:266
  99.8 2.3 shard_map.325
  102.1 3.0 %shard_map.330 = (bf16[256,128]{1,0:T(8,128)(2,1)S(1)}, bf16[8192,128]{1,0:T(8,128)(2,1)S(1)}) custom-call(s32[2]{0:T(128)S(1)} %pad_add_fusion.idx, bf16[256,128]{1,0:T(8,128)(2,1)S(1)} %get-tuple-element.98.q, bf16[8192,128]{1,0:T(8,128)(2,1)} %get-tuple-element.99.kv_all, bf16[256,128]{1,0:T(8,128)(2,1)S(1)} %get-tuple-element.100.d_att, ...), custom_call_target="tpu_custom_call" | custom-call | tf_op jit(solution)/shard_map/pallas_call | solution.py:266
  105.1 4.2 %shard_map.326.inner = f32[8,256]{1,0:T(8,128)S(1)} custom-call(f32[8,256]{1,0:T(8,128)S(1)} %get-tuple-element.85.part), custom_call_target="tpu_custom_call" | custom-call | tf_op jit(solution)/shard_map/pallas_call | solution.py:266
  109.4 2.1 shard_map.327
  111.5 47.1 %shard_map.328.gathered = bf16[12288,128]{1,0:T(8,128)(2,1)S(1)} custom-call(bf16[384,128]{1,0:T(8,128)(2,1)S(1)} %get-tuple-element.90.state), custom_call_target="tpu_custom_call" | custom-call | tf_op jit(solution)/shard_map/pallas_call | solution.py:266
  158.6 1.7 copy-done
  160.3 5.4 %shard_map.329 = (f32[256,640]{1,0:T(8,128)S(1)}, f32[8,640]{1,0:T(8,128)S(1)}) custom-call(s32[2]{0:T(128)S(1)} %pad_add_fusion.idx, bf16[12288,128]{1,0:T(8,128)(2,1)} %copy-done, f32[256,128]{1,0:T(8,128)S(1)} %get-tuple-element.91.logs, f32[256,384]{1,0:T(8,128)S(1)} %get-tuple-element.92.d_ssd, f32[256,384]{1,0:T(8,128)S(1)} %get-tuple-element.93.d_scaled, ...), custom_call_target="tpu_custom_call" | custom-call | tf_op jit(solution)/shard_map/pallas_call | solution.py:266
  165.9 18.4 %shard_map.331 = (bf16[256,128]{1,0:T(8,128)(2,1)S(1)}, f32[8,640]{1,0:T(8,128)S(1)}) custom-call(bf16[8192,128]{1,0:T(8,128)(2,1)S(1)} %get-tuple-element.103.pairs, f32[8,640]{1,0:T(8,128)S(1)} %slice.83.edge), custom_call_target="tpu_custom_call" | custom-call | tf_op jit(solution)/shard_map/pallas_call | solution.py:266
  184.3 6.1 %shard_map.332 = (bf16[2048,640]{1,0:T(8,128)(2,1)}, bf16[1024,256]{1,0:T(8,128)(2,1)S(1)}, f32[8,1024]{1,0:T(8,128)S(1)}) custom-call(s32[2]{0:T(128)S(1)} %pad_add_fusion.idx, f32[256,640]{1,0:T(8,128)S(1)} %get-tuple-element.97.d_pre, f32[8,640]{1,0:T(8,128)S(1)} %get-tuple-element.104.edge, f32[8,640]{1,0:T(8,128)S(1)} %copy-done.14, ...), custom_call_target="tpu_custom_call" | custom-call | tf_op jit(solution)/shard_map/pallas_call | solution.py:266
  190.5 72.6 %shard_map.333 = (bf16[2048,1024]{1,0:T(8,128)(2,1)}, bf16[2048,768]{1,0:T(8,128)(2,1)}, bf16[256,256]{1,0:T(8,128)(2,1)S(1)}, f32[8,1024]{1,0:T(8,128)S(1)}) custom-call(bf16[1536,1024]{1,0:T(8,128)(2,1)} %get-tuple-element.78.xf, bf16[512,1024]{1,0:T(8,128)(2,1)S(1)} %copy-done.6, bf16[2048,640]{1,0:T(8,128)(2,1)} %get-tuple-element.109.ms, ...), custom_call_target="tpu_custom_call" | custom-call | tf_op jit(solution)/shard_map/pallas_call | solution.py:266
  263.0 1.8 convert_add_fusion
  264.9 0.6 slice.100
  265.4 0.6 slice.97
  266.0 0.6 slice_reduce_fusion.2
  266.6 0.6 fusion.1
  267.3 0.6 reduce_sum.9
  267.9 0.6 reshape_squeeze.6
  268.5 1.9 copy-done.1
  270.4 7.1 %shard_map.334 = (f32[512,1024]{1,0:T(8,128)}, f32[2,1024,512]{2,1,0:T(8,128)}, f32[384,1024]{1,0:T(8,128)}, f32[128,1024]{1,0:T(8,128)}, f32[2,1024,384]{2,1,0:...) custom-call(bf16[2048,1024]{1,0:T(8,128)(2,1)} %get-tuple-element.118.down_in.gateup_in.mixout_in.attn_i, ...), custom_call_target="tpu_custom_call" | custom-call | tf_op jit(solution)/shard_map/pallas_call | solution.py:859
  (64 shorter events, 1.0 us)
Async XLA Ops:
  0.7 6.6 %copy-start.9 = (bf16[128,1024]{1,0:T(8,128)(2,1)S(1)}, bf16[128,1024]{1,0:T(8,128)(2,1)}, u32[]{:S(2)}) copy-start(bf16[128,1024]{1,0:T(8,128)(2,1)} %wao.3) | copy-start | bytes 786436
  0.7 6.6 %copy-start.8 = (bf16[1024,128]{1,0:T(8,128)(2,1)S(1)}, bf16[1024,128]{1,0:T(8,128)(2,1)}, u32[]{:S(2)}) copy-start(bf16[1024,128]{1,0:T(8,128)(2,1)} %wq.3) | copy-start | bytes 786436
  0.7 6.6 %copy-start.17 = (f32[1024]{0:T(1024)S(1)}, f32[1024]{0:T(1024)}, u32[]{:S(2)}) copy-start(f32[1024]{0:T(1024)} %param.22) | copy-start | bytes 12292
  3.7 70.4 %copy-start.13 = (f32[8,640]{1,0:T(8,128)}, f32[8,640]{1,0:T(8,128)S(1)}, u32[]{:S(2)}) copy-start(f32[8,640]{1,0:T(8,128)S(1)} %select_maximum_fusion.taps) | copy-start | bytes 61444
  7.1 67.1 %copy-start.2 = (bf16[256,1024]{1,0:T(8,128)(2,1)S(1)}, bf16[256,1024]{1,0:T(8,128)(2,1)}, u32[]{:S(2)}) copy-start(bf16[256,1024]{1,0:T(8,128)(2,1)} %x_ref.5) | copy-start | bytes 1572868
  7.1 67.1 %copy-start.4 = (bf16[256,1024]{1,0:T(8,128)(2,1)S(1)}, bf16[256,1024]{1,0:T(8,128)(2,1)}, u32[]{:S(2)}) copy-start(bf16[256,1024]{1,0:T(8,128)(2,1)} %cot.1) | copy-start | bytes 1572868
  7.1 67.1 %copy-start.7 = (bf16[512,1024]{1,0:T(8,128)(2,1)S(1)}, bf16[512,1024]{1,0:T(8,128)(2,1)}, u32[]{:S(2)}) copy-start(bf16[512,1024]{1,0:T(8,128)(2,1)} %dw.1) | copy-start | bytes 3145732
  7.1 67.1 %copy-start.18 = (f32[1024]{0:T(1024)S(1)}, f32[1024]{0:T(1024)}, u32[]{:S(2)}) copy-start(f32[1024]{0:T(1024)} %param.35) | copy-start | bytes 12292
  74.2 1.0 copy-start.10
  75.2 24.6 %copy-start.3 = (bf16[384,1024]{1,0:T(8,128)(2,1)S(1)}, bf16[384,1024]{1,0:T(8,128)(2,1)}, u32[]{:S(2)}) copy-start(bf16[384,1024]{1,0:T(8,128)(2,1)} %wmo.3) | copy-start | bytes 2359300
  99.8 5.3 %copy-start.15 = (bf16[256,256]{1,0:T(8,128)(2,1)}, bf16[256,256]{1,0:T(8,128)(2,1)S(1)}, u32[]{:S(2)}) copy-start(bf16[256,256]{1,0:T(8,128)(2,1)S(1)} %get-tuple-element.76) | copy-start | bytes 393220
  109.4 50.9 %copy-start.11 = (f32[272,640]{1,0:T(8,128)S(1)}, f32[272,640]{1,0:T(8,128)}, u32[]{:S(2)}) copy-start(f32[272,640]{1,0:T(8,128)} %get-tuple-element.96.ext) | copy-start | bytes 2088964
  109.4 50.9 %copy-start.12 = (f32[256,640]{1,0:T(8,128)S(1)}, f32[256,640]{1,0:T(8,128)}, u32[]{:S(2)}) copy-start(f32[256,640]{1,0:T(8,128)} %get-tuple-element.95.pre) | copy-start | bytes 1966084
  158.6 1.7 copy-start
  160.3 24.0 %copy-start.14 = (f32[8,640]{1,0:T(8,128)S(1)}, f32[8,640]{1,0:T(8,128)}, u32[]{:S(2)}) copy-start(f32[8,640]{1,0:T(8,128)} %copy-done.13) | copy-start | bytes 61444
  165.7 18.6 %copy-start.5 = (bf16[1024,256]{1,0:T(8,128)(2,1)S(1)}, bf16[1024,256]{1,0:T(8,128)(2,1)}, u32[]{:S(2)}) copy-start(bf16[1024,256]{1,0:T(8,128)(2,1)} %ws.3) | copy-start | bytes 1572868
  184.3 6.2 %copy-start.6 = (bf16[512,1024]{1,0:T(8,128)(2,1)S(1)}, bf16[512,1024]{1,0:T(8,128)(2,1)}, u32[]{:S(2)}) copy-start(bf16[512,1024]{1,0:T(8,128)(2,1)} %get-tuple-element.83.xb) | copy-start | bytes 3145732
  190.4 72.6 %copy-start.16 = (bf16[256,256]{1,0:T(8,128)(2,1)S(1)}, bf16[256,256]{1,0:T(8,128)(2,1)}, u32[]{:S(2)}) copy-start(bf16[256,256]{1,0:T(8,128)(2,1)} %copy-done.15) | copy-start | bytes 393220
  268.5 1.9 copy-start.1

commit v2 on v1

v2 whole, which is shorter than its diff:
```python
import functools

import jax
import jax.numpy as jnp
from jax import lax
from jax.experimental import pallas as pl
from jax.experimental.pallas import tpu as pltpu
from jax.sharding import PartitionSpec as P

D = 1024
FF = 2048
AH = 8
KVH = 2
HD = 64
MAMBA_HEADS = 24
MP = 64
NS = 128
KC = 4
EPSILON = 1e-05
SEQ = 32
HEADS = 4
ROWS = 256
MW = 384
CW = 640
HMH = 6
HIGHEST = lax.Precision.HIGHEST
MESH = pl.DeviceIdType.MESH
F32 = jnp.float32
BF16 = jnp.bfloat16
VMEM_LIMIT = 50 * 1024 * 1024


def nn(a, b):
    return jnp.dot(a, b, preferred_element_type=F32)


def nt(a, b):
    return lax.dot_general(a, b, (((1,), (1,)), ((), ())), preferred_element_type=F32)


def tn(a, b):
    return lax.dot_general(a, b, (((0,), (0,)), ((), ())), preferred_element_type=F32)


def exact(a, b, dims):
    return lax.dot_general(
        a, b, (dims, ((), ())), precision=HIGHEST, preferred_element_type=F32
    )


def sigmoid(v):
    return 1.0 / (1.0 + jnp.exp(-v))


def shape(dims, kind):
    return jax.ShapeDtypeStruct(dims, kind)


def seq_bits(s):
    core, y, z = s % 2, (s // 2) % 4, s // 8
    return {
        "c": core,
        "ya": (y + y // 2) % 2,
        "yb": y // 2,
        "za": (z + z // 2) % 2,
        "zb": z // 2,
        "y4": y,
        "z4": z,
    }


SEQ_PATHS = (
    ("c", "ya", "yb", "z4"),
    ("c", "yb", "ya", "z4"),
    ("c", "za", "zb", "y4"),
    ("c", "zb", "za", "y4"),
)
HEAD_PATHS = (("xa", "xb"), ("xb", "xa"))


def ways(name):
    return 4 if name in ("y4", "z4") else 2


def position(bits, path):
    at = 0
    for name in path:
        at = at * ways(name) + bits[name]
    return at


def sizes(rows, path):
    left = []
    for name in path:
        rows = rows // ways(name)
        left.append(rows)
    return left


def block_position(s, p):
    return position(seq_bits(s), SEQ_PATHS[p])


def head_position(h, p):
    bits = {"xa": (h + h // 2) % 2, "xb": h // 2}
    return position(bits, HEAD_PATHS[p])


class Links:
    def __init__(self, send_sem, recv_sem):
        s, h = lax.axis_index("seq"), lax.axis_index("head")
        self.s, self.h = s, h
        core, y, z = s % 2, (s // 2) % 4, s // 8
        self.bits = seq_bits(s)
        self.bits["xa"] = (h + h // 2) % 2
        self.bits["xb"] = h // 2
        self.partner = {
            "c": (s + 1 - 2 * core, h),
            "ya": (s + 2 * (1 - 2 * (y % 2)), h),
            "yb": (s + 2 * (3 - 2 * y), h),
            "za": (s + 8 * (1 - 2 * (z % 2)), h),
            "zb": (s + 8 * (3 - 2 * z), h),
            "xa": (s, h + 1 - 2 * (h % 2)),
            "xb": (s, 3 - h),
            "y41": (s - 2 * y + 2 * ((y + 1) % 4), h),
            "y42": (s - 2 * y + 2 * ((y + 2) % 4), h),
            "y43": (s - 2 * y + 2 * ((y + 3) % 4), h),
            "z41": ((s + 8) % SEQ, h),
            "z42": ((s + 16) % SEQ, h),
            "z43": ((s + 24) % SEQ, h),
            "x1": (s, (h + 1) % HEADS),
            "x2": (s, (h + 2) % HEADS),
            "x3": (s, (h + 3) % HEADS),
            "next": ((s + 1) % SEQ, h),
            "prev": ((s + SEQ - 1) % SEQ, h),
        }
        self.send_sem, self.recv_sem, self.used = send_sem, recv_sem, 0

    def greet(self, names):
        semaphore = pltpu.get_barrier_semaphore()
        for name in names:
            pl.semaphore_signal(
                semaphore, inc=1, device_id=self.partner[name], device_id_type=MESH
            )

    def met(self, names):
        pl.semaphore_wait(pltpu.get_barrier_semaphore(), len(names))

    def barrier(self, names):
        self.greet(names)
        self.met(names)

    def send(self, src, dst, name):
        k = self.used
        self.used += 1
        assert k < self.send_sem.shape[0]
        copy = pltpu.make_async_remote_copy(
            src_ref=src,
            dst_ref=dst,
            send_sem=self.send_sem.at[k],
            recv_sem=self.recv_sem.at[k],
            device_id=self.partner[name],
            device_id_type=MESH,
        )
        copy.start()
        return copy


DONE = object()
SEQ_NAMES = ("c", "y41", "y42", "y43", "z41", "z42", "z43")
DOUBLING = ("c", "ya", "yb", "za", "zb")


def rows_at(start, count, unit=16):
    return pl.ds(pl.multiple_of(start, unit), count)


class Reduce:
    def __init__(self, links, path, rows, src, src_base, work, recv, out, base):
        self.links, self.path, self.rows = links, path, rows
        self.src, self.src_base = src, src_base
        self.work, self.recv, self.out, self.base = work, recv, out, base
        self.left = sizes(rows, path)
        self.start = 0
        self.copies = []

    def source(self, step):
        return (self.src, self.src_base) if step == 0 else (self.work, self.base)

    def landing(self, step):
        return self.base + self.rows - (self.rows if step == 0 else self.left[step - 1])

    def begin(self, step):
        name, size = self.path[step], self.left[step]
        ref, at = self.source(step)
        landing = self.landing(step)
        self.copies = []
        for k in range(1, ways(name)):
            away = (self.links.bits[name] + k) % ways(name)
            to = name if ways(name) == 2 else name + str(k)
            self.copies.append(
                self.links.send(
                    ref.at[rows_at(at + self.start + away * size, size)],
                    self.recv.at[pl.ds(landing + (k - 1) * size, size)],
                    to,
                )
            )

    def finish(self, step):
        name, size = self.path[step], self.left[step]
        keep = self.start + self.links.bits[name] * size
        ref, at = self.source(step)
        landing = self.landing(step)
        last = step == len(self.path) - 1
        target = self.out if last and self.out is not None else self.work
        for copy in self.copies:
            copy.wait()
        chunk = 32 if size % 32 == 0 else 16

        def add(i, carry):
            total = ref[rows_at(at + keep + i * chunk, chunk)].astype(F32)
            for k in range(ways(name) - 1):
                total += self.recv[rows_at(landing + k * size + i * chunk, chunk)].astype(F32)
            target[rows_at(self.base + keep + i * chunk, chunk)] = total.astype(BF16)
            return carry

        lax.fori_loop(0, size // chunk, add, 0)
        self.start = keep

    def send_back(self, step, columns=None):
        name, size = self.path[step], self.left[step]
        at = rows_at(self.base + self.start, size, min(size, 16))
        ref = self.out.at[at] if columns is None else self.out.at[at, pl.ds(0, columns)]
        self.copies = [
            self.links.send(ref, ref, name if ways(name) == 2 else name + str(k))
            for k in range(1, ways(name))
        ]

    def wait_back(self, step):
        name, size = self.path[step], self.left[step]
        for copy in self.copies:
            copy.wait()
        self.start = self.start - self.links.bits[name] * size


def reduce_steps(jobs):
    for job in jobs:
        job.begin(0)
    for step in range(max(len(job.path) for job in jobs)):
        yield
        for job in jobs:
            if step < len(job.path):
                job.finish(step)
                if step + 1 < len(job.path):
                    job.begin(step + 1)


def gather_steps(jobs, columns=None):
    columns = columns or [None] * len(jobs)
    for job, width in zip(jobs, columns):
        job.send_back(len(job.path) - 1, width)
    for step in range(max(len(job.path) for job in jobs) - 1, -1, -1):
        yield
        for job, width in zip(jobs, columns):
            if step < len(job.path):
                job.wait_back(step)
                if step:
                    job.send_back(step - 1, width)


def finish(*runs):
    runs = list(runs)
    while runs:
        for run in list(runs):
            if next(run, DONE) is DONE:
                runs.remove(run)


def advance(*runs):
    for run in runs:
        next(run, DONE)


def reduce_all(jobs):
    finish(reduce_steps(jobs))


def gather_all(jobs, columns=None):
    finish(gather_steps(jobs, columns))


def call(body, outs, args, scratch=(), collective=None, smem=0, copies=0, cost=None):
    vm = pl.BlockSpec(memory_space=pltpu.VMEM)
    scratch = list(scratch)
    if copies:
        scratch += [pltpu.SemaphoreType.DMA((copies,)), pltpu.SemaphoreType.DMA((copies,))]
    if collective is None:
        params = pltpu.CompilerParams(vmem_limit_bytes=VMEM_LIMIT)
    else:
        params = pltpu.CompilerParams(
            vmem_limit_bytes=VMEM_LIMIT, collective_id=collective, has_side_effects=True
        )
    in_specs = [pl.BlockSpec(memory_space=pltpu.SMEM)] * smem + [vm] * (len(args) - smem)
    return pl.pallas_call(
        body,
        out_shape=tuple(outs),
        in_specs=in_specs,
        out_specs=tuple(vm for _ in outs),
        scratch_shapes=scratch,
        compiler_params=params,
    )(*args)


class Gather:
    def __init__(self, links, path, piece, out, base):
        self.links, self.path, self.out, self.base = links, path, out, base
        self.start = position(links.bits, path) * piece
        self.left = sizes(piece * SEQ, path)
        self.copies = []

    send_back = Reduce.send_back
    wait_back = Reduce.wait_back


def gather_rows(links, src, out, paths=SEQ_PATHS):
    piece = src.shape[0] // len(paths)
    jobs = []
    for p, path in enumerate(paths):
        job = Gather(links, path, piece, out, p * piece * SEQ)
        own = rows_at(job.base + job.start, piece, 8 if piece == 8 else 16)
        out[own] = src[pl.ds(p * piece, piece)]
        jobs.append(job)
    return jobs


def own_rows(job, count):
    return job.work[rows_at(job.base + job.start, count)]


def head_spread():
    lane = lax.broadcasted_iota(jnp.int32, (HMH, MW), 1)
    row = lax.broadcasted_iota(jnp.int32, (HMH, MW), 0)
    return jnp.where((lane >= row * MP) & (lane < row * MP + MP), 1.0, 0.0)


def widen(values):
    return exact(values, head_spread(), ((1,), (0,)))


def decay_terms(decay_ref, cum_ref):
    cum_x = widen(cum_ref[...])
    step_x = -widen(decay_ref[...])
    enter_x = jnp.exp(cum_x)
    tail_x = jnp.exp(cum_x[ROWS - 1 : ROWS, :] - cum_x)
    return step_x, enter_x, tail_x


def of_channels(mixer, state, c):
    return (mixer, pl.ds(128 * c, 128)) if c < 3 else (state, pl.ds(128 * (c - 3), 128))


def conv_forward(ext, taps_m, taps_s, bias_m, bias_s, pre, post):
    for c in range(5):
        lanes = pl.ds(128 * c, 128)
        taps, own = of_channels(taps_m, taps_s, c)
        bias, own = of_channels(bias_m, bias_s, c)
        total = bias[:, own] + taps[pl.ds(0, 1), own] * ext[pl.ds(13, ROWS), lanes]
        for k in range(1, KC):
            total = total + taps[pl.ds(k, 1), own] * ext[pl.ds(13 + k, ROWS), lanes]
        pre[:, lanes] = total
        post[:, lanes] = (total * sigmoid(total)).astype(BF16)


def chain(s, gathered, logs, total, forward):
    total[...] = jnp.zeros_like(total)

    def hop(i, run):
        j = s - 1 - i if forward else s + 1 + i
        weight = jnp.exp(run)
        for seg in range(12):
            p, off = seg // 3, (seg % 3) * 32
            at = rows_at(p * 3072 + block_position(j, p) * 96 + off, 32)
            h = seg // 2
            total[pl.ds(32 * seg, 32)] += weight[h : h + 1, :] * gathered[at].astype(F32)
        return run + logs[rows_at(block_position(j, 0) * 8, 8, 8)]

    lax.fori_loop(0, s if forward else SEQ - 1 - s, hop, jnp.zeros((8, 128), F32))


def lower_mask():
    t = lax.broadcasted_iota(jnp.int32, (ROWS, ROWS), 0)
    u = lax.broadcasted_iota(jnp.int32, (ROWS, ROWS), 1)
    return u <= t


def decay_of(cum, cum_t, h, mask):
    diff = cum[:, h : h + 1] - cum_t[h : h + 1, :]
    return jnp.exp(jnp.where(mask, diff, -1e30))


def row_sums(values):
    return exact(jnp.ones((8, values.shape[1]), F32), values, ((1,), (1,)))


def column_of(rows):
    return exact(rows, jnp.full((8, 128), 0.125, F32), ((0,), (0,)))[:, 0:1]


def ssd_forward(post, step_x, enter_x, cum_ref, cumt_ref, skip, gz, state, ssd, mixed, squares):
    mixer_in = post[:, pl.ds(0, MW)].astype(F32)
    scaled = (mixer_in * step_x).astype(BF16)
    b, c = post[:, pl.ds(MW, NS)], post[:, pl.ds(MW + NS, NS)]
    gram = nt(c, b)
    mask = lower_mask()
    cum, cum_t = cum_ref[...], cumt_ref[...]
    left = lax.broadcasted_iota(jnp.int32, (ROWS, 128), 1) < MP
    carried = enter_x * nt(c, state[...]) + widen(skip[...]) * mixer_in
    for pair in range(3):
        lanes = slice(128 * pair, 128 * pair + 128)
        first = nn((gram * decay_of(cum, cum_t, 2 * pair, mask)).astype(BF16), scaled[:, lanes])
        second = nn((gram * decay_of(cum, cum_t, 2 * pair + 1, mask)).astype(BF16), scaled[:, lanes])
        ssd[:, pl.ds(128 * pair, 128)] = jnp.where(left, first, second) + carried[:, lanes]
    z = gz[...]
    m = ssd[...] * (z * sigmoid(z))
    mixed[...] = m
    squares[...] = row_sums(m * m)


def load_block(kv_all, j):
    return jnp.concatenate(
        [kv_all[rows_at(2048 * p + block_position(j, p) * 64, 64)] for p in range(4)], axis=0
    )


def causal(block):
    key = lax.broadcasted_iota(jnp.int32, block.shape, 0)
    query = lax.broadcasted_iota(jnp.int32, block.shape, 1)
    query = jnp.where(query >= ROWS, query - ROWS, query)
    return jnp.where(key <= query, block, -1e30)


def stacked_queries(q):
    q = q.astype(F32) * (HD ** -0.5)
    left = lax.broadcasted_iota(jnp.int32, (ROWS, 128), 1) < HD
    first = jnp.where(left, q, 0.0)
    second = jnp.where(left, pltpu.roll(q, HD, 1), 0.0)
    return jnp.concatenate([first, second], axis=0).astype(BF16)


FORWARD_NAMES = SEQ_NAMES + ("next", "prev", "x1", "x2", "x3")


def forward_kernel(
    x_ref, gain, wq, kvw, wm, ws, taps_m, taps_s, bias_m, bias_s, decay, skip, mgain, wmo, wao,
    cum_ref, cumt_ref, normed, q, kv_all, logs_all, gz, ext, pre, post, attended, attended_f, totals, ssd, mixed,
    squares, state, gated, summed,
    kv, logs, x_edge, edge_normed, local, states, chained, qp, acc, own_squares, slots, proj, part, work,
    recv, send_sem, recv_sem,
):
    links = Links(send_sem, recv_sem)
    s = links.s
    links.greet(FORWARD_NAMES)

    def normalise(rows):
        x = rows.astype(F32)
        r1 = lax.rsqrt(jnp.mean(x * x, axis=1, keepdims=True) + EPSILON)
        return (x * r1 * gain[...]).astype(BF16)

    n = normalise(x_ref[...])
    normed[...] = n
    left = lax.broadcasted_iota(jnp.int32, (ROWS, 128), 1) < HD
    key_cols, value_cols = nn(n, kvw[0]), nn(n, kvw[1])
    key_cols = jnp.where(links.h < 2, key_cols, pltpu.roll(key_cols, HD, 1))
    value_cols = jnp.where(links.h < 2, pltpu.roll(value_cols, HD, 1), value_cols)
    kv[...] = jnp.where(left, key_cols, value_cols).astype(BF16)
    q[...] = nn(n, wq[...]).astype(BF16)
    sums = exact(decay[...], jnp.ones((ROWS, 128), F32), ((0,), (0,)))
    logs[...] = jnp.concatenate([sums, jnp.zeros((8 - HMH, 128), F32)], axis=0)
    key_jobs = gather_rows(links, kv, kv_all) + gather_rows(links, logs, logs_all, SEQ_PATHS[:1])
    links.met(FORWARD_NAMES)
    edge_copy = links.send(x_ref.at[pl.ds(ROWS - 16, 16)], x_edge, "next")
    keys = gather_steps(key_jobs)
    advance(keys)
    gz[...] = nn(normed[...], wm[0])
    lower = jnp.where(lower_mask(), 1.0, 0.0)
    cum_ref[...] = exact(lower, decay[...], ((1,), (0,)))
    cumt_ref[...] = exact(decay[...], lower, ((0,), (1,)))
    advance(keys)
    ext[pl.ds(16, ROWS), pl.ds(0, MW)] = nn(normed[...], wm[1])
    ext[pl.ds(16, ROWS), pl.ds(MW, 256)] = nn(normed[...], ws[...])
    edge_copy.wait()
    advance(keys)
    keep = jnp.where(s > 0, 1.0, 0.0)
    edge_normed[...] = normalise(x_edge[...])
    ext[pl.ds(0, 16), pl.ds(0, MW)] = nn(edge_normed[...], wm[1]) * keep
    ext[pl.ds(0, 16), pl.ds(MW, 256)] = nn(edge_normed[...], ws[...]) * keep
    conv_forward(ext, taps_m, taps_s, bias_m, bias_s, pre, post)
    advance(keys)
    step_x, enter_x, tail_x = decay_terms(decay, cum_ref)
    tail_in = (post[:, pl.ds(0, MW)].astype(F32) * step_x * tail_x).astype(BF16)
    local[...] = tn(tail_in, post[:, pl.ds(MW, NS)]).astype(BF16)
    entering = gather_steps(gather_rows(links, local, states))
    advance(entering, keys)

    qp[...] = stacked_queries(q[...])
    scores = causal(nt(kv[...], qp[...]))
    high = jnp.max(scores, axis=0, keepdims=True)
    weights = jnp.exp(scores - high)
    acc[...] = tn(kv[...], weights.astype(BF16))
    advance(entering)
    finish(keys)

    def merge(blocks, running):
        high, total = running
        scores = [nt(block, qp[...]) for block in blocks]
        new = high
        for block in scores:
            new = jnp.maximum(new, jnp.max(block, axis=0, keepdims=True))
        fade = jnp.exp(high - new)
        weights = [jnp.exp(block - new) for block in scores]
        total = total * fade
        gained = acc[...] * fade
        for block, weight in zip(blocks, weights):
            total = total + jnp.sum(weight, axis=0, keepdims=True)
            gained = gained + tn(block, weight.astype(BF16))
        acc[...] = gained
        return new, total

    def hop(i, running):
        return merge([load_block(kv_all, 2 * i), load_block(kv_all, 2 * i + 1)], running)

    def last_hop(i, running):
        return merge([load_block(kv_all, s - 1)], running)

    running = (high, jnp.sum(weights, axis=0, keepdims=True))
    hops = s // 2
    for turn in range(4):
        running = lax.fori_loop((hops * turn) // 4, (hops * (turn + 1)) // 4, hop, running)
        advance(entering)
    running = lax.fori_loop(0, s % 2, last_hop, running)
    high, total = running
    out = acc[pl.ds(HD, HD)] / total
    out = jnp.concatenate([out[:, :ROWS], out[:, ROWS:]], axis=0).T
    attended_f[...] = out
    attended[...] = out.astype(BF16)
    totals[...] = jnp.broadcast_to(high + jnp.log(total), totals.shape)
    finish(entering)

    chain(s, states, logs_all, chained, True)
    state[...] = chained[...].astype(BF16)
    ssd_forward(post, step_x, enter_x, cum_ref, cumt_ref, skip, gz, state, ssd, mixed, own_squares)
    slots[links.h] = own_squares[...]
    copies = [links.send(own_squares, slots.at[links.h], name) for name in ("x1", "x2", "x3")]
    for c in range(2):
        lanes = pl.ds(512 * c, 512)
        proj[:, lanes] = nn(attended[...], wao[:, lanes])
    for copy in copies:
        copy.wait()
    squares[...] = (slots[0] + slots[1]) + (slots[2] + slots[3])
    scale = lax.rsqrt(column_of(squares[...]) / (MAMBA_HEADS * MP) + EPSILON)
    gated[...] = (mixed[...] * scale * mgain[...]).astype(BF16)
    for c in range(2):
        lanes = pl.ds(512 * c, 512)
        part[:, lanes] = (proj[:, lanes] + nn(gated[...], wmo[:, lanes])).astype(BF16)
    jobs = [
        Reduce(links, path, 128, part, 128 * p, work, recv, summed, 128 * p)
        for p, path in enumerate(HEAD_PATHS)
    ]
    reduce_all(jobs)
    gather_all(jobs)


def put_wide(wide, values):
    for j in range(HEADS):
        for p in range(2):
            at = 512 * p + int(head_position(j, p)) * 128
            wide[pl.ds(at, 128)] = values[128 * p : 128 * p + 128, 256 * j : 256 * j + 256].astype(BF16)


MIDDLE_NAMES = SEQ_NAMES + ("x1", "x2", "x3")


def middle_kernel(
    x_ref, summed, cot_ref, gain, gu, dw, gated, attended, wmo, wao, mixed, squares, mgain, gz, ssd,
    post, decay, cum_ref, cumt_ref, state, q, kv_all, attended_f, totals, logs_all,
    d_sum, share, x_out, xb_piece, second_part, mixgain, d_z, d_ssd, skip_part, d_scaled, d_bc, leaving, d_q, pairs,
    sn, out_acc, d_acc, back, wide, xf, xb, work, recv, wide_work, wide_recv, x_work, x_recv,
    xb_work, xb_recv,
    d_att, d_gated, own_inner, slots, local, grads, chained, qp, dop, acc, send_sem, recv_sem,
):
    links = Links(send_sem, recv_sem)
    s = links.s
    links.greet(MIDDLE_NAMES)

    residual = x_ref[...].astype(F32) + summed[...].astype(F32)
    r2 = lax.rsqrt(jnp.mean(residual * residual, axis=1, keepdims=True) + EPSILON)
    sn[...] = (residual * r2 * gain[...]).astype(BF16)
    out_acc[...] = jnp.zeros_like(out_acc)
    d_acc[...] = jnp.zeros_like(d_acc)

    def part(c, carry):
        cols = pl.ds(pl.multiple_of(c * 256, 256), 256)
        wg, wu, wd = gu[0, :, cols], gu[1, :, cols], dw[cols]
        gate, up = nn(sn[...], wg), nn(sn[...], wu)
        sig = sigmoid(gate)
        act_gate = gate * sig
        act = (act_gate * up).astype(BF16)
        out_acc[...] += nn(act, wd)
        for cb in range(4):
            at = rows_at(1536 * cb + c * 256, 256)
            xf[at] = tn(act, cot_ref[:, pl.ds(256 * cb, 256)]).astype(BF16)
        d_act = nt(cot_ref[...], wd)
        d_gate = (d_act * up * (sig * (1.0 + gate * (1.0 - sig)))).astype(BF16)
        d_up = (d_act * act_gate).astype(BF16)
        xf[rows_at(1536 * c + 512, 1024)] = tn(sn[...], d_gate).astype(BF16)
        xf[rows_at(1536 * c + 3584, 1024)] = tn(sn[...], d_up).astype(BF16)
        d_acc[...] += nt(d_gate, wg) + nt(d_up, wu)
        return carry

    lax.fori_loop(0, 2, part, 0)
    d_second = d_acc[...]
    residual = x_ref[...].astype(F32) + summed[...].astype(F32)
    second_part[...] = jnp.broadcast_to(
        jnp.sum(d_second * residual * r2, axis=0, keepdims=True), second_part.shape
    )
    weighted = d_second * gain[...]
    inner = jnp.sum(weighted * residual, axis=1, keepdims=True)
    back[...] = (r2 * weighted - residual * (r2 * r2 * r2 / D * inner)).astype(BF16)
    links.met(MIDDLE_NAMES)

    sums = [
        Reduce(links, path, 128, back, 128 * p, work, recv, d_sum, 128 * p)
        for p, path in enumerate(HEAD_PATHS)
    ]
    x_jobs = [
        Reduce(links, path, 1536, xf, 1536 * p, x_work, x_recv, x_out, 1536 * p)
        for p, path in enumerate(SEQ_PATHS)
    ]
    summing = reduce_steps(sums)
    first_weights = reduce_steps(x_jobs)
    advance(summing, first_weights)
    put_wide(wide, out_acc[...])
    advance(summing, first_weights, summing)
    back_again = gather_steps(sums)
    advance(back_again, first_weights, back_again, first_weights, back_again)

    low = (cot_ref[...].astype(F32) + d_sum[...].astype(F32)).astype(BF16)
    scale = lax.rsqrt(column_of(squares[...]) / (MAMBA_HEADS * MP) + EPSILON)
    d_gated[...] = nt(low, wmo[...])
    product = d_gated[...] * mixed[...]
    own_inner[...] = row_sums(product * mgain[...])
    slots[links.h] = own_inner[...]
    copies = [links.send(own_inner, slots.at[links.h], name) for name in ("x1", "x2", "x3")]
    mixgain[...] = jnp.broadcast_to(jnp.sum(product * scale, axis=0, keepdims=True), mixgain.shape)
    for cb in range(4):
        lanes = slice(256 * cb, 256 * cb + 256)
        xb[pl.ds(512 * cb, MW)] = tn(gated[...], low[:, lanes]).astype(BF16)
        xb[pl.ds(512 * cb + MW, 128)] = tn(attended[...], low[:, lanes]).astype(BF16)
    d_att[...] = nt(low, wao[...]).astype(BF16)
    finish(first_weights)

    xb_jobs = [
        Reduce(links, path, 512, xb, 512 * p, xb_work, xb_recv, None, 512 * p)
        for p, path in enumerate(SEQ_PATHS)
    ]
    shares = [
        Reduce(links, path, 512, wide, 512 * p, wide_work, wide_recv, None, 512 * p)
        for p, path in enumerate(HEAD_PATHS)
    ]
    others = [gather_steps(x_jobs), reduce_steps(xb_jobs), reduce_steps(shares)]
    advance(*others)
    for copy in copies:
        copy.wait()

    inner_col = column_of((slots[0] + slots[1]) + (slots[2] + slots[3]))
    d_mixed = scale * (d_gated[...] * mgain[...]) - mixed[...] * (
        scale * scale * scale / (MAMBA_HEADS * MP) * inner_col
    )
    z = gz[...]
    sig = sigmoid(z)
    ds = d_mixed * (z * sig)
    d_ssd[...] = ds
    d_z[...] = (d_mixed * ssd[...] * (sig * (1.0 + z * (1.0 - sig)))).astype(BF16)
    step_x, enter_x, _ = decay_terms(decay, cum_ref)
    b, c = post[:, pl.ds(MW, NS)], post[:, pl.ds(MW + NS, NS)]
    entered = (ds * enter_x).astype(BF16)
    local[...] = tn(entered, c).astype(BF16)
    leaving_all = gather_steps(gather_rows(links, local, grads))
    advance(leaving_all)
    mixer_in = post[:, pl.ds(0, MW)].astype(F32)
    skip_part[...] = jnp.broadcast_to(jnp.sum(ds * mixer_in, axis=0, keepdims=True), skip_part.shape)
    scaled = (mixer_in * step_x).astype(BF16)
    gram = nt(c, b)
    mask = lower_mask()
    cum, cum_t = cum_ref[...], cumt_ref[...]
    left = lax.broadcasted_iota(jnp.int32, (ROWS, 128), 1) < MP
    low = ds.astype(BF16)
    d_gram = jnp.zeros((ROWS, ROWS), F32)
    for pair in range(3):
        lanes = slice(128 * pair, 128 * pair + 128)
        halves = []
        for k in range(2):
            decay = decay_of(cum, cum_t, 2 * pair + k, mask)
            here = left if k == 0 else jnp.logical_not(left)
            mine = jnp.where(here, ds[:, lanes], 0.0).astype(BF16)
            halves.append(tn((gram * decay).astype(BF16), low[:, lanes]))
            d_gram = d_gram + decay * nt(mine, scaled[:, lanes])
        d_scaled[:, pl.ds(128 * pair, 128)] = jnp.where(left, halves[0], halves[1])
    d_gram = d_gram.astype(BF16)
    d_bc[:, pl.ds(0, NS)] = tn(d_gram, c)
    d_bc[:, pl.ds(NS, NS)] = nn(d_gram, b) + nn(entered, state[...])

    qp[...] = stacked_queries(q[...])
    d_out = d_att[...].astype(F32)
    dop[...] = jnp.concatenate(
        [jnp.where(left, 0.0, pltpu.roll(d_out, HD, 1)), jnp.where(left, 0.0, d_out)], axis=0
    ).astype(BF16)
    product = (d_out * attended_f[...]).T
    delta = jnp.concatenate(
        [
            jnp.sum(product[:HD], axis=0, keepdims=True),
            jnp.sum(product[HD:], axis=0, keepdims=True),
        ],
        axis=1,
    )
    total = totals[pl.ds(0, 1)]
    pairs[...] = jnp.zeros_like(pairs)

    def block_grads(j, masked):
        block = load_block(kv_all, j)
        scores = nt(block, qp[...])
        if masked:
            scores = causal(scores)
        probs = jnp.exp(scores - total)
        d_probs = nt(block, dop[...])
        d_scores = (probs * (d_probs - delta)).astype(BF16)
        d_pair = (nn(d_scores, qp[...]) + nn(probs.astype(BF16), dop[...])).astype(BF16)
        for p in range(4):
            at = rows_at(2048 * p + block_position(j, p) * 64, 64)
            pairs[at] = d_pair[64 * p : 64 * p + 64]
        return tn(block, d_scores)

    acc[...] = block_grads(s, True)

    def hop(i, carry):
        acc[...] += block_grads(2 * i, False) + block_grads(2 * i + 1, False)
        return carry

    def last_hop(i, carry):
        acc[...] += block_grads(s - 1, False)
        return carry

    hops, turns = s // 2, 5
    for turn in range(turns):
        advance(leaving_all, *others)
        lax.fori_loop((hops * turn) // turns, (hops * (turn + 1)) // turns, hop, 0)
    lax.fori_loop(0, s % 2, last_hop, 0)
    out = acc[pl.ds(0, HD)] * (HD ** -0.5)
    d_q[...] = jnp.concatenate([out[:, :ROWS], out[:, ROWS:]], axis=0).T.astype(BF16)
    finish(leaving_all)
    chain(s, grads, logs_all, chained, False)
    leaving[...] = chained[...].astype(BF16)
    finish(*others)
    for p, job in enumerate(shares):
        share[pl.ds(128 * p, 128)] = own_rows(job, 128)
    for p, job in enumerate(xb_jobs):
        xb_piece[pl.ds(16 * p, 16)] = own_rows(job, 16)


LAST_NAMES = SEQ_NAMES + ("next", "prev", "x1", "x2", "x3")


def last_kernel(
    pairs, leaving, d_ssd, d_scaled, d_bc, skip, decay, cum, post, pre, ext, taps_m, taps_s, d_z, d_q,
    normed, x_ref, gain, wm, ws, wq, kvw, second_part, mixgain, skip_part, xb_piece,
    xb_out, ms_out, kq_out, share, small_out,
    pair_work, pair_recv, d_pre, edge_in, shifted, d_all, acc, kernel_grads, ms, ms_work, ms_recv,
    kq, kq_work, kq_recv, wide, wide_work, wide_recv, ms_slots, kq_slots, small_work, small_recv,
    small_x, send_sem, recv_sem,
):
    links = Links(send_sem, recv_sem)
    s = links.s
    links.greet(LAST_NAMES)
    links.met(LAST_NAMES)
    pair_jobs = [
        Reduce(links, path, 2048, pairs, 2048 * p, pair_work, pair_recv, None, 2048 * p)
        for p, path in enumerate(SEQ_PATHS)
    ]
    pairing = reduce_steps(pair_jobs)
    advance(pairing)
    output_weights = gather_steps(gather_rows(links, xb_piece, xb_out))

    step_x, _, tail_x = decay_terms(decay, cum)
    b = post[:, pl.ds(MW, NS)]
    mixer_in = post[:, pl.ds(0, MW)].astype(F32)
    tail_in = (mixer_in * step_x * tail_x).astype(BF16)
    scaled_grad = d_scaled[...] + tail_x * nt(b, leaving[...])
    d_pre[:, pl.ds(0, MW)] = widen(skip[...]) * d_ssd[...] + scaled_grad * step_x
    d_pre[:, pl.ds(MW, NS)] = d_bc[:, pl.ds(0, NS)] + nn(tail_in, leaving[...])
    d_pre[:, pl.ds(MW + NS, NS)] = d_bc[:, pl.ds(NS, NS)]
    for c in range(5):
        lanes = pl.ds(128 * c, 128)
        v = pre[:, lanes]
        sig = sigmoid(v)
        dp = d_pre[:, lanes] * (sig * (1.0 + v * (1.0 - sig)))
        d_pre[:, lanes] = dp
        rows = [jnp.sum(dp * ext[pl.ds(13 + k, ROWS), lanes], axis=0, keepdims=True) for k in range(KC)]
        rows.append(jnp.sum(dp, axis=0, keepdims=True))
        rows.append(jnp.zeros((3, 128), F32))
        kernel_grads[:, lanes] = jnp.concatenate(rows, axis=0)
    edge_copy = links.send(d_pre.at[pl.ds(0, 8)], edge_in, "prev")
    advance(pairing)
    d_all[:, pl.ds(0, MW)] = d_z[...]
    d_all[:, pl.ds(1024, 128)] = d_q[...]

    def early(i, carry):
        rows = pl.ds(pl.multiple_of(i * 256, 256), 256)
        ms[rows, pl.ds(0, MW)] = tn(normed[:, rows], d_all[:, pl.ds(0, MW)]).astype(BF16)
        kq[rows] = tn(normed[:, rows], d_all[:, pl.ds(1024, 128)]).astype(BF16)
        acc[:, rows] = nt(d_all[:, pl.ds(0, MW)], wm[0, rows]) + nt(d_all[:, pl.ds(1024, 128)], wq[rows])
        return carry

    lax.fori_loop(0, 4, early, 0)
    advance(pairing)
    edge_copy.wait()
    keep = jnp.where(s < SEQ - 1, 1.0, 0.0)
    shifted[pl.ds(0, ROWS)] = d_pre[...]
    shifted[pl.ds(ROWS, 8)] = edge_in[...] * keep
    for c in range(5):
        lanes = pl.ds(128 * c, 128)
        taps, own = of_channels(taps_m, taps_s, c)
        total = taps[pl.ds(0, 1), own] * shifted[pl.ds(3, ROWS), lanes]
        for k in range(1, KC):
            total = total + taps[pl.ds(k, 1), own] * shifted[pl.ds(3 - k, ROWS), lanes]
        to = 640 + 128 * c if c < 3 else 384 + 128 * (c - 3)
        d_all[:, pl.ds(to, 128)] = total.astype(BF16)

    def middle(i, carry):
        rows = pl.ds(pl.multiple_of(i * 256, 256), 256)
        late = pl.ds(pl.multiple_of(i * 256 + 1024, 256), 256)
        mine = normed[:, rows]
        states = tn(mine, d_all[:, pl.ds(MW, 256)]).astype(BF16)
        ms[rows, pl.ds(MW, 128)] = states[:, :128]
        ms[late, pl.ds(MW, 128)] = states[:, 128:]
        ms[late, pl.ds(0, MW)] = tn(mine, d_all[:, pl.ds(640, MW)]).astype(BF16)
        return carry

    lax.fori_loop(0, 4, middle, 0)
    ms_jobs = [
        Reduce(links, path, 512, ms, 512 * p, ms_work, ms_recv, None, 512 * p)
        for p, path in enumerate(SEQ_PATHS)
    ]

    def mixer_weights():
        yield from reduce_steps(ms_jobs)
        for p, job in enumerate(ms_jobs):
            at = rows_at(job.base + job.start, 16)
            ms_slots[links.h, pl.ds(16 * p, 16)] = ms_work[at, pl.ds(MW, 128)]
        slot = ms_slots.at[links.h]
        copies = [links.send(slot, slot, name) for name in ("x1", "x2", "x3")]
        yield
        for copy in copies:
            copy.wait()
        for p, job in enumerate(ms_jobs):
            at = rows_at(job.base + job.start, 16)
            parts = [ms_slots[k, pl.ds(16 * p, 16)].astype(F32) for k in range(HEADS)]
            ms_out[at, pl.ds(0, MW)] = ms_work[at, pl.ds(0, MW)]
            ms_out[at, pl.ds(MW, 128)] = ((parts[0] + parts[1]) + (parts[2] + parts[3])).astype(BF16)
            job.out = ms_out
        yield from gather_steps(ms_jobs)

    mixing = mixer_weights()
    advance(pairing, mixing, output_weights)

    def late_part(i, carry):
        rows = pl.ds(pl.multiple_of(i * 256, 256), 256)
        total = acc[:, rows] + nt(d_all[:, pl.ds(640, MW)], wm[1, rows])
        acc[:, rows] = total + nt(d_all[:, pl.ds(MW, 256)], ws[rows])
        return carry

    lax.fori_loop(0, 4, late_part, 0)
    finish(pairing)
    for p, job in enumerate(pair_jobs):
        d_all[pl.ds(64 * p, 64), pl.ds(1152, 128)] = own_rows(job, 64)
    advance(mixing, output_weights)
    left = lax.broadcasted_iota(jnp.int32, (ROWS, 128), 1) < HD
    d_pair = d_all[:, pl.ds(1152, 128)].astype(F32)
    other = pltpu.roll(d_pair, HD, 1)
    zero = jnp.zeros_like(d_pair)
    low_head = links.h < 2
    d_keys = jnp.where(low_head, jnp.where(left, d_pair, zero), jnp.where(left, zero, other)).astype(BF16)
    d_values = jnp.where(low_head, jnp.where(left, other, zero), jnp.where(left, zero, d_pair)).astype(BF16)

    def pair_part(i, carry):
        rows = pl.ds(pl.multiple_of(i * 256, 256), 256)
        late = pl.ds(pl.multiple_of(i * 256 + 1024, 256), 256)
        pair = d_all[:, pl.ds(1152, 128)]
        kq[late] = tn(normed[:, rows], pair).astype(BF16)
        acc[:, rows] += nt(d_keys, kvw[0, rows]) + nt(d_values, kvw[1, rows])
        return carry

    lax.fori_loop(0, 4, pair_part, 0)
    kq_jobs = [
        Reduce(links, path, 512, kq, 512 * p, kq_work, kq_recv, None, 512 * p)
        for p, path in enumerate(SEQ_PATHS)
    ]

    def head_weights():
        yield from reduce_steps(kq_jobs)
        for p in (2, 3):
            job = kq_jobs[p]
            kq_slots[links.h, pl.ds(16 * (p - 2), 16)] = own_rows(job, 16)
        slot = kq_slots.at[links.h]
        copies = [links.send(slot, slot, name) for name in ("x1", "x2", "x3")]
        yield
        for copy in copies:
            copy.wait()
        for p, job in enumerate(kq_jobs):
            at = rows_at(job.base + job.start, 16)
            job.out = kq_out
            if p < 2:
                kq_out[at, pl.ds(0, 128)] = own_rows(job, 16)
            else:
                parts = [kq_slots[k, pl.ds(16 * (p - 2), 16)].astype(F32) for k in range(HEADS)]
                kq_out[at, pl.ds(0, 128)] = (parts[0] + parts[1]).astype(BF16)
                kq_out[at, pl.ds(128, 128)] = (parts[2] + parts[3]).astype(BF16)
        yield from gather_steps(kq_jobs, [128, 128, None, None])

    heading = head_weights()
    advance(heading)
    x = x_ref[...].astype(F32)
    r1 = lax.rsqrt(jnp.mean(x * x, axis=1, keepdims=True) + EPSILON)
    d_normed = acc[...]
    weighted = d_normed * gain[...]
    inner = jnp.sum(weighted * x, axis=1, keepdims=True)
    put_wide(wide, r1 * weighted - x * (r1 * r1 * r1 / D * inner))
    shares = [
        Reduce(links, path, 512, wide, 512 * p, wide_work, wide_recv, None, 512 * p)
        for p, path in enumerate(HEAD_PATHS)
    ]
    sharing = reduce_steps(shares)
    advance(sharing)
    blank = jnp.zeros((1, 256), F32)
    grads = kernel_grads[...]
    vector_rows = [
        [jnp.sum(d_normed * x * r1, axis=0, keepdims=True)],
        [second_part[pl.ds(0, 1)]],
        [grads[k : k + 1, MW:] for k in range(KC)],
        [grads[KC : KC + 1, MW:], blank, blank, blank],
        [grads[0:1, :MW], grads[KC : KC + 1, :MW], blank],
        [grads[1:2, :MW], mixgain[pl.ds(0, 1)], blank],
        [grads[2:3, :MW], skip_part[pl.ds(0, 1)], blank],
        [grads[3:4, :MW], blank, blank, blank[:, :128]],
    ]
    small_work[0] = jnp.concatenate([jnp.concatenate(row, axis=1) for row in vector_rows], axis=0)

    def vectors():
        for step, name in enumerate(DOUBLING):
            copy = links.send(small_work.at[step], small_recv.at[step], name)
            yield
            copy.wait()
            small_work[step + 1] = small_work[step] + small_recv[step]
        small_x[links.h] = small_work[5]
        copies = [links.send(small_work.at[5], small_x.at[links.h], n) for n in ("x1", "x2", "x3")]
        yield
        for copy in copies:
            copy.wait()
        total = (small_x[0] + small_x[1]) + (small_x[2] + small_x[3])
        row = lax.broadcasted_iota(jnp.int32, (8, 1024), 0)
        small_out[...] = jnp.where(row < 4, total, small_work[5])

    finish(heading, mixing, sharing, vectors(), output_weights)
    for p, job in enumerate(shares):
        share[pl.ds(128 * p, 128)] = own_rows(job, 128)


def widths_kernel(
    h, down0, down1, down2, down3, gate0, gate1, up0, up1, mix0, mix1, mix2, mix3, head, tail, query_in,
    keyval_in, x_ref, summed, out_share, cot, d_sum, in_share, small,
    down, gateup, mixout, attn, mixer, query, keyval, state, block_out, input_grads,
    gain, second, kernel_m, kernel_s, bias_m, bias_s, skip, mgain,
):
    i = pl.program_id(0)
    for cb, block in enumerate((down0, down1, down2, down3)):
        down[:, pl.ds(256 * cb, 256)] = block[...].astype(F32)
    for cb, block in enumerate((gate0, gate1)):
        gateup[0, :, pl.ds(256 * cb, 256)] = block[...].astype(F32)
    for cb, block in enumerate((up0, up1)):
        gateup[1, :, pl.ds(256 * cb, 256)] = block[...].astype(F32)

    @pl.when(i < 3)
    def _():
        for cb, block in enumerate((mix0, mix1, mix2, mix3)):
            mixout[:, pl.ds(256 * cb, 256)] = block[...].astype(F32)

    @pl.when(i == 3)
    def _():
        for cb, block in enumerate((mix0, mix1, mix2, mix3)):
            attn[:, pl.ds(256 * cb, 256)] = block[...].astype(F32)

    mixer[0] = head[:, pl.ds(0, MW)].astype(F32)
    mixer[1] = tail[:, pl.ds(0, MW)].astype(F32)
    state[:, pl.ds(0, 128)] = head[:, pl.ds(MW, 128)].astype(F32)
    state[:, pl.ds(128, 128)] = tail[:, pl.ds(MW, 128)].astype(F32)
    query[...] = query_in[...].astype(F32)
    left = lax.broadcasted_iota(jnp.int32, (256, 128), 1) < HD
    first, second_head = keyval_in[:, pl.ds(0, 128)].astype(F32), keyval_in[:, pl.ds(128, 128)].astype(F32)
    keyval[0] = jnp.where(left, first, pltpu.roll(second_head, HD, 1))
    keyval[1] = jnp.where(left, pltpu.roll(first, HD, 1), second_head)
    block_out[...] = x_ref[...].astype(F32) + summed[...].astype(F32) + out_share[...].astype(F32)
    input_grads[...] = cot[...].astype(F32) + d_sum[...].astype(F32) + in_share[...].astype(F32)

    @pl.when(i == 0)
    def _():
        gain[...] = small[pl.ds(0, 1)]
        second[...] = small[pl.ds(1, 1)]
        kernel_m[...] = small[pl.ds(4, KC), pl.ds(0, MW)]
        for k in range(KC):
            kernel_s[pl.ds(k, 1)] = small[pl.ds(2, 1), pl.ds(256 * k, 256)]
        bias_m[...] = small[pl.ds(4, 1), pl.ds(MW, MW)]
        bias_s[...] = small[pl.ds(3, 1), pl.ds(0, 256)]
        skip[...] = exact(small[pl.ds(6, 1), pl.ds(MW, MW)], head_spread(), ((1,), (1,)))
        mgain[...] = small[pl.ds(5, 1), pl.ds(MW, MW)]


def widened(h, x_out, xb_out, ms_out, kq_out, x_ref, summed, out_share, cot, d_sum, in_share, small):
    def rows(count, width, offset=0):
        return pl.BlockSpec((count, width), lambda i, h: (i + offset, 0))

    def halves(count, width):
        return pl.BlockSpec((2, count, width), lambda i, h: (0, i, 0))

    def whole(count, width):
        return pl.BlockSpec((count, width), lambda i, h: (0, 0))

    own = pl.BlockSpec((64, 256), lambda i, h: (i, h[0]))
    grid = pltpu.PrefetchScalarGridSpec(
        num_scalar_prefetch=1,
        grid=(4,),
        in_specs=[rows(128, 256, 12 * cb) for cb in range(4)]
        + [rows(256, 256, 6 * cb + 2) for cb in range(4)]
        + [rows(128, 256, 4 * cb) for cb in range(4)]
        + [rows(256, 512), rows(256, 512, 4), rows(256, 128), rows(256, 256, 4)]
        + [own, own, rows(64, 256), own, own, rows(64, 256), whole(8, D)],
        out_specs=(
            rows(128, D), halves(256, 512),
            pl.BlockSpec((128, D), lambda i, h: (jnp.minimum(i, 2), 0)), whole(128, D),
            halves(256, MW), rows(256, 128), halves(256, 128), rows(256, 256),
            rows(64, 256), rows(64, 256),
            whole(1, D), whole(1, D), whole(KC, MW), whole(KC, 256), whole(1, MW), whole(1, 256),
            whole(1, HMH), whole(1, MW),
        ),
    )
    return pl.pallas_call(
        widths_kernel,
        grid_spec=grid,
        out_shape=(
            shape((512, D), F32), shape((2, D, 512), F32), shape((MW, D), F32), shape((128, D), F32),
            shape((2, D, MW), F32), shape((D, 128), F32), shape((2, D, 128), F32), shape((D, 256), F32),
            shape((ROWS, 256), F32), shape((ROWS, 256), F32),
            shape((1, D), F32), shape((1, D), F32), shape((KC, MW), F32), shape((KC, 256), F32),
            shape((1, MW), F32), shape((1, 256), F32), shape((1, HMH), F32), shape((1, MW), F32),
        ),
        compiler_params=pltpu.CompilerParams(vmem_limit_bytes=VMEM_LIMIT),
    )(
        h, *[x_out] * 8, *[xb_out] * 4, ms_out, ms_out, kq_out, kq_out, x_ref, summed, out_share, cot,
        d_sum, in_share, small,
    )


def on_device(
    hidden_in, cotangent, log_decay, norm_gain, query_weight, keyvalue_weight, attention_output,
    mixer_weight, state_weight, kernel_mixer, kernel_state, bias_mixer, bias_state, skip_gain,
    mixer_gain, mixer_output, second_gain, gate_up, down_weight,
):
    gain1 = norm_gain.reshape(1, D)
    gain2 = second_gain.reshape(1, D)
    mgain = mixer_gain.reshape(1, MW)
    skip = skip_gain.reshape(1, HMH)
    bias_m, bias_s = bias_mixer.reshape(1, MW), bias_state.reshape(1, 256)
    (
        cum, cum_t, normed, q, kv_all, logs_all, gz, ext, pre, post, attended, attended_f, totals, ssd, mixed,
        squares, state, gated, summed,
    ) = call(
        forward_kernel,
        [
            shape((ROWS, HMH), F32), shape((HMH, ROWS), F32),
            shape((ROWS, D), BF16), shape((ROWS, 128), BF16), shape((8192, 128), BF16),
            shape((256, 128), F32), shape((ROWS, MW), F32), shape((ROWS + 16, CW), F32),
            shape((ROWS, CW), F32), shape((ROWS, CW), BF16), shape((ROWS, 128), BF16),
            shape((ROWS, 128), F32), shape((8, 512), F32), shape((ROWS, MW), F32),
            shape((ROWS, MW), F32), shape((8, ROWS), F32), shape((MW, NS), BF16),
            shape((ROWS, MW), BF16), shape((ROWS, D), BF16),
        ],
        (
            hidden_in, gain1, query_weight, keyvalue_weight, mixer_weight, state_weight, kernel_mixer,
            kernel_state, bias_m, bias_s, log_decay, skip, mgain, mixer_output, attention_output,
        ),
        scratch=[
            pltpu.VMEM((ROWS, 128), BF16), pltpu.VMEM((8, 128), F32),
            pltpu.VMEM((16, D), BF16), pltpu.VMEM((16, D), BF16),
            pltpu.VMEM((MW, NS), BF16), pltpu.VMEM((12288, NS), BF16), pltpu.VMEM((MW, NS), F32),
            pltpu.VMEM((512, 128), BF16), pltpu.VMEM((128, 512), F32), pltpu.VMEM((8, ROWS), F32),
            pltpu.VMEM((HEADS, 8, ROWS), F32), pltpu.VMEM((ROWS, D), F32),
            pltpu.VMEM((ROWS, D), BF16), pltpu.VMEM((ROWS, D), BF16), pltpu.VMEM((ROWS, D), BF16),
        ],
        collective=1, copies=80,
    )
    (
        d_sum, out_share, x_out, xb_piece, second_part, mixgain, d_z, d_ssd, skip_part, d_scaled, d_bc, leaving,
        d_q, pairs,
    ) = call(
        middle_kernel,
        [
            shape((ROWS, D), BF16), shape((ROWS, 256), BF16), shape((6144, 256), BF16),
            shape((64, 256), BF16),
            shape((8, D), F32), shape((8, MW), F32), shape((ROWS, MW), BF16), shape((ROWS, MW), F32),
            shape((8, MW), F32), shape((ROWS, MW), F32), shape((ROWS, 256), F32),
            shape((MW, NS), BF16), shape((ROWS, 128), BF16), shape((8192, 128), BF16),
        ],
        (
            hidden_in, summed, cotangent, gain2, gate_up, down_weight, gated, attended, mixer_output,
            attention_output, mixed, squares, mgain, gz, ssd, post, log_decay, cum, cum_t, state, q, kv_all,
            attended_f, totals, logs_all,
        ),
        scratch=[
            pltpu.VMEM((ROWS, D), BF16), pltpu.VMEM((ROWS, D), F32), pltpu.VMEM((ROWS, D), F32),
            pltpu.VMEM((ROWS, D), BF16), pltpu.VMEM((1024, 256), BF16), pltpu.VMEM((6144, 256), BF16),
            pltpu.VMEM((2048, 256), BF16), pltpu.VMEM((ROWS, D), BF16), pltpu.VMEM((ROWS, D), BF16),
            pltpu.VMEM((1024, 256), BF16), pltpu.VMEM((1024, 256), BF16),
            pltpu.VMEM((6144, 256), BF16), pltpu.VMEM((6144, 256), BF16),
            pltpu.VMEM((2048, 256), BF16), pltpu.VMEM((2048, 256), BF16),
            pltpu.VMEM((ROWS, 128), BF16), pltpu.VMEM((ROWS, MW), F32), pltpu.VMEM((8, ROWS), F32),
            pltpu.VMEM((HEADS, 8, ROWS), F32), pltpu.VMEM((MW, NS), BF16),
            pltpu.VMEM((12288, NS), BF16), pltpu.VMEM((MW, NS), F32), pltpu.VMEM((512, 128), BF16),
            pltpu.VMEM((512, 128), BF16), pltpu.VMEM((128, 512), F32),
        ],
        collective=2, copies=150,
    )
    xb_out, ms_out, kq_out, in_share, small = call(
        last_kernel,
        [
            shape((2048, 256), BF16), shape((2048, 512), BF16), shape((2048, 256), BF16),
            shape((ROWS, 256), BF16),
            shape((8, D), F32),
        ],
        (
            pairs, leaving, d_ssd, d_scaled, d_bc, skip, log_decay, cum, post, pre, ext, kernel_mixer,
            kernel_state, d_z, d_q, normed, hidden_in, gain1, mixer_weight, state_weight, query_weight,
            keyvalue_weight, second_part, mixgain, skip_part, xb_piece,
        ),
        scratch=[
            pltpu.VMEM((8192, 128), BF16), pltpu.VMEM((8192, 128), BF16), pltpu.VMEM((ROWS, CW), F32),
            pltpu.VMEM((8, CW), F32), pltpu.VMEM((ROWS + 8, CW), F32), pltpu.VMEM((ROWS, 1280), BF16),
            pltpu.VMEM((ROWS, D), F32), pltpu.VMEM((8, CW), F32),
            pltpu.VMEM((2048, 512), BF16), pltpu.VMEM((2048, 512), BF16), pltpu.VMEM((2048, 512), BF16),
            pltpu.VMEM((2048, 128), BF16), pltpu.VMEM((2048, 128), BF16), pltpu.VMEM((2048, 128), BF16),
            pltpu.VMEM((1024, 256), BF16), pltpu.VMEM((1024, 256), BF16), pltpu.VMEM((1024, 256), BF16),
            pltpu.VMEM((HEADS, 64, 128), BF16), pltpu.VMEM((HEADS, 32, 128), BF16),
            pltpu.VMEM((6, 8, D), F32), pltpu.VMEM((5, 8, D), F32), pltpu.VMEM((HEADS, 8, D), F32),
        ],
        collective=3, copies=190,
    )

    h = lax.axis_index("head").astype(jnp.int32).reshape(1)
    (
        down, gateup, mixout, attn, mixer, query, keyval, state_grads, block_out, input_grads,
        gain_grads, second_grads, mixkernel, statekernel, mixbias, statebias, skip_grads, mixgain_grads,
    ) = widened(
        h, x_out, xb_out, ms_out, kq_out, hidden_in, summed, out_share, cotangent, d_sum, in_share, small
    )
    return (
        block_out,
        input_grads,
        gain_grads.reshape(D),
        query,
        keyval,
        attn,
        mixer,
        state_grads,
        mixkernel,
        statekernel,
        mixbias.reshape(MW),
        statebias.reshape(256),
        skip_grads.reshape(HMH),
        mixgain_grads.reshape(MW),
        mixout,
        second_grads.reshape(D),
        gateup,
        down,
    )


def solution(mesh):
    return jax.shard_map(
        on_device,
        mesh=mesh,
        in_specs=(
            P("seq", None), P("seq", None), P("seq", "head"), P(), P(None, "head"), P(),
            P("head", None), P(None, None, "head"), P(), P(None, "head"), P(), P("head"), P(),
            P("head"), P("head"), P("head", None), P(), P(None, None, "head"), P("head", None),
        ),
        out_specs=(
            P("seq", "head"), P("seq", "head"), P(), P(None, "head"), P(), P("head", None),
            P(None, None, "head"), P(), P(None, "head"), P(), P("head"), P(), P("head"), P("head"),
            P("head", None), P(), P(None, None, "head"), P("head", None),
        ),
        check_vma=False,
    )
```

time: 278 us -> 214 us (0.77)
  Pallas kernels: 260 us -> 202 us
  other arithmetic: 4.81 us -> 1.19 us
    pallas_call x12 -> x3, Pallas kernels: 253 us -> 193 us  [call(): pl.pallas_call(body, out_shape=tuple(outs), in_specs=in_specs, out_specs=...]
    unnamed x41 -> x45, local copies, waits for them, and re-layouts: 5.5 us -> 8.93 us
where the time goes in v2:
time: 214 us
  Pallas kernels  202 us (94%)
  local copies, waits for them, and re-layouts  10.3 us (5%)
    pallas_call x3, Pallas kernels, call(): pl.pallas_call(body, out_shape=tuple(outs), in_specs=in_specs, out_specs=...  193 us
    unnamed x45, local copies, waits for them, and re-layouts  8.93 us
    pallas_call x1, Pallas kernels, widened(): pl.pallas_call(widths_kernel, grid_spec=grid, out_shape=(shape((512, D),...  8.63 us

profile of v2, /device:TPU:1, one launch (start us, length us, event | category | flops | bytes accessed | tf_op | source)
XLA Modules:
  0.0 213.9 jit_solution(7535438373830241733)
XLA Ops:
  0.7 0.7 reshape.80.mgain
  1.3 0.7 reshape.77.bias_m
  2.0 0.8 copy.37.decay
  2.9 0.0 copy-start.6
  2.9 0.9 copy-done.6
  3.8 0.9 copy-done.8
  4.8 0.7 copy-done.12
  5.5 0.7 copy-done.14
  6.1 0.7 copy-done.16
  6.8 0.7 copy-done.19
  7.5 0.7 copy-done.21
  8.2 63.6 %shard_map.322 = (f32[256,6]{1,0:T(8,128)S(1)}, f32[6,256]{1,0:T(8,128)S(1)}, bf16[256,1024]{1,0:T(8,128)(2,1)S(1)}, bf16[256,128]{1,0:T(8,128)(2,1)S(1)}, bf16[...) custom-call(bf16[256,1024]{1,0:T(8,128)(2,1)} %x_ref.7, ...), custom_call_target="tpu_custom_call" | custom-call | tf_op jit(solution)/shard_map/pallas_call | solution.py:304
  71.8 0.0 copy-start.3
  71.8 0.8 copy-done.3
  72.6 0.7 copy-done.11
  73.3 0.0 copy-done.7
  73.4 0.0 copy-start.9
  73.4 0.0 copy-start.13
  73.4 0.0 copy-start.15
  73.4 0.0 copy-start.17
  73.4 0.0 copy-start.20
  73.4 67.0 %shard_map.323 = (bf16[256,1024]{1,0:T(8,128)(2,1)}, bf16[256,256]{1,0:T(8,128)(2,1)S(1)}, bf16[6144,256]{1,0:T(8,128)(2,1)}, bf16[64,256]{1,0:T(8,128)(2,1)S(1)...) custom-call(bf16[256,1024]{1,0:T(8,128)(2,1)} %x_ref.7, ...), custom_call_target="tpu_custom_call" | custom-call | tf_op jit(solution)/shard_map/pallas_call | solution.py:304
  140.4 0.0 copy-done.1
  140.4 0.0 copy-done.5
  140.4 0.0 copy-done.9
  140.5 0.0 copy-start.2
  140.5 0.0 copy-start.4
  140.5 62.3 %shard_map.324 = (bf16[2048,256]{1,0:T(8,128)(2,1)}, bf16[2048,512]{1,0:T(8,128)(2,1)}, bf16[2048,256]{1,0:T(8,128)(2,1)}, bf16[256,256]{1,0:T(8,128)(2,1)S(1)}, f32[8,1024]{1,0:T(8,128)S(1)}) custom-call(bf16[8192,128]{1,0:T(8,128)(2,1)} %get-tuple-element.91.pairs, bf16[384,128]{1,0:T(8,128)(2,1)S(1)} %get-tuple-element.92.leaving, ...), custom_call_target="tpu_custom_call" | custom-call | tf_op jit(solution)/shard_map/pallas_call | solution.py:304
  202.8 1.2 copy-done
  204.0 8.6 %shard_map.325 = (f32[512,1024]{1,0:T(8,128)}, f32[2,1024,512]{2,1,0:T(8,128)}, f32[384,1024]{1,0:T(8,128)}, f32[128,1024]{1,0:T(8,128)}, f32[2,1024,384]{2,1,0:...) custom-call(s32[1]{0:T(128)} %bitcast.h, ...), custom_call_target="tpu_custom_call" | custom-call | tf_op jit(solution)/shard_map/pallas_call | solution.py:1054
  212.7 0.6 reduce
  213.3 0.6 reduce.1
  (21 shorter events, 0.0 us)
Async XLA Ops:
  2.9 1.0 copy-start.6
  3.8 0.9 copy-start.8
  4.8 0.7 copy-start.12
  5.5 0.7 copy-start.14
  6.1 0.7 copy-start.16
  6.8 0.7 copy-start.19
  7.5 0.7 copy-start.21
  8.2 65.2 %copy-start.7 = (bf16[128,1024]{1,0:T(8,128)(2,1)S(1)}, bf16[128,1024]{1,0:T(8,128)(2,1)}, u32[]{:S(2)}) copy-start(bf16[128,1024]{1,0:T(8,128)(2,1)} %wao.3) | copy-start | bytes 786436
  8.2 65.2 %copy-start.18 = (f32[1024]{0:T(1024)S(1)}, f32[1024]{0:T(1024)}, u32[]{:S(2)}) copy-start(f32[1024]{0:T(1024)} %param.35) | copy-start | bytes 12292
  71.8 0.8 copy-start.3
  72.6 0.7 copy-start.11
  73.3 67.1 %copy-start.1 = (bf16[256,1024]{1,0:T(8,128)(2,1)S(1)}, bf16[256,1024]{1,0:T(8,128)(2,1)}, u32[]{:S(2)}) copy-start(bf16[256,1024]{1,0:T(8,128)(2,1)} %x_ref.7) | copy-start | bytes 1572868
  73.3 67.1 %copy-start.5 = (bf16[1024,256]{1,0:T(8,128)(2,1)S(1)}, bf16[1024,256]{1,0:T(8,128)(2,1)}, u32[]{:S(2)}) copy-start(bf16[1024,256]{1,0:T(8,128)(2,1)} %ws.3) | copy-start | bytes 1572868
  73.4 67.1 %copy-start.9 = (bf16[1024,128]{1,0:T(8,128)(2,1)S(1)}, bf16[1024,128]{1,0:T(8,128)(2,1)}, u32[]{:S(2)}) copy-start(bf16[1024,128]{1,0:T(8,128)(2,1)} %wq.3) | copy-start | bytes 786436
  73.4 67.1 %copy-start.13 = (f32[4,384]{1,0:T(4,128)S(1)}, f32[4,384]{1,0:T(4,128)}, u32[]{:S(2)}) copy-start(f32[4,384]{1,0:T(4,128)} %taps_m.3) | copy-start | bytes 18436
  73.4 67.1 %copy-start.15 = (f32[1024]{0:T(1024)S(1)}, f32[1024]{0:T(1024)}, u32[]{:S(2)}) copy-start(f32[1024]{0:T(1024)} %param.22) | copy-start | bytes 12292
  73.4 67.1 %copy-start.17 = (f32[4,256]{1,0:T(4,128)S(1)}, f32[4,256]{1,0:T(4,128)}, u32[]{:S(2)}) copy-start(f32[4,256]{1,0:T(4,128)} %taps_s.3) | copy-start | bytes 12292
  73.4 67.1 %copy-start.20 = (f32[6]{0:T(128)S(1)}, f32[6]{0:T(128)}, u32[]{:S(2)}) copy-start(f32[6]{0:T(128)} %param.32) | copy-start | bytes 76
  140.5 62.3 %copy-start.2 = (bf16[256,1024]{1,0:T(8,128)(2,1)S(1)}, bf16[256,1024]{1,0:T(8,128)(2,1)}, u32[]{:S(2)}) copy-start(bf16[256,1024]{1,0:T(8,128)(2,1)} %cot.1) | copy-start | bytes 1572868
  140.5 62.3 %copy-start.4 = (bf16[256,1024]{1,0:T(8,128)(2,1)S(1)}, bf16[256,1024]{1,0:T(8,128)(2,1)}, u32[]{:S(2)}) copy-start(bf16[256,1024]{1,0:T(8,128)(2,1)} %copy-done.3) | copy-start | bytes 1572868
  140.5 62.3 %copy-start.10 = (bf16[256,1024]{1,0:T(8,128)(2,1)S(1)}, bf16[256,1024]{1,0:T(8,128)(2,1)}, u32[]{:S(2)}) copy-start(bf16[256,1024]{1,0:T(8,128)(2,1)} %get-tuple-element.109.d_sum) | copy-start | bytes 1572868
  202.8 1.2 copy-start

commit v3 on v2

--- a/solution.py
+++ b/solution.py
@@ -75,6 +75,8 @@
     ("c", "za", "zb", "y4"),
     ("c", "zb", "za", "y4"),
 )
+LOG_PATH = ("c", "y4", "z4")
+SHORT_PATHS = (("c", "y4", "z4"), ("c", "z4", "y4"))
 HEAD_PATHS = (("xa", "xb"), ("xb", "xa"))
 
 
@@ -168,7 +170,6 @@
 
 DONE = object()
 SEQ_NAMES = ("c", "y41", "y42", "y43", "z41", "z42", "z43")
-DOUBLING = ("c", "ya", "yb", "za", "zb")
 
 
 def rows_at(start, count, unit=16):
@@ -364,27 +365,87 @@
         lanes = pl.ds(128 * c, 128)
         taps, own = of_channels(taps_m, taps_s, c)
         bias, own = of_channels(bias_m, bias_s, c)
-        total = bias[:, own] + taps[pl.ds(0, 1), own] * ext[pl.ds(13, ROWS), lanes]
+        offset = bias[own].reshape(1, 128) if c < 3 else bias[:, own]
+        total = offset + taps[pl.ds(0, 1), own] * ext[pl.ds(13, ROWS), lanes]
         for k in range(1, KC):
             total = total + taps[pl.ds(k, 1), own] * ext[pl.ds(13 + k, ROWS), lanes]
         pre[:, lanes] = total
         post[:, lanes] = (total * sigmoid(total)).astype(BF16)
 
 
-def chain(s, gathered, logs, total, forward):
-    total[...] = jnp.zeros_like(total)
-
-    def hop(i, run):
-        j = s - 1 - i if forward else s + 1 + i
-        weight = jnp.exp(run)
-        for seg in range(12):
-            p, off = seg // 3, (seg % 3) * 32
-            at = rows_at(p * 3072 + block_position(j, p) * 96 + off, 32)
-            h = seg // 2
-            total[pl.ds(32 * seg, 32)] += weight[h : h + 1, :] * gathered[at].astype(F32)
-        return run + logs[rows_at(block_position(j, 0) * 8, 8, 8)]
-
-    lax.fori_loop(0, s if forward else SEQ - 1 - s, hop, jnp.zeros((8, 128), F32))
+def scan_steps(links, local, logs, sibling, row_slots, plane_slots, halves, result, forward):
+    s, core, y, z = links.s, links.bits["c"], links.bits["y4"], links.bits["z4"]
+    turn = range(4) if forward else range(3, -1, -1)
+    copy = links.send(local, sibling, "c")
+    yield
+
+    def log_of(j):
+        return logs[rows_at(position(seq_bits(j), LOG_PATH) * 8, 8, 8)]
+
+    def of_half(tile, k):
+        return jnp.where(core == 0, tile[k : k + 1], tile[HMH // 2 + k : HMH // 2 + k + 1])
+
+    first = core == (0 if forward else 1)
+    other = s + 1 - 2 * core
+    own_weight = jnp.where(first, jnp.exp(log_of(other)), 1.0)
+    other_weight = jnp.where(first, 1.0, jnp.exp(log_of(s)))
+    row_logs = [log_of(8 * z + 2 * k) + log_of(8 * z + 2 * k + 1) for k in range(4)]
+    plane_logs = []
+    for k in range(4):
+        total = log_of(8 * k)
+        for j in range(1, 8):
+            total = total + log_of(8 * k + j)
+        plane_logs.append(total)
+
+    def exclusive(slots, tiles, at, k):
+        rows = pl.ds(64 * k, 64)
+        total = jnp.zeros((64, NS), F32)
+        before = total
+        for j in turn:
+            before = jnp.where(at == j, total, before)
+            total = of_half(jnp.exp(tiles[j]), k) * total + slots[j, rows].astype(F32)
+        return before, total
+
+    copy.wait()
+    for k in range(3):
+        rows = rows_at(192 * core + 64 * k, 64)
+        total = of_half(own_weight, k) * local[rows].astype(F32)
+        total = total + of_half(other_weight, k) * sibling[rows].astype(F32)
+        row_slots[y, pl.ds(64 * k, 64)] = total.astype(BF16)
+    slot = row_slots.at[y]
+    copies = [links.send(slot, slot, name) for name in ("y41", "y42", "y43")]
+    yield
+    for copy in copies:
+        copy.wait()
+    within = []
+    for k in range(3):
+        before, total = exclusive(row_slots, row_logs, y, k)
+        within.append(before)
+        plane_slots[z, pl.ds(64 * k, 64)] = total.astype(BF16)
+    slot = plane_slots.at[z]
+    copies = [links.send(slot, slot, name) for name in ("z41", "z42", "z43")]
+    ahead = jnp.zeros((8, 128), F32)
+    passed = ahead
+    for j in turn:
+        passed = jnp.where(y == j, ahead, passed)
+        ahead = ahead + row_logs[j]
+    yield
+    for copy in copies:
+        copy.wait()
+    for k in range(3):
+        before, _ = exclusive(plane_slots, plane_logs, z, k)
+        total = of_half(jnp.exp(passed), k) * before + within[k]
+        halves[rows_at(192 * core + 64 * k, 64)] = total.astype(BF16)
+    mine = halves.at[rows_at(192 * core, 192)]
+    copy = links.send(mine, mine, "c")
+    yield
+    copy.wait()
+    fade = jnp.exp(log_of(other))
+    for k in range(HMH):
+        rows = pl.ds(64 * k, 64)
+        chip = halves[rows].astype(F32)
+        later = fade[k : k + 1] * chip + sibling[rows].astype(F32)
+        result[rows] = jnp.where(first, chip, later).astype(BF16)
 
 
 def lower_mask():
@@ -454,7 +515,7 @@
     x_ref, gain, wq, kvw, wm, ws, taps_m, taps_s, bias_m, bias_s, decay, skip, mgain, wmo, wao,
     cum_ref, cumt_ref, normed, q, kv_all, logs_all, gz, ext, pre, post, attended, attended_f, totals, ssd, mixed,
     squares, state, gated, summed,
-    kv, logs, x_edge, edge_normed, local, states, chained, qp, acc, own_squares, slots, proj, part, work,
+    kv, logs, x_edge, edge_normed, local, sibling, row_slots, plane_slots, halves, qp, acc, own_squares, slots, proj, part, work,
     recv, send_sem, recv_sem,
 ):
     links = Links(send_sem, recv_sem)
@@ -476,31 +537,35 @@
     q[...] = nn(n, wq[...]).astype(BF16)
     sums = exact(decay[...], jnp.ones((ROWS, 128), F32), ((0,), (0,)))
     logs[...] = jnp.concatenate([sums, jnp.zeros((8 - HMH, 128), F32)], axis=0)
-    key_jobs = gather_rows(links, kv, kv_all) + gather_rows(links, logs, logs_all, SEQ_PATHS[:1])
+    key_jobs = gather_rows(links, kv, kv_all)
+    log_jobs = gather_rows(links, logs, logs_all, (LOG_PATH,))
     links.met(FORWARD_NAMES)
     edge_copy = links.send(x_ref.at[pl.ds(ROWS - 16, 16)], x_edge, "next")
-    keys = gather_steps(key_jobs)
-    advance(keys)
+    keys, every_log = gather_steps(key_jobs), gather_steps(log_jobs)
+    advance(keys, every_log)
     gz[...] = nn(normed[...], wm[0])
     lower = jnp.where(lower_mask(), 1.0, 0.0)
     cum_ref[...] = exact(lower, decay[...], ((1,), (0,)))
     cumt_ref[...] = exact(decay[...], lower, ((0,), (1,)))
-    advance(keys)
+    advance(keys, every_log)
     ext[pl.ds(16, ROWS), pl.ds(0, MW)] = nn(normed[...], wm[1])
     ext[pl.ds(16, ROWS), pl.ds(MW, 256)] = nn(normed[...], ws[...])
     edge_copy.wait()
-    advance(keys)
+    advance(keys, every_log)
     keep = jnp.where(s > 0, 1.0, 0.0)
     edge_normed[...] = normalise(x_edge[...])
     ext[pl.ds(0, 16), pl.ds(0, MW)] = nn(edge_normed[...], wm[1]) * keep
     ext[pl.ds(0, 16), pl.ds(MW, 256)] = nn(edge_normed[...], ws[...]) * keep
     conv_forward(ext, taps_m, taps_s, bias_m, bias_s, pre, post)
     advance(keys)
+    finish(every_log)
     step_x, enter_x, tail_x = decay_terms(decay, cum_ref)
     tail_in = (post[:, pl.ds(0, MW)].astype(F32) * step_x * tail_x).astype(BF16)
     local[...] = tn(tail_in, post[:, pl.ds(MW, NS)]).astype(BF16)
-    entering = gather_steps(gather_rows(links, local, states))
-    advance(entering, keys)
+    entering = scan_steps(
+        links, local, logs_all, sibling, row_slots, plane_slots, halves, state, True
+    )
+    advance(entering)
 
     qp[...] = stacked_queries(q[...])
     scores = causal(nt(kv[...], qp[...]))
@@ -535,6 +600,15 @@
     running = (high, jnp.sum(weights, axis=0, keepdims=True))
     hops = s // 2
     for turn in range(4):
+        if turn == 3:
+            finish(entering)
+            ssd_forward(
+                post, step_x, enter_x, cum_ref, cumt_ref, skip, gz, state, ssd, mixed, own_squares
+            )
+            slots[links.h] = own_squares[...]
+            square_copies = [
+                links.send(own_squares, slots.at[links.h], name) for name in ("x1", "x2", "x3")
+            ]
         running = lax.fori_loop((hops * turn) // 4, (hops * (turn + 1)) // 4, hop, running)
         advance(entering)
     running = lax.fori_loop(0, s % 2, last_hop, running)
@@ -544,27 +618,20 @@
     attended_f[...] = out
     attended[...] = out.astype(BF16)
     totals[...] = jnp.broadcast_to(high + jnp.log(total), totals.shape)
-    finish(entering)
-
-    chain(s, states, logs_all, chained, True)
-    state[...] = chained[...].astype(BF16)
-    ssd_forward(post, step_x, enter_x, cum_ref, cumt_ref, skip, gz, state, ssd, mixed, own_squares)
-    slots[links.h] = own_squares[...]
-    copies = [links.send(own_squares, slots.at[links.h], name) for name in ("x1", "x2", "x3")]
     for c in range(2):
         lanes = pl.ds(512 * c, 512)
         proj[:, lanes] = nn(attended[...], wao[:, lanes])
-    for copy in copies:
+    for copy in square_copies:
         copy.wait()
     squares[...] = (slots[0] + slots[1]) + (slots[2] + slots[3])
     scale = lax.rsqrt(column_of(squares[...]) / (MAMBA_HEADS * MP) + EPSILON)
-    gated[...] = (mixed[...] * scale * mgain[...]).astype(BF16)
+    gated[...] = (mixed[...] * scale * mgain[...].reshape(1, MW)).astype(BF16)
     for c in range(2):
         lanes = pl.ds(512 * c, 512)
         part[:, lanes] = (proj[:, lanes] + nn(gated[...], wmo[:, lanes])).astype(BF16)
     jobs = [
-        Reduce(links, path, 128, part, 128 * p, work, recv, summed, 128 * p)
-        for p, path in enumerate(HEAD_PATHS)
+        Reduce(links, path, 64, part, 64 * p, work, recv, summed, 64 * p)
+        for p, path in enumerate(HEAD_PATHS * 2)
     ]
     reduce_all(jobs)
     gather_all(jobs)
@@ -583,10 +650,10 @@
 def middle_kernel(
     x_ref, summed, cot_ref, gain, gu, dw, gated, attended, wmo, wao, mixed, squares, mgain, gz, ssd,
     post, decay, cum_ref, cumt_ref, state, q, kv_all, attended_f, totals, logs_all,
-    d_sum, share, x_out, xb_piece, second_part, mixgain, d_z, d_ssd, skip_part, d_scaled, d_bc, leaving, d_q, pairs,
+    d_sum, share, x_piece, xb_piece, second_part, mixgain, d_z, d_ssd, skip_part, d_scaled, d_bc, leaving, d_q, pairs,
     sn, out_acc, d_acc, back, wide, xf, xb, work, recv, wide_work, wide_recv, x_work, x_recv,
     xb_work, xb_recv,
-    d_att, d_gated, own_inner, slots, local, grads, chained, qp, dop, acc, send_sem, recv_sem,
+    d_att, d_gated, own_inner, slots, local, sibling, row_slots, plane_slots, halves, qp, dop, acc, send_sem, recv_sem,
 ):
     links = Links(send_sem, recv_sem)
     s = links.s
@@ -629,11 +696,11 @@
     links.met(MIDDLE_NAMES)
 
     sums = [
-        Reduce(links, path, 128, back, 128 * p, work, recv, d_sum, 128 * p)
-        for p, path in enumerate(HEAD_PATHS)
+        Reduce(links, path, 64, back, 64 * p, work, recv, d_sum, 64 * p)
+        for p, path in enumerate(HEAD_PATHS * 2)
     ]
     x_jobs = [
-        Reduce(links, path, 1536, xf, 1536 * p, x_work, x_recv, x_out, 1536 * p)
+        Reduce(links, path, 1536, xf, 1536 * p, x_work, x_recv, None, 1536 * p)
         for p, path in enumerate(SEQ_PATHS)
     ]
     summing = reduce_steps(sums)
@@ -642,13 +709,13 @@
     put_wide(wide, out_acc[...])
     advance(summing, first_weights, summing)
     back_again = gather_steps(sums)
-    advance(back_again, first_weights, back_again, first_weights, back_again)
+    advance(back_again, back_again, first_weights, back_again)
 
     low = (cot_ref[...].astype(F32) + d_sum[...].astype(F32)).astype(BF16)
     scale = lax.rsqrt(column_of(squares[...]) / (MAMBA_HEADS * MP) + EPSILON)
     d_gated[...] = nt(low, wmo[...])
     product = d_gated[...] * mixed[...]
-    own_inner[...] = row_sums(product * mgain[...])
+    own_inner[...] = row_sums(product * mgain[...].reshape(1, MW))
     slots[links.h] = own_inner[...]
     copies = [links.send(own_inner, slots.at[links.h], name) for name in ("x1", "x2", "x3")]
     mixgain[...] = jnp.broadcast_to(jnp.sum(product * scale, axis=0, keepdims=True), mixgain.shape)
@@ -657,7 +724,6 @@
         xb[pl.ds(512 * cb, MW)] = tn(gated[...], low[:, lanes]).astype(BF16)
         xb[pl.ds(512 * cb + MW, 128)] = tn(attended[...], low[:, lanes]).astype(BF16)
     d_att[...] = nt(low, wao[...]).astype(BF16)
-    finish(first_weights)
 
     xb_jobs = [
         Reduce(links, path, 512, xb, 512 * p, xb_work, xb_recv, None, 512 * p)
@@ -667,13 +733,13 @@
         Reduce(links, path, 512, wide, 512 * p, wide_work, wide_recv, None, 512 * p)
         for p, path in enumerate(HEAD_PATHS)
     ]
-    others = [gather_steps(x_jobs), reduce_steps(xb_jobs), reduce_steps(shares)]
+    others = [first_weights, reduce_steps(xb_jobs), reduce_steps(shares)]
     advance(*others)
     for copy in copies:
         copy.wait()
 
     inner_col = column_of((slots[0] + slots[1]) + (slots[2] + slots[3]))
-    d_mixed = scale * (d_gated[...] * mgain[...]) - mixed[...] * (
+    d_mixed = scale * (d_gated[...] * mgain[...].reshape(1, MW)) - mixed[...] * (
         scale * scale * scale / (MAMBA_HEADS * MP) * inner_col
     )
     z = gz[...]
@@ -685,7 +751,9 @@
     b, c = post[:, pl.ds(MW, NS)], post[:, pl.ds(MW + NS, NS)]
     entered = (ds * enter_x).astype(BF16)
     local[...] = tn(entered, c).astype(BF16)
-    leaving_all = gather_steps(gather_rows(links, local, grads))
+    leaving_all = scan_steps(
+        links, local, logs_all, sibling, row_slots, plane_slots, halves, leaving, False
+    )
     advance(leaving_all)
     mixer_in = post[:, pl.ds(0, MW)].astype(F32)
     skip_part[...] = jnp.broadcast_to(jnp.sum(ds * mixer_in, axis=0, keepdims=True), skip_part.shape)
@@ -758,13 +826,13 @@
     out = acc[pl.ds(0, HD)] * (HD ** -0.5)
     d_q[...] = jnp.concatenate([out[:, :ROWS], out[:, ROWS:]], axis=0).T.astype(BF16)
     finish(leaving_all)
-    chain(s, grads, logs_all, chained, False)
-    leaving[...] = chained[...].astype(BF16)
     finish(*others)
     for p, job in enumerate(shares):
         share[pl.ds(128 * p, 128)] = own_rows(job, 128)
     for p, job in enumerate(xb_jobs):
         xb_piece[pl.ds(16 * p, 16)] = own_rows(job, 16)
+    for p, job in enumerate(x_jobs):
+        x_piece[pl.ds(48 * p, 48)] = own_rows(job, 48)
 
 
 LAST_NAMES = SEQ_NAMES + ("next", "prev", "x1", "x2", "x3")
@@ -772,22 +840,27 @@
 
 def last_kernel(
     pairs, leaving, d_ssd, d_scaled, d_bc, skip, decay, cum, post, pre, ext, taps_m, taps_s, d_z, d_q,
-    normed, x_ref, gain, wm, ws, wq, kvw, second_part, mixgain, skip_part, xb_piece,
-    xb_out, ms_out, kq_out, share, small_out,
-    pair_work, pair_recv, d_pre, edge_in, shifted, d_all, acc, kernel_grads, ms, ms_work, ms_recv,
-    kq, kq_work, kq_recv, wide, wide_work, wide_recv, ms_slots, kq_slots, small_work, small_recv,
-    small_x, send_sem, recv_sem,
+    normed, x_ref, gain, wm, ws, wq, kvw, second_part, mixgain, skip_part, x_piece, xb_piece,
+    x_out, xb_out, zq_out, mix_out, st_out, kv_out, share, small_out,
+    pair_work, pair_recv, d_pre, edge_in, shifted, d_all, acc, kernel_grads,
+    zq, zq_work, zq_recv, mix, mix_work, mix_recv, st, st_work, st_recv, kv, kv_work, kv_recv,
+    wide, wide_work, wide_recv, st_slots, kv_slots, small_work, small_slots, send_sem, recv_sem,
 ):
     links = Links(send_sem, recv_sem)
     s = links.s
     links.greet(LAST_NAMES)
     links.met(LAST_NAMES)
-    pair_jobs = [
-        Reduce(links, path, 2048, pairs, 2048 * p, pair_work, pair_recv, None, 2048 * p)
-        for p, path in enumerate(SEQ_PATHS)
-    ]
+
+    def reduces(paths, rows, src, work, recv):
+        return [
+            Reduce(links, path, rows, src, rows * k, work, recv, None, rows * k)
+            for k, path in enumerate(paths)
+        ]
+
+    pair_jobs = reduces(SEQ_PATHS, 2048, pairs, pair_work, pair_recv)
     pairing = reduce_steps(pair_jobs)
     advance(pairing)
+    feed_weights = gather_steps(gather_rows(links, x_piece, x_out))
     output_weights = gather_steps(gather_rows(links, xb_piece, xb_out))
 
     step_x, _, tail_x = decay_terms(decay, cum)
@@ -804,24 +877,39 @@
         sig = sigmoid(v)
         dp = d_pre[:, lanes] * (sig * (1.0 + v * (1.0 - sig)))
         d_pre[:, lanes] = dp
+    edge_copy = links.send(d_pre.at[pl.ds(0, 8)], edge_in, "prev")
+    advance(pairing, feed_weights)
+    for c in range(5):
+        lanes = pl.ds(128 * c, 128)
+        dp = d_pre[:, lanes]
         rows = [jnp.sum(dp * ext[pl.ds(13 + k, ROWS), lanes], axis=0, keepdims=True) for k in range(KC)]
         rows.append(jnp.sum(dp, axis=0, keepdims=True))
         rows.append(jnp.zeros((3, 128), F32))
         kernel_grads[:, lanes] = jnp.concatenate(rows, axis=0)
-    edge_copy = links.send(d_pre.at[pl.ds(0, 8)], edge_in, "prev")
-    advance(pairing)
     d_all[:, pl.ds(0, MW)] = d_z[...]
-    d_all[:, pl.ds(1024, 128)] = d_q[...]
+    d_all[:, pl.ds(MW, 128)] = d_q[...]
 
     def early(i, carry):
         rows = pl.ds(pl.multiple_of(i * 256, 256), 256)
-        ms[rows, pl.ds(0, MW)] = tn(normed[:, rows], d_all[:, pl.ds(0, MW)]).astype(BF16)
-        kq[rows] = tn(normed[:, rows], d_all[:, pl.ds(1024, 128)]).astype(BF16)
-        acc[:, rows] = nt(d_all[:, pl.ds(0, MW)], wm[0, rows]) + nt(d_all[:, pl.ds(1024, 128)], wq[rows])
+        block = tn(normed[:, rows], d_all[:, pl.ds(0, 512)]).astype(BF16)
+        for k in range(4):
+            zq[rows_at(1024 * k + i * 256, 256)] = block[:, 128 * k : 128 * k + 128]
+        acc[:, rows] = nt(d_all[:, pl.ds(0, MW)], wm[0, rows]) + nt(d_all[:, pl.ds(MW, 128)], wq[rows])
         return carry
 
     lax.fori_loop(0, 4, early, 0)
-    advance(pairing)
+    zq_jobs = reduces(SHORT_PATHS, 2048, zq, zq_work, zq_recv)
+
+    def gate_weights():
+        yield from reduce_steps(zq_jobs)
+        for job in zq_jobs:
+            at = rows_at(job.base + job.start, 64)
+            zq_out[at] = zq_work[at]
+            job.out = zq_out
+        yield from gather_steps(zq_jobs)
+
+    zq_weights = gate_weights()
+    advance(zq_weights, pairing, feed_weights, output_weights)
     edge_copy.wait()
     keep = jnp.where(s < SEQ - 1, 1.0, 0.0)
     shifted[pl.ds(0, ROWS)] = d_pre[...]
@@ -832,57 +920,53 @@
         total = taps[pl.ds(0, 1), own] * shifted[pl.ds(3, ROWS), lanes]
         for k in range(1, KC):
             total = total + taps[pl.ds(k, 1), own] * shifted[pl.ds(3 - k, ROWS), lanes]
-        to = 640 + 128 * c if c < 3 else 384 + 128 * (c - 3)
-        d_all[:, pl.ds(to, 128)] = total.astype(BF16)
+        d_all[:, pl.ds(512 + 128 * c, 128)] = total.astype(BF16)
 
     def middle(i, carry):
         rows = pl.ds(pl.multiple_of(i * 256, 256), 256)
-        late = pl.ds(pl.multiple_of(i * 256 + 1024, 256), 256)
-        mine = normed[:, rows]
-        states = tn(mine, d_all[:, pl.ds(MW, 256)]).astype(BF16)
-        ms[rows, pl.ds(MW, 128)] = states[:, :128]
-        ms[late, pl.ds(MW, 128)] = states[:, 128:]
-        ms[late, pl.ds(0, MW)] = tn(mine, d_all[:, pl.ds(640, MW)]).astype(BF16)
+        block = tn(normed[:, rows], d_all[:, pl.ds(512, CW)]).astype(BF16)
+        mix[rows] = block[:, :MW]
+        st[rows] = block[:, MW:]
         return carry
 
     lax.fori_loop(0, 4, middle, 0)
-    ms_jobs = [
-        Reduce(links, path, 512, ms, 512 * p, ms_work, ms_recv, None, 512 * p)
-        for p, path in enumerate(SEQ_PATHS)
-    ]
+    mix_jobs = reduces(SHORT_PATHS, 512, mix, mix_work, mix_recv)
+    st_jobs = reduces(SHORT_PATHS, 512, st, st_work, st_recv)
 
     def mixer_weights():
-        yield from reduce_steps(ms_jobs)
-        for p, job in enumerate(ms_jobs):
+        yield from reduce_steps(mix_jobs + st_jobs)
+        for k, job in enumerate(st_jobs):
+            st_slots[links.h, pl.ds(16 * k, 16)] = own_rows(job, 16)
+        slot = st_slots.at[links.h]
+        copies = [links.send(slot, slot, name) for name in ("x1", "x2", "x3")]
+        for job in mix_jobs:
             at = rows_at(job.base + job.start, 16)
-            ms_slots[links.h, pl.ds(16 * p, 16)] = ms_work[at, pl.ds(MW, 128)]
-        slot = ms_slots.at[links.h]
-        copies = [links.send(slot, slot, name) for name in ("x1", "x2", "x3")]
+            mix_out[at] = mix_work[at]
+            job.out = mix_out
         yield
         for copy in copies:
             copy.wait()
-        for p, job in enumerate(ms_jobs):
+        for k, job in enumerate(st_jobs):
             at = rows_at(job.base + job.start, 16)
-            parts = [ms_slots[k, pl.ds(16 * p, 16)].astype(F32) for k in range(HEADS)]
-            ms_out[at, pl.ds(0, MW)] = ms_work[at, pl.ds(0, MW)]
-            ms_out[at, pl.ds(MW, 128)] = ((parts[0] + parts[1]) + (parts[2] + parts[3])).astype(BF16)
-            job.out = ms_out
-        yield from gather_steps(ms_jobs)
+            parts = [st_slots[j, pl.ds(16 * k, 16)].astype(F32) for j in range(HEADS)]
+            st_out[at] = ((parts[0] + parts[1]) + (parts[2] + parts[3])).astype(BF16)
+            job.out = st_out
+        yield from gather_steps(mix_jobs + st_jobs)
 
     mixing = mixer_weights()
-    advance(pairing, mixing, output_weights)
+    advance(mixing, pairing)
 
     def late_part(i, carry):
         rows = pl.ds(pl.multiple_of(i * 256, 256), 256)
-        total = acc[:, rows] + nt(d_all[:, pl.ds(640, MW)], wm[1, rows])
-        acc[:, rows] = total + nt(d_all[:, pl.ds(MW, 256)], ws[rows])
+        total = acc[:, rows] + nt(d_all[:, pl.ds(512, MW)], wm[1, rows])
+        acc[:, rows] = total + nt(d_all[:, pl.ds(512 + MW, 256)], ws[rows])
         return carry
 
     lax.fori_loop(0, 4, late_part, 0)
+    advance(zq_weights, feed_weights, output_weights)
     finish(pairing)
     for p, job in enumerate(pair_jobs):
         d_all[pl.ds(64 * p, 64), pl.ds(1152, 128)] = own_rows(job, 64)
-    advance(mixing, output_weights)
     left = lax.broadcasted_iota(jnp.int32, (ROWS, 128), 1) < HD
     d_pair = d_all[:, pl.ds(1152, 128)].astype(F32)
     other = pltpu.roll(d_pair, HD, 1)
@@ -893,53 +977,35 @@
 
     def pair_part(i, carry):
         rows = pl.ds(pl.multiple_of(i * 256, 256), 256)
-        late = pl.ds(pl.multiple_of(i * 256 + 1024, 256), 256)
-        pair = d_all[:, pl.ds(1152, 128)]
-        kq[late] = tn(normed[:, rows], pair).astype(BF16)
+        kv[rows] = tn(normed[:, rows], d_all[:, pl.ds(1152, 128)]).astype(BF16)
         acc[:, rows] += nt(d_keys, kvw[0, rows]) + nt(d_values, kvw[1, rows])
         return carry
 
     lax.fori_loop(0, 4, pair_part, 0)
-    kq_jobs = [
-        Reduce(links, path, 512, kq, 512 * p, kq_work, kq_recv, None, 512 * p)
-        for p, path in enumerate(SEQ_PATHS)
-    ]
+    kv_jobs = reduces(SHORT_PATHS, 512, kv, kv_work, kv_recv)
 
     def head_weights():
-        yield from reduce_steps(kq_jobs)
-        for p in (2, 3):
-            job = kq_jobs[p]
-            kq_slots[links.h, pl.ds(16 * (p - 2), 16)] = own_rows(job, 16)
-        slot = kq_slots.at[links.h]
+        yield from reduce_steps(kv_jobs)
+        for k, job in enumerate(kv_jobs):
+            kv_slots[links.h, pl.ds(16 * k, 16)] = own_rows(job, 16)
+        slot = kv_slots.at[links.h]
         copies = [links.send(slot, slot, name) for name in ("x1", "x2", "x3")]
         yield
         for copy in copies:
             copy.wait()
-        for p, job in enumerate(kq_jobs):
+        for k, job in enumerate(kv_jobs):
             at = rows_at(job.base + job.start, 16)
-            job.out = kq_out
-            if p < 2:
-                kq_out[at, pl.ds(0, 128)] = own_rows(job, 16)
-            else:
-                parts = [kq_slots[k, pl.ds(16 * (p - 2), 16)].astype(F32) for k in range(HEADS)]
-                kq_out[at, pl.ds(0, 128)] = (parts[0] + parts[1]).astype(BF16)
-                kq_out[at, pl.ds(128, 128)] = (parts[2] + parts[3]).astype(BF16)
-        yield from gather_steps(kq_jobs, [128, 128, None, None])
+            parts = [kv_slots[j, pl.ds(16 * k, 16)].astype(F32) for j in range(HEADS)]
+            kv_out[at, pl.ds(0, 128)] = (parts[0] + parts[1]).astype(BF16)
+            kv_out[at, pl.ds(128, 128)] = (parts[2] + parts[3]).astype(BF16)
+            job.out = kv_out
+        yield from gather_steps(kv_jobs)
 
     heading = head_weights()
     advance(heading)
     x = x_ref[...].astype(F32)
     r1 = lax.rsqrt(jnp.mean(x * x, axis=1, keepdims=True) + EPSILON)
     d_normed = acc[...]
-    weighted = d_normed * gain[...]
-    inner = jnp.sum(weighted * x, axis=1, keepdims=True)
-    put_wide(wide, r1 * weighted - x * (r1 * r1 * r1 / D * inner))
-    shares = [
-        Reduce(links, path, 512, wide, 512 * p, wide_work, wide_recv, None, 512 * p)
-        for p, path in enumerate(HEAD_PATHS)
-    ]
-    sharing = reduce_steps(shares)
-    advance(sharing)
     blank = jnp.zeros((1, 256), F32)
     grads = kernel_grads[...]
     vector_rows = [
@@ -955,28 +1021,47 @@
     small_work[0] = jnp.concatenate([jnp.concatenate(row, axis=1) for row in vector_rows], axis=0)
 
     def vectors():
-        for step, name in enumerate(DOUBLING):
-            copy = links.send(small_work.at[step], small_recv.at[step], name)
+        at = 0
+        for names, me in (
+            (("c",), links.bits["c"]),
+            (("y41", "y42", "y43"), links.bits["y4"]),
+            (("z41", "z42", "z43"), links.bits["z4"]),
+            (("x1", "x2", "x3"), links.h),
+        ):
+            step, count = at, len(names) + 1
+            slots = small_slots.at[pl.ds(4 * step, 4)]
+            slots[me] = small_work[step]
+            copies = [links.send(small_work.at[step], slots.at[me], name) for name in names]
             yield
-            copy.wait()
-            small_work[step + 1] = small_work[step] + small_recv[step]
-        small_x[links.h] = small_work[5]
-        copies = [links.send(small_work.at[5], small_x.at[links.h], n) for n in ("x1", "x2", "x3")]
-        yield
-        for copy in copies:
-            copy.wait()
-        total = (small_x[0] + small_x[1]) + (small_x[2] + small_x[3])
+            for copy in copies:
+                copy.wait()
+            total = slots[0] + slots[1]
+            if count == 4:
+                total = total + (slots[2] + slots[3])
+            small_work[step + 1] = total
+            at += 1
         row = lax.broadcasted_iota(jnp.int32, (8, 1024), 0)
-        small_out[...] = jnp.where(row < 4, total, small_work[5])
-
-    finish(heading, mixing, sharing, vectors(), output_weights)
+        small_out[...] = jnp.where(row < 4, small_work[4], small_work[3])
+
+    adding = vectors()
+    advance(adding)
+    weighted = d_normed * gain[...]
+    inner = jnp.sum(weighted * x, axis=1, keepdims=True)
+    put_wide(wide, r1 * weighted - x * (r1 * r1 * r1 / D * inner))
+    shares = [
+        Reduce(links, path, 512, wide, 512 * p, wide_work, wide_recv, None, 512 * p)
+        for p, path in enumerate(HEAD_PATHS)
+    ]
+    sharing = reduce_steps(shares)
+    advance(sharing)
+    finish(heading, adding, mixing, sharing, zq_weights, feed_weights, output_weights)
     for p, job in enumerate(shares):
         share[pl.ds(128 * p, 128)] = own_rows(job, 128)
 
 
 def widths_kernel(
-    h, down0, down1, down2, down3, gate0, gate1, up0, up1, mix0, mix1, mix2, mix3, head, tail, query_in,
-    keyval_in, x_ref, summed, out_share, cot, d_sum, in_share, small,
+    h, down0, down1, down2, down3, gate0, gate1, up0, up1, mix0, mix1, mix2, mix3, z0, z1, z2, query_in,
+    raw_in, state_in, keyval_in, x_ref, summed, out_share, cot, d_sum, in_share, small,
     down, gateup, mixout, attn, mixer, query, keyval, state, block_out, input_grads,
     gain, second, kernel_m, kernel_s, bias_m, bias_s, skip, mgain,
 ):
@@ -998,10 +1083,10 @@
         for cb, block in enumerate((mix0, mix1, mix2, mix3)):
             attn[:, pl.ds(256 * cb, 256)] = block[...].astype(F32)
 
-    mixer[0] = head[:, pl.ds(0, MW)].astype(F32)
-    mixer[1] = tail[:, pl.ds(0, MW)].astype(F32)
-    state[:, pl.ds(0, 128)] = head[:, pl.ds(MW, 128)].astype(F32)
-    state[:, pl.ds(128, 128)] = tail[:, pl.ds(MW, 128)].astype(F32)
+    for k, block in enumerate((z0, z1, z2)):
+        mixer[0, :, pl.ds(128 * k, 128)] = block[...].astype(F32)
+    mixer[1] = raw_in[...].astype(F32)
+    state[...] = state_in[...].astype(F32)
     query[...] = query_in[...].astype(F32)
     left = lax.broadcasted_iota(jnp.int32, (256, 128), 1) < HD
     first, second_head = keyval_in[:, pl.ds(0, 128)].astype(F32), keyval_in[:, pl.ds(128, 128)].astype(F32)
@@ -1017,13 +1102,13 @@
         kernel_m[...] = small[pl.ds(4, KC), pl.ds(0, MW)]
         for k in range(KC):
             kernel_s[pl.ds(k, 1)] = small[pl.ds(2, 1), pl.ds(256 * k, 256)]
-        bias_m[...] = small[pl.ds(4, 1), pl.ds(MW, MW)]
+        bias_m[...] = small[4, pl.ds(MW, MW)]
         bias_s[...] = small[pl.ds(3, 1), pl.ds(0, 256)]
         skip[...] = exact(small[pl.ds(6, 1), pl.ds(MW, MW)], head_spread(), ((1,), (1,)))
-        mgain[...] = small[pl.ds(5, 1), pl.ds(MW, MW)]
-
-
-def widened(h, x_out, xb_out, ms_out, kq_out, x_ref, summed, out_share, cot, d_sum, in_share, small):
+        mgain[...] = small[5, pl.ds(MW, MW)]
+
+
+def widened(h, x_out, xb_out, zq_out, mix_out, st_out, kv_out, x_ref, summed, out_share, cot, d_sum, in_share, small):
     def rows(count, width, offset=0):
         return pl.BlockSpec((count, width), lambda i, h: (i + offset, 0))
 
@@ -1032,6 +1117,9 @@
 
     def whole(count, width):
         return pl.BlockSpec((count, width), lambda i, h: (0, 0))
+
+    def line(width):
+        return pl.BlockSpec((width,), lambda i, h: (0,))
 
     own = pl.BlockSpec((64, 256), lambda i, h: (i, h[0]))
     grid = pltpu.PrefetchScalarGridSpec(
@@ -1040,15 +1128,16 @@
         in_specs=[rows(128, 256, 12 * cb) for cb in range(4)]
         + [rows(256, 256, 6 * cb + 2) for cb in range(4)]
         + [rows(128, 256, 4 * cb) for cb in range(4)]
-        + [rows(256, 512), rows(256, 512, 4), rows(256, 128), rows(256, 256, 4)]
+        + [rows(256, 128, 4 * k) for k in range(4)]
+        + [rows(256, MW), rows(256, 256), rows(256, 256)]
         + [own, own, rows(64, 256), own, own, rows(64, 256), whole(8, D)],
         out_specs=(
             rows(128, D), halves(256, 512),
             pl.BlockSpec((128, D), lambda i, h: (jnp.minimum(i, 2), 0)), whole(128, D),
             halves(256, MW), rows(256, 128), halves(256, 128), rows(256, 256),
             rows(64, 256), rows(64, 256),
-            whole(1, D), whole(1, D), whole(KC, MW), whole(KC, 256), whole(1, MW), whole(1, 256),
-            whole(1, HMH), whole(1, MW),
+            whole(1, D), whole(1, D), whole(KC, MW), whole(KC, 256), line(MW), whole(1, 256),
+            whole(1, HMH), line(MW),
         ),
     )
     return pl.pallas_call(
@@ -1059,13 +1148,19 @@
             shape((2, D, MW), F32), shape((D, 128), F32), shape((2, D, 128), F32), shape((D, 256), F32),
             shape((ROWS, 256), F32), shape((ROWS, 256), F32),
             shape((1, D), F32), shape((1, D), F32), shape((KC, MW), F32), shape((KC, 256), F32),
-            shape((1, MW), F32), shape((1, 256), F32), shape((1, HMH), F32), shape((1, MW), F32),
+            shape((MW,), F32), shape((1, 256), F32), shape((1, HMH), F32), shape((MW,), F32),
         ),
         compiler_params=pltpu.CompilerParams(vmem_limit_bytes=VMEM_LIMIT),
     )(
-        h, *[x_out] * 8, *[xb_out] * 4, ms_out, ms_out, kq_out, kq_out, x_ref, summed, out_share, cot,
+        h, *[x_out] * 8, *[xb_out] * 4, *[zq_out] * 4, mix_out, st_out, kv_out, x_ref, summed, out_share, cot,
         d_sum, in_share, small,
     )
+
+
+SCAN_SCRATCH = (
+    pltpu.VMEM((MW, NS), BF16), pltpu.VMEM((MW, NS), BF16), pltpu.VMEM((4, MW // 2, NS), BF16),
+    pltpu.VMEM((4, MW // 2, NS), BF16), pltpu.VMEM((MW, NS), BF16),
+)
 
 
 def on_device(
@@ -1075,9 +1170,9 @@
 ):
     gain1 = norm_gain.reshape(1, D)
     gain2 = second_gain.reshape(1, D)
-    mgain = mixer_gain.reshape(1, MW)
+    mgain = mixer_gain
     skip = skip_gain.reshape(1, HMH)
-    bias_m, bias_s = bias_mixer.reshape(1, MW), bias_state.reshape(1, 256)
+    bias_m, bias_s = bias_mixer, bias_state.reshape(1, 256)
     (
         cum, cum_t, normed, q, kv_all, logs_all, gz, ext, pre, post, attended, attended_f, totals, ssd, mixed,
         squares, state, gated, summed,
@@ -1099,7 +1194,7 @@
         scratch=[
             pltpu.VMEM((ROWS, 128), BF16), pltpu.VMEM((8, 128), F32),
             pltpu.VMEM((16, D), BF16), pltpu.VMEM((16, D), BF16),
-            pltpu.VMEM((MW, NS), BF16), pltpu.VMEM((12288, NS), BF16), pltpu.VMEM((MW, NS), F32),
+            *SCAN_SCRATCH,
             pltpu.VMEM((512, 128), BF16), pltpu.VMEM((128, 512), F32), pltpu.VMEM((8, ROWS), F32),
             pltpu.VMEM((HEADS, 8, ROWS), F32), pltpu.VMEM((ROWS, D), F32),
             pltpu.VMEM((ROWS, D), BF16), pltpu.VMEM((ROWS, D), BF16), pltpu.VMEM((ROWS, D), BF16),
@@ -1107,12 +1202,12 @@
         collective=1, copies=80,
     )
     (
-        d_sum, out_share, x_out, xb_piece, second_part, mixgain, d_z, d_ssd, skip_part, d_scaled, d_bc, leaving,
+        d_sum, out_share, x_piece, xb_piece, second_part, mixgain, d_z, d_ssd, skip_part, d_scaled, d_bc, leaving,
         d_q, pairs,
     ) = call(
         middle_kernel,
         [
-            shape((ROWS, D), BF16), shape((ROWS, 256), BF16), shape((6144, 256), BF16),
+            shape((ROWS, D), BF16), shape((ROWS, 256), BF16), shape((192, 256), BF16),
             shape((64, 256), BF16),
             shape((8, D), F32), shape((8, MW), F32), shape((ROWS, MW), BF16), shape((ROWS, MW), F32),
             shape((8, MW), F32), shape((ROWS, MW), F32), shape((ROWS, 256), F32),
@@ -1132,42 +1227,42 @@
             pltpu.VMEM((2048, 256), BF16), pltpu.VMEM((2048, 256), BF16),
             pltpu.VMEM((ROWS, 128), BF16), pltpu.VMEM((ROWS, MW), F32), pltpu.VMEM((8, ROWS), F32),
             pltpu.VMEM((HEADS, 8, ROWS), F32), pltpu.VMEM((MW, NS), BF16),
-            pltpu.VMEM((12288, NS), BF16), pltpu.VMEM((MW, NS), F32), pltpu.VMEM((512, 128), BF16),
+            *SCAN_SCRATCH[1:], pltpu.VMEM((512, 128), BF16),
             pltpu.VMEM((512, 128), BF16), pltpu.VMEM((128, 512), F32),
         ],
         collective=2, copies=150,
     )
-    xb_out, ms_out, kq_out, in_share, small = call(
+    x_out, xb_out, zq_out, mix_out, st_out, kv_out, in_share, small = call(
         last_kernel,
         [
-            shape((2048, 256), BF16), shape((2048, 512), BF16), shape((2048, 256), BF16),
-            shape((ROWS, 256), BF16),
-            shape((8, D), F32),
+            shape((6144, 256), BF16), shape((2048, 256), BF16), shape((4096, 128), BF16),
+            shape((D, MW), BF16), shape((D, 256), BF16), shape((D, 256), BF16),
+            shape((ROWS, 256), BF16), shape((8, D), F32),
         ],
         (
             pairs, leaving, d_ssd, d_scaled, d_bc, skip, log_decay, cum, post, pre, ext, kernel_mixer,
             kernel_state, d_z, d_q, normed, hidden_in, gain1, mixer_weight, state_weight, query_weight,
-            keyvalue_weight, second_part, mixgain, skip_part, xb_piece,
+            keyvalue_weight, second_part, mixgain, skip_part, x_piece, xb_piece,
         ),
         scratch=[
             pltpu.VMEM((8192, 128), BF16), pltpu.VMEM((8192, 128), BF16), pltpu.VMEM((ROWS, CW), F32),
             pltpu.VMEM((8, CW), F32), pltpu.VMEM((ROWS + 8, CW), F32), pltpu.VMEM((ROWS, 1280), BF16),
             pltpu.VMEM((ROWS, D), F32), pltpu.VMEM((8, CW), F32),
-            pltpu.VMEM((2048, 512), BF16), pltpu.VMEM((2048, 512), BF16), pltpu.VMEM((2048, 512), BF16),
-            pltpu.VMEM((2048, 128), BF16), pltpu.VMEM((2048, 128), BF16), pltpu.VMEM((2048, 128), BF16),
-            pltpu.VMEM((1024, 256), BF16), pltpu.VMEM((1024, 256), BF16), pltpu.VMEM((1024, 256), BF16),
-            pltpu.VMEM((HEADS, 64, 128), BF16), pltpu.VMEM((HEADS, 32, 128), BF16),
-            pltpu.VMEM((6, 8, D), F32), pltpu.VMEM((5, 8, D), F32), pltpu.VMEM((HEADS, 8, D), F32),
+            *[pltpu.VMEM((4096, 128), BF16)] * 3, *[pltpu.VMEM((D, MW), BF16)] * 3,
+            *[pltpu.VMEM((D, 256), BF16)] * 3, *[pltpu.VMEM((D, 128), BF16)] * 3,
+            *[pltpu.VMEM((D, 256), BF16)] * 3,
+            pltpu.VMEM((HEADS, 32, 256), BF16), pltpu.VMEM((HEADS, 32, 128), BF16),
+            pltpu.VMEM((5, 8, D), F32), pltpu.VMEM((16, 8, D), F32),
         ],
-        collective=3, copies=190,
-    )
-
+        collective=3, copies=230,
+    )
     h = lax.axis_index("head").astype(jnp.int32).reshape(1)
     (
         down, gateup, mixout, attn, mixer, query, keyval, state_grads, block_out, input_grads,
         gain_grads, second_grads, mixkernel, statekernel, mixbias, statebias, skip_grads, mixgain_grads,
     ) = widened(
-        h, x_out, xb_out, ms_out, kq_out, hidden_in, summed, out_share, cotangent, d_sum, in_share, small
+        h, x_out, xb_out, zq_out, mix_out, st_out, kv_out, hidden_in, summed, out_share, cotangent,
+        d_sum, in_share, small,
     )
     return (
         block_out,
@@ -1180,10 +1275,10 @@
         state_grads,
         mixkernel,
         statekernel,
-        mixbias.reshape(MW),
+        mixbias,
         statebias.reshape(256),
         skip_grads.reshape(HMH),
-        mixgain_grads.reshape(MW),
+        mixgain_grads,
         mixout,
         second_grads.reshape(D),
         gateup,

time: 214 us -> 197 us (0.921)
  Pallas kernels: 202 us -> 185 us
    pallas_call x3, Pallas kernels: 193 us -> 177 us  [call(): pl.pallas_call(body, out_shape=tuple(outs), in_specs=in_specs, out_specs=...]
    unnamed x45 -> x43, local copies, waits for them, and re-layouts: 8.93 us -> 9.85 us
where the time goes in v3:
time: 197 us; the launch traced here: 196 us
  Pallas kernels  185 us (94%)
  local copies, waits for them, and re-layouts  9.85 us (5%)
    pallas_call x3, Pallas kernels, call(): pl.pallas_call(body, out_shape=tuple(outs), in_specs=in_specs, out_specs=...  177 us
    unnamed x43, local copies, waits for them, and re-layouts  9.85 us
    pallas_call x1, Pallas kernels, widened(): pl.pallas_call(widths_kernel, grid_spec=grid, out_shape=(shape((512, D),...  8.75 us

profile of v3, /device:TPU:1, one launch (start us, length us, event | category | flops | bytes accessed | tf_op | source)
XLA Modules:
  0.0 196.2 jit_solution(15275294180186109226)
XLA Ops:
  0.7 0.8 copy.37.decay
  1.5 0.0 copy-start.4
  1.5 0.9 copy-done.4
  2.4 0.9 copy-done.6
  3.4 0.7 copy-done.11
  4.1 0.7 copy-done.12
  4.8 0.7 copy-done.13
  5.5 0.7 copy-done.14
  6.1 0.7 copy-done.17
  6.8 0.7 copy-done.18
  7.5 0.7 copy-done.20
  8.2 56.8 %shard_map.322 = (f32[256,6]{1,0:T(8,128)S(1)}, f32[6,256]{1,0:T(8,128)S(1)}, bf16[256,1024]{1,0:T(8,128)(2,1)S(1)}, bf16[256,128]{1,0:T(8,128)(2,1)S(1)}, bf16[...) custom-call(bf16[256,1024]{1,0:T(8,128)(2,1)} %x_ref.7, ...), custom_call_target="tpu_custom_call" | custom-call | tf_op jit(solution)/shard_map/pallas_call | solution.py:305
  65.0 0.0 copy-start.2
  65.0 0.8 copy-done.2
  65.8 0.8 copy-done.9
  66.6 0.7 copy-done.10
  67.3 0.0 copy-done.7
  67.3 0.0 copy-done.15
  67.4 0.0 copy-done.16
  67.4 0.0 copy-start.19
  67.4 52.7 %shard_map.323 = (bf16[256,1024]{1,0:T(8,128)(2,1)}, bf16[256,256]{1,0:T(8,128)(2,1)S(1)}, bf16[192,256]{1,0:T(8,128)(2,1)S(1)}, bf16[64,256]{1,0:T(8,128)(2,1)S...) custom-call(bf16[256,1024]{1,0:T(8,128)(2,1)} %x_ref.7, ...), custom_call_target="tpu_custom_call" | custom-call | tf_op jit(solution)/shard_map/pallas_call | solution.py:305
  120.0 0.0 copy-done.5
  120.1 0.0 copy-done.19
  120.1 0.0 copy-start
  120.1 0.0 copy-start.1
  120.1 0.0 copy-start.3
  120.1 0.0 copy-start.8
  120.1 67.1 %shard_map.324 = (bf16[6144,256]{1,0:T(8,128)(2,1)}, bf16[2048,256]{1,0:T(8,128)(2,1)}, bf16[4096,128]{1,0:T(8,128)(2,1)}, bf16[1024,384]{1,0:T(8,128)(2,1)}, bf...) custom-call(bf16[8192,128]{1,0:T(8,128)(2,1)} %get-tuple-element.93., ...), custom_call_target="tpu_custom_call" | custom-call | tf_op jit(solution)/shard_map/pallas_call | solution.py:305
  187.2 0.0 copy-done
  187.2 0.0 copy-done.1
  187.2 0.0 copy-done.3
  187.3 8.7 %shard_map.325 = (f32[512,1024]{1,0:T(8,128)}, f32[2,1024,512]{2,1,0:T(8,128)}, f32[384,1024]{1,0:T(8,128)}, f32[128,1024]{1,0:T(8,128)}, f32[2,1024,384]{2,1,0:...) custom-call(s32[1]{0:T(128)} %bitcast.h, ...), custom_call_target="tpu_custom_call" | custom-call | tf_op jit(solution)/shard_map/pallas_call | solution.py:1143
  (15 shorter events, 0.0 us)
Async XLA Ops:
  1.5 1.0 copy-start.4
  2.4 0.9 copy-start.6
  3.4 0.7 copy-start.11
  4.1 0.7 copy-start.12
  4.8 0.7 copy-start.13
  5.5 0.7 copy-start.14
  6.1 0.7 copy-start.17
  6.8 0.7 copy-start.18
  7.5 0.7 copy-start.20
  8.2 59.2 %copy-start.7 = (bf16[128,1024]{1,0:T(8,128)(2,1)S(1)}, bf16[128,1024]{1,0:T(8,128)(2,1)}, u32[]{:S(2)}) copy-start(bf16[128,1024]{1,0:T(8,128)(2,1)} %wao.3) | copy-start | bytes 786436
  8.2 59.2 %copy-start.15 = (f32[384]{0:T(512)S(1)}, f32[384]{0:T(512)}, u32[]{:S(2)}) copy-start(f32[384]{0:T(512)} %mgain.3) | copy-start | bytes 4612
  8.2 59.2 %copy-start.16 = (f32[1024]{0:T(1024)S(1)}, f32[1024]{0:T(1024)}, u32[]{:S(2)}) copy-start(f32[1024]{0:T(1024)} %param.35) | copy-start | bytes 12292
  65.0 0.8 copy-start.2
  65.8 0.8 copy-start.9
  66.6 0.7 copy-start.10
  67.4 52.7 %copy-start.5 = (bf16[1024,128]{1,0:T(8,128)(2,1)S(1)}, bf16[1024,128]{1,0:T(8,128)(2,1)}, u32[]{:S(2)}) copy-start(bf16[1024,128]{1,0:T(8,128)(2,1)} %wq.3) | copy-start | bytes 786436
  67.4 52.7 %copy-start.19 = (f32[6]{0:T(128)S(1)}, f32[6]{0:T(128)}, u32[]{:S(2)}) copy-start(f32[6]{0:T(128)} %param.32) | copy-start | bytes 76
  120.1 67.2 %copy-start = (bf16[256,1024]{1,0:T(8,128)(2,1)S(1)}, bf16[256,1024]{1,0:T(8,128)(2,1)}, u32[]{:S(2)}) copy-start(bf16[256,1024]{1,0:T(8,128)(2,1)} %x_ref.7) | copy-start | bytes 1572868
  120.1 67.2 %copy-start.1 = (bf16[256,1024]{1,0:T(8,128)(2,1)S(1)}, bf16[256,1024]{1,0:T(8,128)(2,1)}, u32[]{:S(2)}) copy-start(bf16[256,1024]{1,0:T(8,128)(2,1)} %cot.1) | copy-start | bytes 1572868
  120.1 67.1 %copy-start.3 = (bf16[256,1024]{1,0:T(8,128)(2,1)S(1)}, bf16[256,1024]{1,0:T(8,128)(2,1)}, u32[]{:S(2)}) copy-start(bf16[256,1024]{1,0:T(8,128)(2,1)} %copy-done.2) | copy-start | bytes 1572868
  120.1 67.1 %copy-start.8 = (bf16[256,1024]{1,0:T(8,128)(2,1)S(1)}, bf16[256,1024]{1,0:T(8,128)(2,1)}, u32[]{:S(2)}) copy-start(bf16[256,1024]{1,0:T(8,128)(2,1)} %get-tuple-element.115.d_sum) | copy-start | bytes 1572868

commit v4 on v3

--- a/solution.py
+++ b/solution.py
@@ -290,7 +290,7 @@
     finish(gather_steps(jobs, columns))
 
 
-def call(body, outs, args, scratch=(), collective=None, smem=0, copies=0, cost=None):
+def call(body, outs, args, scratch=(), collective=None, smem=0, copies=0, limit=VMEM_LIMIT):
     vm = pl.BlockSpec(memory_space=pltpu.VMEM)
     scratch = list(scratch)
     if copies:
@@ -299,7 +299,7 @@
         params = pltpu.CompilerParams(vmem_limit_bytes=VMEM_LIMIT)
     else:
         params = pltpu.CompilerParams(
-            vmem_limit_bytes=VMEM_LIMIT, collective_id=collective, has_side_effects=True
+            vmem_limit_bytes=limit, collective_id=collective, has_side_effects=True
         )
     in_specs = [pl.BlockSpec(memory_space=pltpu.SMEM)] * smem + [vm] * (len(args) - smem)
     return pl.pallas_call(
@@ -1199,7 +1199,7 @@
             pltpu.VMEM((HEADS, 8, ROWS), F32), pltpu.VMEM((ROWS, D), F32),
             pltpu.VMEM((ROWS, D), BF16), pltpu.VMEM((ROWS, D), BF16), pltpu.VMEM((ROWS, D), BF16),
         ],
-        collective=1, copies=80,
+        collective=1, copies=80, limit=60 * 1024 * 1024,
     )
     (
         d_sum, out_share, x_piece, xb_piece, second_part, mixgain, d_z, d_ssd, skip_part, d_scaled, d_bc, leaving,

time: 197 us -> 202 us (1.025)
  local copies, waits for them, and re-layouts: 9.85 us -> 12.8 us
    unnamed x43 -> x57, local copies, waits for them, and re-layouts: 9.85 us -> 12.8 us
where the time goes in v4:
time: 202 us; the launch traced here: 201 us
  Pallas kernels  187 us (93%)
  local copies, waits for them, and re-layouts  12.8 us (6%)
    pallas_call x3, Pallas kernels, call(): pl.pallas_call(body, out_shape=tuple(outs), in_specs=in_specs, out_specs=...  178 us
    unnamed x57, local copies, waits for them, and re-layouts  12.8 us
    pallas_call x1, Pallas kernels, widened(): pl.pallas_call(widths_kernel, grid_spec=grid, out_shape=(shape((512, D),...  8.75 us

profile of v4, /device:TPU:1, one launch (start us, length us, event | category | flops | bytes accessed | tf_op | source)
XLA Modules:
  0.0 200.9 jit_solution(17953448131517183091)
XLA Ops:
  0.7 1.5 copy.37.decay
  2.2 58.2 %shard_map.322 = (f32[256,6]{1,0:T(8,128)}, f32[6,256]{1,0:T(8,128)}, bf16[256,1024]{1,0:T(8,128)(2,1)}, bf16[256,128]{1,0:T(8,128)(2,1)}, bf16[8192,128]{1,0:T(...) custom-call(bf16[256,1024]{1,0:T(8,128)(2,1)} %x_ref.7, ...), custom_call_target="tpu_custom_call" | custom-call | tf_op jit(solution)/shard_map/pallas_call | solution.py:305
  60.4 1.0 copy-done.4
  61.4 0.9 copy-done.9
  62.3 1.0 copy-done.11
  63.3 1.0 copy-done.12
  64.3 0.9 copy-done.13
  65.2 0.9 copy-done.14
  66.1 0.9 copy-done.15
  67.0 0.9 copy-done.16
  67.9 0.8 copy-done.17
  68.8 0.8 copy-done.18
  69.6 0.7 copy-done.20
  70.3 0.7 copy-done.23
  71.0 0.7 copy-done.24
  71.7 0.0 copy-start.21
  71.7 0.0 copy-start.22
  71.8 0.0 copy-start.27
  71.8 52.6 %shard_map.323 = (bf16[256,1024]{1,0:T(8,128)(2,1)}, bf16[256,256]{1,0:T(8,128)(2,1)S(1)}, bf16[192,256]{1,0:T(8,128)(2,1)S(1)}, bf16[64,256]{1,0:T(8,128)(2,1)S...) custom-call(bf16[256,1024]{1,0:T(8,128)(2,1)} %x_ref.7, ...), custom_call_target="tpu_custom_call" | custom-call | tf_op jit(solution)/shard_map/pallas_call | solution.py:305
  124.3 0.0 copy-done.5
  124.4 0.0 copy-done.6
  124.4 0.0 copy-done.10
  124.4 0.0 copy-done.19
  124.4 0.0 copy-done.21
  124.4 0.0 copy-done.22
  124.4 0.0 copy-done.27
  124.4 0.0 copy-start
  124.4 0.0 copy-start.2
  124.5 67.4 %shard_map.324 = (bf16[6144,256]{1,0:T(8,128)(2,1)}, bf16[2048,256]{1,0:T(8,128)(2,1)}, bf16[4096,128]{1,0:T(8,128)(2,1)}, bf16[1024,384]{1,0:T(8,128)(2,1)}, bf...) custom-call(bf16[8192,128]{1,0:T(8,128)(2,1)} %get-tuple-element.93., ...), custom_call_target="tpu_custom_call" | custom-call | tf_op jit(solution)/shard_map/pallas_call | solution.py:305
  191.9 0.0 copy-done
  191.9 0.0 copy-done.2
  191.9 8.7 %shard_map.325 = (f32[512,1024]{1,0:T(8,128)}, f32[2,1024,512]{2,1,0:T(8,128)}, f32[384,1024]{1,0:T(8,128)}, f32[128,1024]{1,0:T(8,128)}, f32[2,1024,384]{2,1,0:...) custom-call(s32[1]{0:T(128)} %bitcast.h, ...), custom_call_target="tpu_custom_call" | custom-call | tf_op jit(solution)/shard_map/pallas_call | solution.py:1143
  (29 shorter events, 0.1 us)
Async XLA Ops:
  2.2 58.2 %copy-start.1 = (f32[256,6]{1,0:T(8,128)S(1)}, f32[256,6]{1,0:T(8,128)}, u32[]{:S(2)}) copy-start(f32[256,6]{1,0:T(8,128)} %copy.37.decay) | copy-start | bytes 18436
  2.2 58.2 %copy-start.7 = (bf16[128,1024]{1,0:T(8,128)(2,1)S(1)}, bf16[128,1024]{1,0:T(8,128)(2,1)}, u32[]{:S(2)}) copy-start(bf16[128,1024]{1,0:T(8,128)(2,1)} %wao.3) | copy-start | bytes 786436
  2.2 58.2 %copy-start.25 = (f32[384]{0:T(512)S(1)}, f32[384]{0:T(512)}, u32[]{:S(2)}) copy-start(f32[384]{0:T(512)} %mgain.3) | copy-start | bytes 4612
  2.2 58.3 %copy-start.26 = (f32[1024]{0:T(1024)S(1)}, f32[1024]{0:T(1024)}, u32[]{:S(2)}) copy-start(f32[1024]{0:T(1024)} %param.35) | copy-start | bytes 12292
  60.4 1.0 copy-start.4
  61.4 0.9 copy-start.9
  62.3 1.0 copy-start.11
  63.3 1.0 copy-start.12
  64.3 0.9 copy-start.13
  65.2 0.9 copy-start.14
  66.1 0.9 copy-start.15
  67.0 0.9 copy-start.16
  67.9 0.8 copy-start.17
  68.8 0.8 copy-start.18
  69.6 0.7 copy-start.20
  70.3 0.7 copy-start.23
  71.0 0.7 copy-start.24
  71.7 52.6 %copy-start.5 = (bf16[256,640]{1,0:T(8,128)(2,1)S(1)}, bf16[256,640]{1,0:T(8,128)(2,1)}, u32[]{:S(2)}) copy-start(bf16[256,640]{1,0:T(8,128)(2,1)} %get-tuple-element.84.post) | copy-start | bytes 983044
  71.7 52.6 %copy-start.6 = (bf16[1024,128]{1,0:T(8,128)(2,1)S(1)}, bf16[1024,128]{1,0:T(8,128)(2,1)}, u32[]{:S(2)}) copy-start(bf16[1024,128]{1,0:T(8,128)(2,1)} %wq.3) | copy-start | bytes 786436
  71.7 52.7 %copy-start.10 = (f32[256,6]{1,0:T(8,128)S(1)}, f32[256,6]{1,0:T(8,128)}, u32[]{:S(2)}) copy-start(f32[256,6]{1,0:T(8,128)} %get-tuple-element.85.cum_ref.cum) | copy-start | bytes 18436
  71.7 52.7 %copy-start.19 = (f32[4,384]{1,0:T(4,128)S(1)}, f32[4,384]{1,0:T(4,128)}, u32[]{:S(2)}) copy-start(f32[4,384]{1,0:T(4,128)} %taps_m.3) | copy-start | bytes 18436
  71.7 52.7 %copy-start.21 = (f32[1024]{0:T(1024)S(1)}, f32[1024]{0:T(1024)}, u32[]{:S(2)}) copy-start(f32[1024]{0:T(1024)} %param.22) | copy-start | bytes 12292
  71.7 52.7 %copy-start.22 = (f32[4,256]{1,0:T(4,128)S(1)}, f32[4,256]{1,0:T(4,128)}, u32[]{:S(2)}) copy-start(f32[4,256]{1,0:T(4,128)} %taps_s.3) | copy-start | bytes 12292
  71.8 52.7 %copy-start.27 = (f32[6]{0:T(128)S(1)}, f32[6]{0:T(128)}, u32[]{:S(2)}) copy-start(f32[6]{0:T(128)} %param.32) | copy-start | bytes 76
  124.4 67.5 %copy-start = (bf16[256,1024]{1,0:T(8,128)(2,1)S(1)}, bf16[256,1024]{1,0:T(8,128)(2,1)}, u32[]{:S(2)}) copy-start(bf16[256,1024]{1,0:T(8,128)(2,1)} %x_ref.7) | copy-start | bytes 1572868
  124.4 67.5 %copy-start.2 = (bf16[256,1024]{1,0:T(8,128)(2,1)S(1)}, bf16[256,1024]{1,0:T(8,128)(2,1)}, u32[]{:S(2)}) copy-start(bf16[256,1024]{1,0:T(8,128)(2,1)} %cot.1) | copy-start | bytes 1572868
  124.4 67.5 %copy-start.3 = (bf16[256,1024]{1,0:T(8,128)(2,1)S(1)}, bf16[256,1024]{1,0:T(8,128)(2,1)}, u32[]{:S(2)}) copy-start(bf16[256,1024]{1,0:T(8,128)(2,1)} %get-tuple-element.77.summed) | copy-start | bytes 1572868
  124.5 67.5 %copy-start.8 = (bf16[256,1024]{1,0:T(8,128)(2,1)S(1)}, bf16[256,1024]{1,0:T(8,128)(2,1)}, u32[]{:S(2)}) copy-start(bf16[256,1024]{1,0:T(8,128)(2,1)} %get-tuple-element.115.d_sum) | copy-start | bytes 1572868
